TPU v7x, 32 devices: a whole 2x2x4 slice. The times are simulated.
32 devices in a mesh: group: 2 (over y), space: 16 (over z, x, core).
Axes of the slice: x: 2, y: 2, z: 4, core: 2. Of those that a mesh axis runs over, the one named last changes fastest.
Arguments:
- flow_field: float32 [64, 32, 128, 128], P(('group', 'space')), parts along dimension 0, may hold values from -6 to 6
- cotangent: float32 [64, 32, 128, 128], P(('group', 'space')), parts along dimension 0, may hold values from -6 to 6
- spec_weight: float32 [512, 2, 32, 1024], P('space'), may hold values from -0.75 to 0.75
- point_weight: float32 [32, 32], replicated, may hold values from -1 to 1
- pointwise_bias: float32 [32], replicated, may hold values from -3 to 3
Outputs:
- output: float32 [64, 32, 128, 128], P(('group', 'space')), parts along dimension 0
- grad_field: float32 [64, 32, 128, 128], P(('group', 'space')), parts along dimension 0
- grad_spec: float32 [1024, 2, 32, 1024], P(('group', 'space')), parts along dimension 0
- grad_point: float32 [64, 32], P('group'), parts along dimension 0
- grad_bias: float32 [64], P('group'), parts along dimension 0
There are 2 independent parts, one for each index of `group`. A program takes and returns all parts, laid end to end along the dimension named above; an argument that names none is the same for every part. Nothing has to cross between parts.
All inputs are finite; a program needn't handle non-finite values.
Results may differ from a plain program's by a relative error of at most 0.00012.
Values sent between devices are 32-bit elements; how exact they have to be, the bound alone decides.
No kernel may reach another device: no remote copies, remote signals or barrier semaphores. Data moves between devices by JAX's collectives and lax.ppermute only.
A program may use at most 256 MiB of HBM per device.

v0:
```python
import math

import jax
import jax.numpy as jnp
from jax import lax
from jax.sharding import PartitionSpec as P

MODES = 16


highest = lax.Precision.HIGHEST


def contract(form, left, right):
    return jnp.einsum(form, left, right, precision=highest)


def phase_table(positions, wavenums, length):
    phases = positions[:, None] * wavenums[None, :] % length
    angles = phases.astype(jnp.float32) * (2.0 * math.pi / length)
    return (jnp.cos(angles), jnp.sin(angles))


def signed_modes(mode_count):
    indices = jnp.arange(mode_count, dtype=jnp.int32)
    return jnp.where(indices < mode_count // 2, indices, indices - mode_count)


def yz_forward(values, z_cos, z_sin, y_cos, y_sin):
    cosine_part = contract("xcyz,zk->xcyk", values, z_cos)
    sine_part = -contract("xcyz,zk->xcyk", values, z_sin)
    real_part = contract("xcyk,yj->xjkc", cosine_part, y_cos) + contract(
        "xcyk,yj->xjkc", sine_part, y_sin
    )
    imag_part = contract("xcyk,yj->xjkc", sine_part, y_cos) - contract(
        "xcyk,yj->xjkc", cosine_part, y_sin
    )
    row_count, ky_count, kz_count, channels = real_part.shape
    shaped = (row_count, ky_count * kz_count, channels)
    return jnp.stack([real_part.reshape(shaped), imag_part.reshape(shaped)], axis=2)


def yz_inverse(spectrum, z_cos, z_sin, y_cos, y_sin, kz_weights):
    row_count, pair_count, _, channels = spectrum.shape
    kz_count = z_cos.shape[1]
    ky_count = pair_count // kz_count
    part_real = spectrum[:, :, 0].reshape(row_count, ky_count, kz_count, channels)
    part_imag = spectrum[:, :, 1].reshape(row_count, ky_count, kz_count, channels)
    back_real = contract("xjkc,yj->xcyk", part_real, y_cos) - contract(
        "xjkc,yj->xcyk", part_imag, y_sin
    )
    back_imag = contract("xjkc,yj->xcyk", part_real, y_sin) + contract(
        "xjkc,yj->xcyk", part_imag, y_cos
    )
    return contract("xcyk,zk->xcyz", back_real, z_cos * kz_weights[None, :]) - contract(
        "xcyk,zk->xcyz", back_imag, z_sin * kz_weights[None, :]
    )


def x_forward(spectrum, x_cos, x_sin):
    part_real = spectrum[:, :, 0]
    part_imag = spectrum[:, :, 1]
    mode_real = contract("xpc,xq->pqc", part_real, x_cos) + contract(
        "xpc,xq->pqc", part_imag, x_sin
    )
    mode_imag = contract("xpc,xq->pqc", part_imag, x_cos) - contract(
        "xpc,xq->pqc", part_real, x_sin
    )
    return jnp.stack([mode_real, mode_imag], axis=2)


def x_inverse(mode_data, x_cos, x_sin):
    mode_real = mode_data[:, :, 0]
    mode_imag = mode_data[:, :, 1]
    part_real = contract("pqc,xq->xpc", mode_real, x_cos) - contract(
        "pqc,xq->xpc", mode_imag, x_sin
    )
    part_imag = contract("pqc,xq->xpc", mode_real, x_sin) + contract(
        "pqc,xq->xpc", mode_imag, x_cos
    )
    return jnp.stack([part_real, part_imag], axis=2)


def split_weight(weights, kx_total):
    pair_total, _, channels, _ = weights.shape
    shaped = weights.reshape(pair_total, 2, channels, kx_total, channels)
    return (shaped[:, 0], shaped[:, 1])


def mode_mix(mode_data, weights):
    w_real, w_imag = split_weight(weights, mode_data.shape[1])
    in_real = mode_data[:, :, 0]
    in_imag = mode_data[:, :, 1]
    out_real = contract("pqi,piqo->pqo", in_real, w_real) - contract(
        "pqi,piqo->pqo", in_imag, w_imag
    )
    out_imag = contract("pqi,piqo->pqo", in_imag, w_real) + contract(
        "pqi,piqo->pqo", in_real, w_imag
    )
    return jnp.stack([out_real, out_imag], axis=2)


def mode_adjoint(grad_modes, weights):
    w_real, w_imag = split_weight(weights, grad_modes.shape[1])
    grad_real = grad_modes[:, :, 0]
    grad_imag = grad_modes[:, :, 1]
    in_real = contract("pqo,piqo->pqi", grad_real, w_real) + contract(
        "pqo,piqo->pqi", grad_imag, w_imag
    )
    in_imag = contract("pqo,piqo->pqi", grad_imag, w_real) - contract(
        "pqo,piqo->pqi", grad_real, w_imag
    )
    return jnp.stack([in_real, in_imag], axis=2)


def mode_grad(mode_data, grad_modes):
    pair_total, kx_total, _, channels = mode_data.shape
    in_real = mode_data[:, :, 0]
    in_imag = mode_data[:, :, 1]
    grad_real = grad_modes[:, :, 0]
    grad_imag = grad_modes[:, :, 1]
    dw_real = contract("pqi,pqo->piqo", in_real, grad_real) + contract(
        "pqi,pqo->piqo", in_imag, grad_imag
    )
    dw_imag = contract("pqi,pqo->piqo", in_real, grad_imag) - contract(
        "pqi,pqo->piqo", in_imag, grad_real
    )
    return jnp.stack([dw_real, dw_imag], axis=1).reshape(
        pair_total, 2, channels, kx_total * channels
    )


def per_device(flow_field, cotangent, spec_weight, point_weight, pointwise_bias):
    slab_rows, channels, ny_cells, nz_cells = flow_field.shape
    devices_space = lax.axis_size("space")
    device_id = lax.axis_index("space")
    nx_cells = slab_rows * devices_space
    pair_local = spec_weight.shape[0]
    kx_count = 2 * MODES
    pair_count = 2 * MODES * MODES
    fwd_scale = float(nx_cells * ny_cells * nz_cells) ** (-0.5)
    inv_scale = float(4 * MODES**3) ** (-0.5)
    kz_modes = jnp.arange(MODES, dtype=jnp.int32)
    z_cos, z_sin = phase_table(jnp.arange(nz_cells, dtype=jnp.int32), kz_modes, nz_cells)
    y_cos, y_sin = phase_table(
        jnp.arange(ny_cells, dtype=jnp.int32), signed_modes(2 * MODES), ny_cells
    )
    kx_modes = signed_modes(kx_count)
    full_cos, full_sin = phase_table(jnp.arange(nx_cells, dtype=jnp.int32), kx_modes, nx_cells)
    z_factor = jnp.where(kz_modes == 0, 1.0, 2.0).astype(jnp.float32)
    own_pairs = device_id * pair_local + jnp.arange(pair_local, dtype=jnp.int32)
    own_factor = jnp.where(own_pairs % MODES == 0, 1.0, 2.0).astype(jnp.float32)

    def to_modes(spectrum):
        blocks = spectrum.reshape(slab_rows, devices_space, pair_local, 2 * channels)
        portion = lax.all_to_all(blocks, "space", split_axis=1, concat_axis=0, tiled=True)
        item_total = portion.shape[2]
        return x_forward(portion.reshape(nx_cells, item_total, 2, channels), full_cos, full_sin)

    def to_slab(mode_data):
        columns = x_inverse(mode_data, full_cos, full_sin).reshape(
            nx_cells, 1, pair_local * 2 * channels
        )
        moved = lax.all_to_all(columns, "space", split_axis=0, concat_axis=1, tiled=True)
        return moved.reshape(slab_rows, pair_count, 2, channels)

    spec_in = to_modes(yz_forward(flow_field, z_cos, z_sin, y_cos, y_sin)) * fwd_scale
    spec_out = mode_mix(spec_in, spec_weight)
    spectral = yz_inverse(to_slab(spec_out), z_cos, z_sin, y_cos, y_sin, inv_scale * z_factor)
    pre_act = (
        spectral
        + contract("xiyz,io->xoyz", flow_field, point_weight)
        + pointwise_bias[None, :, None, None]
    )
    output, gelu_pull = jax.vjp(jax.nn.gelu, pre_act)
    grad_pre = gelu_pull(cotangent)[0]
    local_weight = contract("xiyz,xoyz->io", flow_field, grad_pre)
    local_bias = jnp.sum(grad_pre, axis=(0, 2, 3))
    summed_weight, summed_bias = lax.psum((local_weight, local_bias), "space")
    grad_modes = (
        to_modes(yz_forward(grad_pre, z_cos, z_sin, y_cos, y_sin))
        * (inv_scale * own_factor)[:, None, None, None]
    )
    grad_spec = mode_grad(spec_in, grad_modes)
    grad_in = mode_adjoint(grad_modes, spec_weight)
    unit_weights = jnp.full((MODES,), fwd_scale, jnp.float32)
    grad_field = yz_inverse(to_slab(grad_in), z_cos, z_sin, y_cos, y_sin, unit_weights) + contract(
        "xoyz,io->xiyz", grad_pre, point_weight
    )
    return (output, grad_field, grad_spec, summed_weight * fwd_scale, summed_bias * fwd_scale)


def solution(mesh):
    in_specs = (
        P(("group", "space"), None, None, None),
        P(("group", "space"), None, None, None),
        P("space", None, None, None),
        P(),
        P(),
    )
    out_specs = (
        P(("group", "space"), None, None, None),
        P(("group", "space"), None, None, None),
        P(("group", "space"), None, None, None),
        P("group", None),
        P("group"),
    )
    return jax.shard_map(
        per_device, mesh=mesh, in_specs=in_specs, out_specs=out_specs, check_vma=False
    )
```

profile of v0, /device:TPU:0, one launch (start us, length us, event | category | flops | bytes accessed | tf_op | source)
XLA Modules:
  0.0 536.7 jit_solution(10518263123060271754)
XLA Ops:
  0.7 5.5 %fusion.14 = f32[2,32,128,16]{2,3,1,0:T(8,128)S(1)} fusion(f32[2,32,128,128]{3,2,1,0:T(8,128)} %param.5), kind=kOutput, calls=%fused_computation.26 | convolution fusion | flops 201486336 | bytes 4718592 | tf_op jit(solution)/shard_map/xcyz,zk->xcyk/dot_general | solution.py:15
  6.2 3.6 convolution_bitcast_fusion
  9.7 2.6 fusion.46
  12.3 2.6 fusion.50
  14.9 2.6 fusion.29
  18.0 2.6 fusion.30
  21.8 1.0 reshape.124
  22.8 7.8 %all-to-all-start = ((f32[16,1,4096]{2,1,0:T(1,128)}), f32[16,1,4096]{2,1,0:T(1,128)S(1)}, u32[]{:S(2)}, u32[]{:S(2)}) async-start(f32[16,1,4096]{2,1,0:T(1,128)} %reshape.124), calls=%async_computation | async-start | bytes 524288 | tf_op jit(solution)/shard_map/all_to_all | solution.py:156
  30.7 21.8 %reshape.82 = f32[32,2,32,32,32]{4,3,2,1,0:T(8,128)} reshape(f32[32,2,32,1024]{3,2,1,0:T(8,128)} %param.7) | data formatting | bytes 16777216 | tf_op jit(solution)/shard_map/reshape | solution.py:86
  52.5 21.3 %slice_bitcast_fusion = (f32[32,32,32,32]{3,2,1,0:T(8,128)}, f32[32,32,32,32]{3,2,1,0:T(8,128)}) fusion(f32[32,2,32,32,32]{4,3,2,1,0:T(8,128)} %reshape.82), kind=kLoop, calls=%fused_computation | loop fusion | bytes 16777216 | tf_op jit(solution)/shard_map/squeeze | solution.py:87
  73.8 18.9 %copy.202 = f32[32,32,32,32]{1,3,2,0:T(8,128)} copy(f32[32,32,32,32]{3,2,1,0:T(8,128)} %get-tuple-element.30) | data formatting | bytes 8388608 | tf_op jit(solution)/shard_map/squeeze | solution.py:87
  92.6 18.9 %copy.205 = f32[32,32,32,32]{1,3,2,0:T(8,128)} copy(f32[32,32,32,32]{3,2,1,0:T(8,128)} %get-tuple-element.29) | data formatting | bytes 8388608 | tf_op jit(solution)/shard_map/squeeze | solution.py:87
  112.0 1.2 reduce
  114.2 1.2 fusion.355
  115.3 0.9 fusion.37
  116.3 0.9 fusion.36
  117.2 0.9 fusion.27
  118.2 0.9 fusion.28
  119.5 29.6 %fusion.356 = f32[32,32,1,32]{3,2,1,0:T(1,128)S(1)} fusion(f32[32,32,32,1]{2,3,1,0:T(1,128)S(1)} %bitcast.342, f32[32,32,32,32]{1,3,2,0:T(8,128)} %copy.202), kind=kOutput, calls=%fused_computation.375 | convolution fusion | flops 12582912 | bytes 4456448 | tf_op jit(solution)/shard_map/pqi,piqo->pqo/dot_general | solution.py:15
  149.2 26.5 %fusion.358 = f32[32,32,1,32]{3,2,1,0:T(1,128)S(1)} fusion(f32[32,32,32,1]{2,3,1,0:T(1,128)S(1)} %bitcast.344, f32[32,32,32,32]{1,3,2,0:T(8,128)S(1)} %bitcast.333), kind=kOutput, calls=%fused_computation.377 | convolution fusion | flops 12582912 | bytes 4456448 | tf_op jit(solution)/shard_map/pqi,piqo->pqo/dot_general | solution.py:15
  175.7 26.5 %fusion.357 = f32[32,32,1,32]{3,2,1,0:T(1,128)S(1)} fusion(f32[32,32,32,1]{2,3,1,0:T(1,128)S(1)} %bitcast.345, f32[32,32,32,32]{1,3,2,0:T(8,128)S(1)} %bitcast.337), kind=kOutput, calls=%fused_computation.376 | convolution fusion | flops 12582912 | bytes 4456448 | tf_op jit(solution)/shard_map/pqi,piqo->pqo/dot_general | solution.py:15
  202.3 26.9 %fusion.359 = f32[32,32,1,32]{3,2,1,0:T(1,128)S(1)} fusion(f32[32,32,32,1]{2,3,1,0:T(1,128)S(1)} %bitcast.343, f32[32,32,32,32]{1,3,2,0:T(8,128)S(1)} %bitcast.337), kind=kOutput, calls=%fused_computation.378 | convolution fusion | flops 12582912 | bytes 4456448 | tf_op jit(solution)/shard_map/pqi,piqo->pqo/dot_general | solution.py:15
  231.9 0.8 copy.139
  232.7 1.8 reshape.122
  234.5 6.1 %all-to-all-start.1 = ((f32[32,1,2048]{2,1,0:T(1,128)}), f32[32,1,2048]{2,1,0:T(1,128)S(1)}, u32[]{:S(2)}, u32[]{:S(2)}) async-start(f32[32,1,2048]{2,1,0:T(1,128)} %reshape.122), calls=%async_computation.1 | async-start | bytes 524288 | tf_op jit(solution)/shard_map/all_to_all | solution.py:164
  240.6 9.8 %fusion.12 = f32[32,2,128,128]{3,0,2,1:T(8,128)} fusion(f32[2,32,128,128]{3,2,1,0:T(8,128)} %param.5, f32[32,32]{1,0:T(8,128)S(1)} %copy-done), kind=kOutput, calls=%fused_computation.21 | convolution fusion | flops 402653184 | bytes 8392704 | tf_op jit(solution)/shard_map/xiyz,io->xoyz/dot_general | solution.py:15
  251.0 0.9 reshape.84
  251.9 1.6 fusion.354
  255.3 1.4 copy.143
  258.1 7.1 %fusion.121 = f32[2,32,128,128]{3,2,1,0:T(8,128)S(1)} fusion(f32[2,32,128,16]{2,3,1,0:T(8,128)S(1)} %fusion.24, f32[16]{0:T(128)S(1)} %fusion.185), kind=kOutput, calls=%fused_computation.167 | convolution fusion | flops 201357312 | bytes 4718656 | tf_op jit(solution)/shard_map/xcyk,zk->xcyz/dot_general | solution.py:15
  265.2 17.3 %fusion.350 = (f32[32]{0:T(128)S(1)}, f32[2,32,128,128]{3,2,1,0:T(8,128)S(1)}, f32[2,32,128,128]{3,2,1,0:T(8,128)}) fusion(f32[2,32,128,128]{3,2,1,0:T(8,128)} %param.6, f32[32]{0:T(128)S(1)} %copy-done.6, f32[32,2,128,128]{3,0,2,1:T(8,128)S(1)} %copy-done.5, f32[2,32,128,128]{3,2,1,0:T(8,128)S(1)} %fusion.121, f32[2,32,128,16]{2,3,1,0:T(8,128)S(1)} %fusion.23, ...), kind=kOutput, calls=%fused_computation.368 | convolution fusion | flops 226523104 | bytes 21496128 | tf_op jit(solution)/shard_map/xcyk,zk->xcyz/dot_general | solution.py:15
  282.6 3.7 convolution_negate_fusion
  286.2 3.6 fusion.125
  289.9 8.4 %fusion.31 = f32[32,32]{0,1:T(8,128)S(1)} fusion(f32[2,32,128,128]{3,2,1,0:T(8,128)S(1)} %copy-done.3, f32[2,32,128,128]{3,2,1,0:T(8,128)S(1)} %get-tuple-element.28), kind=kOutput, calls=%fused_computation.60 | convolution fusion | flops 402653184 | bytes 8392704 | tf_op jit(solution)/shard_map/xiyz,xoyz->io/dot_general | solution.py:15
  298.3 2.6 fusion.40
  300.9 2.6 fusion.44
  303.5 2.6 fusion.21
  306.5 2.6 fusion.22
  310.4 1.0 reshape.126
  311.4 6.0 %all-to-all-start.2 = ((f32[16,1,4096]{2,1,0:T(1,128)}), f32[16,1,4096]{2,1,0:T(1,128)S(1)}, u32[]{:S(2)}, u32[]{:S(2)}) async-start(f32[16,1,4096]{2,1,0:T(1,128)} %reshape.126), calls=%async_computation.2 | async-start | bytes 524288 | tf_op jit(solution)/shard_map/all_to_all | solution.py:156
  317.4 62.4 %all-reduce = (f32[32,32]{0,1:T(8,128)S(1)}, f32[32]{0:T(128)S(1)}) all-reduce(f32[32,32]{0,1:T(8,128)S(1)} %fusion.31, f32[32]{0:T(128)S(1)} %get-tuple-element.27), channel_id=1, replica_groups=mesh['group'=2,'space'=16] {'space'}, use_global_device_ids=true, to_apply=%region_0.1 | all-reduce | flops 1056 | bytes 8448 | tf_op jit(solution)/shard_map/psum | solution.py:179
  381.0 10.3 %fusion.9 = f32[2,128,128,32]{2,3,1,0:T(8,128)} fusion(f32[2,32,128,128]{3,2,1,0:T(8,128)} %copy-done.1, f32[32,32]{1,0:T(8,128)S(1)} %copy-done), kind=kOutput, calls=%fused_computation.18 | convolution fusion | flops 402653184 | bytes 8392704 | tf_op jit(solution)/shard_map/xoyz,io->xiyz/dot_general | solution.py:15
  391.4 1.2 reduce.1
  393.5 1.2 fusion.353
  394.6 0.9 fusion.39
  395.6 0.9 fusion.38
  396.5 0.9 fusion.19
  397.5 1.1 fusion.20
  398.9 16.1 %fusion.361 = f32[32,32,1,32]{3,2,1,0:T(1,128)S(1)} fusion(f32[32,32,32,1]{2,3,1,0:T(1,128)S(1)} %bitcast.346, f32[32,32,32,32]{1,3,2,0:T(8,128)} %copy.205), kind=kOutput, calls=%fused_computation.380 | convolution fusion | flops 12582912 | bytes 4456448 | tf_op jit(solution)/shard_map/pqo,piqo->pqi/dot_general | solution.py:15
  415.1 13.5 %fusion.362 = f32[32,32,1,32]{3,2,1,0:T(1,128)S(1)} fusion(f32[32,32,32,1]{2,3,1,0:T(1,128)S(1)} %bitcast.347, f32[32,32,32,32]{1,3,2,0:T(8,128)S(1)} %bitcast.335), kind=kOutput, calls=%fused_computation.381 | convolution fusion | flops 12582912 | bytes 4456448 | tf_op jit(solution)/shard_map/pqo,piqo->pqi/dot_general | solution.py:15
  428.7 13.7 %fusion.360 = f32[32,32,1,32]{3,2,1,0:T(1,128)S(1)} fusion(f32[32,32,32,1]{2,3,1,0:T(1,128)S(1)} %bitcast.340, f32[32,32,32,32]{1,3,2,0:T(8,128)S(1)} %bitcast.335), kind=kOutput, calls=%fused_computation.379 | convolution fusion | flops 12582912 | bytes 4456448 | tf_op jit(solution)/shard_map/pqo,piqo->pqi/dot_general | solution.py:15
  442.4 13.9 %fusion.363 = f32[32,32,1,32]{3,2,1,0:T(1,128)S(1)} fusion(f32[32,32,32,1]{2,3,1,0:T(1,128)S(1)} %bitcast.341, f32[32,32,32,32]{1,3,2,0:T(8,128)S(1)} %bitcast.339), kind=kOutput, calls=%fused_computation.382 | convolution fusion | flops 12582912 | bytes 4456448 | tf_op jit(solution)/shard_map/pqo,piqo->pqi/dot_general | solution.py:15
  459.1 0.8 copy.164
  459.9 1.8 reshape.123
  461.7 3.5 all-to-all-start.3
  465.2 11.6 %add_bitcast_fusion = (f32[32,32,32,32]{3,2,1,0:T(8,128)}, f32[32,32,32,32]{3,2,1,0:T(8,128)}) fusion(f32[32,32,32]{1,2,0:T(8,128)S(1)} %copy.174, f32[32,32,32]{2,1,0:T(8,128)S(1)} %get-tuple-element.35, f32[32,32,32]{1,2,0:T(8,128)S(1)} %copy.173, f32[32,32,32]{2,1,0:T(8,128)S(1)} %get-tuple-element.34), kind=kLoop, calls=%fused_computation.3 | loop fusion | flops 6291456 | bytes 8912896 | tf_op jit(solution)/shard_map/add | solution.py:122
  476.9 13.7 %stack.66 = f32[32,1,32,1024]{3,2,1,0:T(8,128)} reshape(f32[32,32,32,32]{3,2,1,0:T(8,128)} %get-tuple-element.33) | data formatting | bytes 8388608 | tf_op jit(solution)/shard_map/stack | solution.py:128
  490.6 13.8 %stack.65 = f32[32,1,32,1024]{3,2,1,0:T(8,128)} reshape(f32[32,32,32,32]{3,2,1,0:T(8,128)} %get-tuple-element.32) | data formatting | bytes 8388608 | tf_op jit(solution)/shard_map/stack | solution.py:128
  504.4 8.5 %pad_maximum_fusion = f32[32,2,32,1024]{3,2,1,0:T(8,128)} fusion(f32[32,1,32,1024]{3,2,1,0:T(8,128)} %stack.66, f32[32,1,32,1024]{3,2,1,0:T(8,128)} %stack.65), kind=kLoop, calls=%fused_computation.4 | loop fusion | flops 2097152 | bytes 16777216 | tf_op jit(solution)/shard_map/stack | solution.py:128
  513.1 0.9 reshape.88
  514.0 0.8 fusion.352
  517.7 6.9 %fusion.118 = f32[2,32,128,128]{3,2,1,0:T(8,128)S(1)} fusion(f32[2,32,128,16]{2,3,1,0:T(8,128)S(1)} %fusion.16), kind=kOutput, calls=%fused_computation.164 | convolution fusion | flops 201357312 | bytes 4718592 | tf_op jit(solution)/shard_map/xcyk,zk->xcyz/dot_general | solution.py:15
  524.6 0.7 fusion.15
  525.3 11.1 %bitcast_add_fusion = f32[2,32,128,128]{3,2,1,0:T(8,128)} fusion(f32[2,128,128,32]{2,3,1,0:T(8,128)S(1)} %copy-done.4, f32[2,32,128,128]{3,2,1,0:T(8,128)S(1)} %fusion.118, f32[2,32,128,16]{2,3,1,0:T(8,128)S(1)} %fusion.15), kind=kOutput, calls=%fused_computation.13 | convolution fusion | flops 203454464 | bytes 13107200 | tf_op jit(solution)/shard_map/xcyk,zk->xcyz/dot_general | solution.py:15
  (109 shorter events, 19.7 us)
Async XLA Ops:
  0.6 240.0 %copy-start = (f32[32,32]{1,0:T(8,128)S(1)}, f32[32,32]{1,0:T(8,128)}, u32[]{:S(2)}) copy-start(f32[32,32]{1,0:T(8,128)} %param.8) | copy-start | bytes 12292
  0.6 5.5 %copy-start.2 = (f32[2,32,128,128]{3,2,1,0:T(8,128)S(1)}, f32[2,32,128,128]{3,2,1,0:T(8,128)}, u32[]{:S(2)}) copy-start(f32[2,32,128,128]{3,2,1,0:T(8,128)} %param.5) | copy-start | bytes 12582916
  22.8 88.7 %all-to-all-start = ((f32[16,1,4096]{2,1,0:T(1,128)}), f32[16,1,4096]{2,1,0:T(1,128)S(1)}, u32[]{:S(2)}, u32[]{:S(2)}) async-start(f32[16,1,4096]{2,1,0:T(1,128)} %reshape.124), calls=%async_computation | async-start | bytes 524288 | tf_op jit(solution)/shard_map/all_to_all | solution.py:156
  119.1 30.0 %slice-start = ((s8[16777216]{0:T(1024)(128)(4,1)}), s8[4194304]{0:T(1024)(128)(4,1)S(1)}, s32[]{:S(2)}) async-start(s8[16777216]{0:T(1024)(128)(4,1)} %bitcast.332), calls=%async_computation.4 | async-start | bytes 8388608
  119.4 29.7 %slice-start.1 = ((s8[16777216]{0:T(1024)(128)(4,1)}), s8[4194304]{0:T(1024)(128)(4,1)S(1)}, s32[]{:S(2)}) async-start(s8[16777216]{0:T(1024)(128)(4,1)} %bitcast.332), calls=%async_computation.5 | async-start | bytes 8388608
  119.4 29.7 %slice-start.2 = ((s8[16777216]{0:T(1024)(128)(4,1)}), s8[4194304]{0:T(1024)(128)(4,1)S(1)}, s32[]{:S(2)}) async-start(s8[16777216]{0:T(1024)(128)(4,1)} %bitcast.332), calls=%async_computation.6 | async-start | bytes 8388608
  119.5 29.7 %slice-start.3 = ((s8[16777216]{0:T(1024)(128)(4,1)}), s8[4194304]{0:T(1024)(128)(4,1)S(1)}, s32[]{:S(2)}) async-start(s8[16777216]{0:T(1024)(128)(4,1)} %bitcast.332), calls=%async_computation.7 | async-start | bytes 8388608
  119.5 56.2 %slice-start.8 = ((s8[16777216]{0:T(1024)(128)(4,1)}), s8[4194304]{0:T(1024)(128)(4,1)S(1)}, s32[]{:S(2)}) async-start(s8[16777216]{0:T(1024)(128)(4,1)} %bitcast.336), calls=%async_computation.12 | async-start | bytes 8388608
  119.5 56.2 %slice-start.9 = ((s8[16777216]{0:T(1024)(128)(4,1)}), s8[4194304]{0:T(1024)(128)(4,1)S(1)}, s32[]{:S(2)}) async-start(s8[16777216]{0:T(1024)(128)(4,1)} %bitcast.336), calls=%async_computation.13 | async-start | bytes 8388608
  149.1 26.6 %slice-start.10 = ((s8[16777216]{0:T(1024)(128)(4,1)}), s8[4194304]{0:T(1024)(128)(4,1)S(1)}, s32[]{:S(2)}) async-start(s8[16777216]{0:T(1024)(128)(4,1)} %bitcast.336), calls=%async_computation.14 | async-start | bytes 8388608
  149.2 26.5 %slice-start.11 = ((s8[16777216]{0:T(1024)(128)(4,1)}), s8[4194304]{0:T(1024)(128)(4,1)S(1)}, s32[]{:S(2)}) async-start(s8[16777216]{0:T(1024)(128)(4,1)} %bitcast.336), calls=%async_computation.15 | async-start | bytes 8388608
  234.5 16.3 %all-to-all-start.1 = ((f32[32,1,2048]{2,1,0:T(1,128)}), f32[32,1,2048]{2,1,0:T(1,128)S(1)}, u32[]{:S(2)}, u32[]{:S(2)}) async-start(f32[32,1,2048]{2,1,0:T(1,128)} %reshape.122), calls=%async_computation.1 | async-start | bytes 524288 | tf_op jit(solution)/shard_map/all_to_all | solution.py:164
  256.6 8.6 %copy-start.5 = (f32[32,2,128,128]{3,0,2,1:T(8,128)S(1)}, f32[32,2,128,128]{3,0,2,1:T(8,128)}, u32[]{:S(2)}) copy-start(f32[32,2,128,128]{3,0,2,1:T(8,128)} %fusion.12) | copy-start | bytes 12582916
  256.7 8.6 %copy-start.6 = (f32[32]{0:T(128)S(1)}, f32[32]{0:T(128)}, u32[]{:S(2)}) copy-start(f32[32]{0:T(128)} %param.9) | copy-start | bytes 388
  282.6 7.3 %copy-start.1 = (f32[2,32,128,128]{3,2,1,0:T(8,128)}, f32[2,32,128,128]{3,2,1,0:T(8,128)S(1)}, u32[]{:S(2)}) copy-start(f32[2,32,128,128]{3,2,1,0:T(8,128)S(1)} %get-tuple-element.28) | copy-start | bytes 12582916
  282.6 7.3 %copy-start.3 = (f32[2,32,128,128]{3,2,1,0:T(8,128)S(1)}, f32[2,32,128,128]{3,2,1,0:T(8,128)}, u32[]{:S(2)}) copy-start(f32[2,32,128,128]{3,2,1,0:T(8,128)} %param.5) | copy-start | bytes 12582916
  311.4 79.9 %all-to-all-start.2 = ((f32[16,1,4096]{2,1,0:T(1,128)}), f32[16,1,4096]{2,1,0:T(1,128)S(1)}, u32[]{:S(2)}, u32[]{:S(2)}) async-start(f32[16,1,4096]{2,1,0:T(1,128)} %reshape.126), calls=%async_computation.2 | async-start | bytes 524288 | tf_op jit(solution)/shard_map/all_to_all | solution.py:156
  397.5 17.6 %slice-start.4 = ((s8[16777216]{0:T(1024)(128)(4,1)}), s8[4194304]{0:T(1024)(128)(4,1)S(1)}, s32[]{:S(2)}) async-start(s8[16777216]{0:T(1024)(128)(4,1)} %bitcast.334), calls=%async_computation.8 | async-start | bytes 8388608
  398.9 16.2 %slice-start.5 = ((s8[16777216]{0:T(1024)(128)(4,1)}), s8[4194304]{0:T(1024)(128)(4,1)S(1)}, s32[]{:S(2)}) async-start(s8[16777216]{0:T(1024)(128)(4,1)} %bitcast.334), calls=%async_computation.9 | async-start | bytes 8388608
  398.9 16.2 %slice-start.6 = ((s8[16777216]{0:T(1024)(128)(4,1)}), s8[4194304]{0:T(1024)(128)(4,1)S(1)}, s32[]{:S(2)}) async-start(s8[16777216]{0:T(1024)(128)(4,1)} %bitcast.334), calls=%async_computation.10 | async-start | bytes 8388608
  398.9 16.2 %slice-start.7 = ((s8[16777216]{0:T(1024)(128)(4,1)}), s8[4194304]{0:T(1024)(128)(4,1)S(1)}, s32[]{:S(2)}) async-start(s8[16777216]{0:T(1024)(128)(4,1)} %bitcast.334), calls=%async_computation.11 | async-start | bytes 8388608
  415.1 27.3 %slice-start.12 = ((s8[16777216]{0:T(1024)(128)(4,1)}), s8[4194304]{0:T(1024)(128)(4,1)S(1)}, s32[]{:S(2)}) async-start(s8[16777216]{0:T(1024)(128)(4,1)} %bitcast.338), calls=%async_computation.16 | async-start | bytes 8388608
  415.1 27.3 %slice-start.13 = ((s8[16777216]{0:T(1024)(128)(4,1)}), s8[4194304]{0:T(1024)(128)(4,1)S(1)}, s32[]{:S(2)}) async-start(s8[16777216]{0:T(1024)(128)(4,1)} %bitcast.338), calls=%async_computation.17 | async-start | bytes 8388608
  428.6 13.8 %slice-start.14 = ((s8[16777216]{0:T(1024)(128)(4,1)}), s8[4194304]{0:T(1024)(128)(4,1)S(1)}, s32[]{:S(2)}) async-start(s8[16777216]{0:T(1024)(128)(4,1)} %bitcast.338), calls=%async_computation.18 | async-start | bytes 8388608
  428.7 13.8 %slice-start.15 = ((s8[16777216]{0:T(1024)(128)(4,1)}), s8[4194304]{0:T(1024)(128)(4,1)S(1)}, s32[]{:S(2)}) async-start(s8[16777216]{0:T(1024)(128)(4,1)} %bitcast.338), calls=%async_computation.19 | async-start | bytes 8388608
  461.7 51.2 %all-to-all-start.3 = ((f32[32,1,2048]{2,1,0:T(1,128)}), f32[32,1,2048]{2,1,0:T(1,128)S(1)}, u32[]{:S(2)}, u32[]{:S(2)}) async-start(f32[32,1,2048]{2,1,0:T(1,128)} %reshape.123), calls=%async_computation.3 | async-start | bytes 524288 | tf_op jit(solution)/shard_map/all_to_all | solution.py:164
  516.9 8.4 %copy-start.4 = (f32[2,128,128,32]{2,3,1,0:T(8,128)S(1)}, f32[2,128,128,32]{2,3,1,0:T(8,128)}, u32[]{:S(2)}) copy-start(f32[2,128,128,32]{2,3,1,0:T(8,128)} %fusion.9) | copy-start | bytes 12582916
where the time goes:
time: 547 us; the launch traced here: 537 us
  matrix products  293 us (54%)
  local copies, waits for them, and re-layouts  132 us (24%)
  blocking collectives  62.4 us (11%)
  other arithmetic  23.7 us (4%)
  starting transfers between devices  23.5 us (4%)
    dot_general x51, matrix products, contract(): return jnp.einsum(form, left, right, precision=highest)  293 us
    psum x1, blocking collectives, per_device(): summed_weight, summed_bias = lax.psum((local_weight, local_bias), 'space')  62.4 us
    squeeze x3, local copies, waits for them, and re-layouts, split_weight(): return (shaped[:, 0], shaped[:, 1])  59 us
    another operation x2, local copies, waits for them, and re-layouts, mode_grad(): jnp.stack([dw_real, dw_imag], axis=1)  27.5 us
    reshape x1, local copies, waits for them, and re-layouts, split_weight(): shaped = weights.reshape(pair_total, 2, channels, kx_total, channels)  21.8 us
    all_to_all x2, starting transfers between devices, to_modes(): lax.all_to_all(blocks, 'space', split_axis=1, concat_axis=0, tiled=True)  13.8 us
    add x1, other arithmetic, mode_grad(): contract('pqi,pqo->piqo', in_real, grad_real)  11.6 us
  transfers between devices with their start and end apart: 4, of which 0 were waited for; matrix products, arithmetic and copies ran while one was open for 28% of the time, Pallas kernels for 0%

commit v1 on v0

v1 whole, which is shorter than its diff:
```python
import functools
import math

import jax
import jax.numpy as jnp
import ml_dtypes
import numpy as np
from jax import lax
from jax.experimental import pallas as pl
from jax.experimental.pallas import tpu as pltpu
from jax.sharding import PartitionSpec as P

MODES = 16
KY = 2 * MODES
KX = 2 * MODES
MIB = 1024 * 1024
NT = (((1,), (1,)), ((), ()))
TN = (((0,), (0,)), ((), ()))
f32 = jnp.float32
bf16 = jnp.bfloat16


def signed(n):
    j = np.arange(n)
    return np.where(j < n // 2, j, j - n)


def phases(positions, waves, length):
    angle = ((positions[:, None] * waves[None, :]) % length) * (2.0 * math.pi / length)
    return np.cos(angle), np.sin(angle)


def halves(table):
    table = np.asarray(table, np.float32)
    high = table.astype(ml_dtypes.bfloat16)
    low = (table - high.astype(np.float32)).astype(ml_dtypes.bfloat16)
    return high, low


def stack3(table, axis):
    high, low = halves(table)
    return np.concatenate([high, high, low], axis=axis)


def y_table(ny):
    cos, sin = phases(np.arange(ny), signed(KY), ny)
    return np.concatenate([cos.T, -sin.T], axis=0)


def z_table(nz, scale, factor):
    cos, sin = phases(np.arange(nz), np.arange(MODES), nz)
    weight = scale * np.where(np.arange(MODES) == 0, 1.0, factor)
    cos, sin = cos.T * weight[:, None], sin.T * weight[:, None]
    real = np.concatenate([cos, sin], axis=1)
    imag = np.concatenate([-sin, cos], axis=1)
    both = np.stack([real, imag], axis=1).reshape(4, 4, 2, 2 * nz)
    return both.transpose(1, 0, 2, 3).reshape(2 * MODES, 2 * nz)


def x_forward_table(nx, scale):
    cos, sin = phases(np.arange(nx), signed(KX), nx)
    top = np.concatenate([cos, -sin], axis=1)
    bottom = np.concatenate([sin, cos], axis=1)
    return scale * np.concatenate([top, bottom], axis=0)


def x_inverse_table(nx):
    cos, sin = phases(np.arange(nx), signed(KX), nx)
    top = np.concatenate([cos, -sin], axis=1)
    bottom = np.concatenate([sin, cos], axis=1)
    return np.concatenate([top, bottom], axis=0)


def by_low(table, axis):
    order = np.arange(2 * KX).reshape(2, KX // 4, 4).transpose(0, 2, 1).reshape(-1)
    return np.take(table, order, axis=axis)


def split(values):
    high = values.astype(bf16)
    low = (values - high.astype(f32)).astype(bf16)
    return high, low


def data3(values):
    high, low = split(values)
    return jnp.concatenate([high, low, high], axis=0)


def dot(left, right, dims=(((1,), (0,)), ((), ()))):
    return lax.dot_general(left, right, dims, preferred_element_type=f32)


def group_transpose(tiles):
    group = lax.broadcasted_iota(jnp.int32, tiles[0].shape, 1) // 32
    result = []
    for m in range(4):
        moved = [pltpu.roll(tiles[n], ((n - m) * 32) % 128, 1) if n != m else tiles[n] for n in range(4)]
        low = jnp.where(group == 0, moved[0], moved[1])
        high = jnp.where(group == 2, moved[2], moved[3])
        result.append(jnp.where(group < 2, low, high))
    return result


def block_row(ky, plane, slab, ky_own):
    return (((ky // ky_own) * slab + plane) * ky_own + ky % ky_own) * 8


def forward_plane(load_channel, channels, fy_ref, tz_ref, scratch, out_ref, row_of):
    nz = scratch.shape[1]
    size = KY * channels
    for c in range(0, channels, 2):
        pair = jnp.concatenate([load_channel(c), load_channel(c + 1)], axis=1)
        high, low = split(pair)
        both = dot(fy_ref[...], jnp.concatenate([high, low], axis=0))
        half = both[: 2 * KY] + both[2 * KY :]
        for e in range(2):
            for part in range(2):
                scratch[pl.ds(part * size + c + e, KY, stride=channels), :] = half[
                    part * KY : (part + 1) * KY, e * nz : (e + 1) * nz
                ]
    high, low = split(jnp.concatenate([scratch[:size], scratch[size:]], axis=1))
    first = dot(tz_ref[...], high, NT)
    rows = first[: 2 * MODES] + first[2 * MODES :] + dot(tz_ref[: 2 * MODES, :], low, NT)
    for q in range(KY // 4):
        tiles = [rows[8 * j : 8 * j + 8, q * 128 : (q + 1) * 128] for j in range(4)]
        for e, tile in enumerate(group_transpose(tiles)):
            out_ref[pl.ds(row_of(4 * q + e), 8), :] = tile


def inverse_plane(in_ref, row_of, tz_ref, ty_ref, scratch, channels, emit):
    nz = scratch.shape[1]
    size = KY * channels
    columns = [[] for _ in range(4)]
    for q in range(KY // 4):
        tiles = [in_ref[pl.ds(row_of(4 * q + e), 8), :] for e in range(4)]
        for j, tile in enumerate(group_transpose(tiles)):
            columns[j].append(tile)
    rows = jnp.concatenate([jnp.concatenate(c, axis=1) for c in columns], axis=0)
    modes = dot(data3(rows), tz_ref[...], TN)
    for part in range(2):
        scratch[part * size : (part + 1) * size, :] = modes[:, part * nz : (part + 1) * nz]
    for c in range(0, channels, 2):
        sides = []
        for e in range(2):
            parts = [
                scratch[pl.ds(part * size + c + e, KY, stride=channels), :] for part in range(2)
            ]
            sides.append(jnp.concatenate(parts, axis=0))
        pair = dot(ty_ref[...], data3(jnp.concatenate(sides, axis=1)))
        for e in range(2):
            emit(c + e, pair[:, e * nz : (e + 1) * nz])


def spread_weight(weight, high_ref, low_ref):
    size = weight.shape[0]
    row = lax.broadcasted_iota(jnp.int32, (8 * size, size), 0) // 8
    column = lax.broadcasted_iota(jnp.int32, (8 * size, size), 1)
    expand = (row == column).astype(f32)
    tall = lax.dot_general(
        expand, weight, (((1,), (0,)), ((), ())), precision=lax.Precision.HIGHEST, preferred_element_type=f32
    )
    wide = lax.dot_general(tall, expand, NT, precision=lax.Precision.HIGHEST, preferred_element_type=f32)
    row = lax.broadcasted_iota(jnp.int32, wide.shape, 0) % 8
    column = lax.broadcasted_iota(jnp.int32, wide.shape, 1) % 8
    high, low = split(jnp.where(row == column, wide, 0.0))
    high_ref[...] = high
    low_ref[...] = low


def cell_tile(ref, start):
    sides = []
    for e in range(2):
        piece = ref[0, :, pl.ds(start + 8 * e, 8), :]
        sides.append(piece.reshape(piece.shape[0] * 8, piece.shape[2]))
    return jnp.concatenate(sides, axis=1)


def put_tile(ref, start, tile):
    channels, nz = ref.shape[1], ref.shape[3]
    for e in range(2):
        ref[0, :, pl.ds(start + 8 * e, 8), :] = tile[:, e * nz : (e + 1) * nz].reshape(channels, 8, nz)


def mix_cells(high_ref, low_ref, high, low):
    return dot(high_ref[...], high) + dot(low_ref[...], high) + dot(high_ref[...], low)


def first_kernel(slab, ky_own, field_ref, fy_ref, tz_ref, out_ref, scratch):
    plane = pl.program_id(0)
    forward_plane(
        lambda c: field_ref[0, c],
        field_ref.shape[1],
        fy_ref,
        tz_ref,
        scratch,
        out_ref,
        lambda ky: pl.multiple_of(block_row(ky, plane, slab, ky_own), 8),
    )


def quad_rows(ref, nx, lines, u):
    return jnp.concatenate([ref[pl.ds(2 * u + part, nx, stride=lines), :] for part in range(2)], axis=0)


def mix_kernel(nx, lines, in_ref, weight_ref, fx_ref, inv_ref, out_ref, sums):
    u = pl.program_id(0)
    wide = KX * 32
    modes = dot(data3(quad_rows(in_ref, nx, lines, u)), fx_ref[...], TN)
    tiles = [[], []]
    for j in range(4):
        real = modes[32 * j : 32 * j + 32, :wide]
        imag = modes[32 * j : 32 * j + 32, wide:]
        w_real, w_imag = weight_ref[j, 0], weight_ref[j, 1]
        products = (real * w_real - imag * w_imag, imag * w_real + real * w_imag)
        for part in range(2):
            total = jnp.sum(products[part].reshape(4, 8, wide), axis=0)
            base = (2 * j + part) * 64
            for a in range(8):
                sums[base + 8 * a : base + 8 * a + 8, :] = total[:, 128 * a : 128 * a + 128]
            tile = sums[pl.ds(base, 8, stride=8), :]
            for s in range(1, 8):
                tile = tile + sums[pl.ds(base + s, 8, stride=8), :]
            tiles[part].append(tile)
    mixed = jnp.concatenate(group_transpose(tiles[0]) + group_transpose(tiles[1]), axis=0)
    planes = dot(inv_ref[...], data3(mixed))
    for part in range(2):
        out_ref[pl.ds(2 * u + part, nx, stride=lines), :] = planes[part * nx : (part + 1) * nx]


def adjoint_kernel(
    nx, lines, in_ref, grad_ref, weight_ref, fx_ref, gx_ref, inv_ref, out_ref, dweight_ref, high_ref, low_ref
):
    u = pl.program_id(0)
    wide = KX * 32
    modes = dot(data3(quad_rows(in_ref, nx, lines, u)), fx_ref[...], TN)
    grads = dot(gx_ref[...], data3(quad_rows(grad_ref, nx, lines, u)))
    tiles = []
    for part in range(2):
        tiles.append(group_transpose([grads[part * 32 + 8 * b : part * 32 + 8 * b + 8, :] for b in range(4)]))
    for j in range(4):
        rows = slice(32 * j, 32 * j + 32)
        for a in range(8):
            cols = slice(128 * a, 128 * a + 128)
            late = slice(wide + 128 * a, wide + 128 * a + 128)
            g_real = jnp.broadcast_to(tiles[0][j][a : a + 1, :], (32, 128))
            g_imag = jnp.broadcast_to(tiles[1][j][a : a + 1, :], (32, 128))
            s_real, s_imag = modes[rows, cols], modes[rows, late]
            w_real, w_imag = weight_ref[j, 0, :, cols], weight_ref[j, 1, :, cols]
            dweight_ref[j, 0, :, cols] = s_real * g_real + s_imag * g_imag
            dweight_ref[j, 1, :, cols] = s_real * g_imag - s_imag * g_real
            high, low = split(g_real * w_real + g_imag * w_imag)
            high_ref[rows, cols], low_ref[rows, cols] = high, low
            high, low = split(g_imag * w_real - g_real * w_imag)
            high_ref[rows, late], low_ref[rows, late] = high, low
    first = dot(inv_ref[...], high_ref[...], NT)
    planes = first[: 2 * nx] + first[2 * nx :] + dot(inv_ref[: 2 * nx, :], low_ref[...], NT)
    for part in range(2):
        out_ref[pl.ds(2 * u + part, nx, stride=lines), :] = planes[part * nx : (part + 1) * nx]


def middle_kernel(
    slab,
    ky_own,
    in_ref,
    field_ref,
    cot_ref,
    weight_ref,
    bias_ref,
    tzi_ref,
    ty_ref,
    fy_ref,
    tzf_ref,
    output_ref,
    gpre_ref,
    spec_ref,
    sums_ref,
    scratch,
    pre,
    kron_high,
    kron_low,
    bias_wide,
    outer,
    total,
):
    plane = pl.program_id(0)
    channels, ny, nz = field_ref.shape[1:]
    row_of = lambda ky: pl.multiple_of(block_row(ky, plane, slab, ky_own), 8)

    @pl.when(plane == 0)
    def _():
        spread_weight(jnp.transpose(weight_ref[...]), kron_high, kron_low)
        row = lax.broadcasted_iota(jnp.int32, (8 * channels, channels), 0) // 8
        column = lax.broadcasted_iota(jnp.int32, (8 * channels, channels), 1)
        picked = jnp.where(row == column, bias_ref[...], 0.0)
        bias_wide[...] = jnp.broadcast_to(jnp.sum(picked, axis=1, keepdims=True), bias_wide.shape)
        outer[...] = jnp.zeros_like(outer)
        total[...] = jnp.zeros_like(total)

    def emit(channel, values):
        pre[0, channel] = values

    inverse_plane(in_ref, row_of, tzi_ref, ty_ref, scratch, channels, emit)

    rate = math.sqrt(2.0 / math.pi)

    def body(step, carry):
        start = pl.multiple_of(step * 16, 16)
        high, low = split(cell_tile(field_ref, start))
        values = cell_tile(pre, start) + mix_cells(kron_high, kron_low, high, low)
        values = values + jnp.concatenate([bias_wide[...]] * (2 * nz // 128), axis=1)
        square = values * values
        bent = jnp.tanh(rate * values * (1.0 + 0.044715 * square))
        half = 0.5 + 0.5 * bent
        put_tile(output_ref, start, values * half)
        slope = half + (0.5 * rate) * values * (1.0 - bent * bent) * (1.0 + (3 * 0.044715) * square)
        gpre = cell_tile(cot_ref, start) * slope
        put_tile(gpre_ref, start, gpre)
        g_high, g_low = split(gpre)
        outer[...] += dot(high, g_high, NT) + dot(low, g_high, NT) + dot(high, g_low, NT)
        total[...] += gpre
        return carry

    lax.fori_loop(0, ny // 16, body, 0)

    forward_plane(lambda c: gpre_ref[0, c], channels, fy_ref, tzf_ref, scratch, spec_ref, row_of)

    @pl.when(plane == slab - 1)
    def _():
        highest = dict(precision=lax.Precision.HIGHEST, preferred_element_type=f32)
        row = lax.broadcasted_iota(jnp.int32, outer.shape, 0) % 8
        column = lax.broadcasted_iota(jnp.int32, outer.shape, 1) % 8
        kept = jnp.where(row == column, outer[...], 0.0)
        kept = jnp.sum(kept.reshape(channels, 8, 8 * channels), axis=1)
        row = lax.broadcasted_iota(jnp.int32, (8 * channels, channels), 0) // 8
        column = lax.broadcasted_iota(jnp.int32, (8 * channels, channels), 1)
        pick = (row == column).astype(f32)
        sums_ref[:channels, :] = lax.dot_general(kept, pick, (((1,), (0,)), ((), ())), **highest)
        ones = jnp.ones((8, total.shape[1]), f32)
        line = lax.dot_general(ones, total[...], NT, **highest)
        sums_ref[channels:, :] = lax.dot_general(line, pick, (((1,), (0,)), ((), ())), **highest)


def last_kernel(
    slab, ky_own, in_ref, gpre_ref, weight_ref, tzi_ref, ty_ref, out_ref, scratch, kron_high, kron_low
):
    plane = pl.program_id(0)
    channels, ny, nz = gpre_ref.shape[1:]
    row_of = lambda ky: pl.multiple_of(block_row(ky, plane, slab, ky_own), 8)

    @pl.when(plane == 0)
    def _():
        spread_weight(weight_ref[...], kron_high, kron_low)

    def emit(channel, values):
        out_ref[0, channel] = values

    inverse_plane(in_ref, row_of, tzi_ref, ty_ref, scratch, channels, emit)

    def body(step, carry):
        start = pl.multiple_of(step * 16, 16)
        high, low = split(cell_tile(gpre_ref, start))
        put_tile(out_ref, start, cell_tile(out_ref, start) + mix_cells(kron_high, kron_low, high, low))
        return carry

    lax.fori_loop(0, ny // 16, body, 0)


def whole(array):
    zeros = (0,) * array.ndim
    return pl.BlockSpec(array.shape, lambda *_: zeros)


def params(megabytes):
    return pltpu.CompilerParams(vmem_limit_bytes=megabytes * MIB, dimension_semantics=("arbitrary",))


def per_device(flow_field, cotangent, spec_weight, point_weight, pointwise_bias):
    slab, channels, ny, nz = flow_field.shape
    devices = lax.axis_size("space")
    nx = slab * devices
    pair_local = spec_weight.shape[0]
    assert pair_local % MODES == 0 or slab == 1
    assert channels == 32 and nz == 128 and pair_local % 4 == 0
    ky_own = max(1, pair_local // MODES)
    lines = pair_local // 2
    rows = nx * lines
    quads = pair_local // 4
    wide = KX * channels
    fwd_scale = float(nx * ny * nz) ** (-0.5)
    inv_scale = float(4 * MODES**3) ** (-0.5)

    fy_high, fy_low = halves(y_table(ny))
    fy = np.concatenate(
        [np.concatenate([fy_high, fy_high], axis=1), np.concatenate([fy_low, fy_low], axis=1)], axis=0
    )
    fy = jnp.asarray(fy)
    ty = jnp.asarray(stack3(y_table(ny).T, 1))
    tz_first = jnp.asarray(np.concatenate(halves(z_table(nz, 1.0, 1.0)), axis=0))
    tz_grad = jnp.asarray(np.concatenate(halves(z_table(nz, inv_scale, 2.0)), axis=0))
    tzi_out = jnp.asarray(stack3(z_table(nz, inv_scale, 2.0), 0))
    tzi_grad = jnp.asarray(stack3(z_table(nz, fwd_scale, 1.0), 0))
    fx = x_forward_table(nx, fwd_scale)
    fx_wide = jnp.asarray(np.repeat(stack3(fx, 0), channels, axis=1))
    gx = jnp.asarray(stack3(by_low(x_forward_table(nx, 1.0), 1).T, 1))
    inv = x_inverse_table(nx)
    inv_low = jnp.asarray(stack3(by_low(inv, 1), 1))
    inv_wide = jnp.asarray(np.repeat(np.concatenate(halves(inv), axis=0), channels, axis=1))

    plane_spec = pl.BlockSpec((1, channels, ny, nz), lambda p: (p, 0, 0, 0))
    line_shape = jax.ShapeDtypeStruct((rows, 128), f32)
    line_spec = pl.BlockSpec((rows, 128), lambda p: (0, 0))
    weight_spec = pl.BlockSpec((4, 2, channels, wide), lambda u: (u, 0, 0, 0))
    field_shape = jax.ShapeDtypeStruct(flow_field.shape, f32)
    mode_scratch = pltpu.VMEM((2 * KY * channels, nz), f32)
    kron_scratch = pltpu.VMEM((8 * channels, 8 * channels), bf16)

    def exchange(lines_out):
        blocks = lines_out.reshape(devices, rows // devices, 128)
        return lax.all_to_all(blocks, "space", split_axis=0, concat_axis=0, tiled=True).reshape(rows, 128)

    first = pl.pallas_call(
        functools.partial(first_kernel, slab, ky_own),
        grid=(slab,),
        in_specs=[plane_spec, whole(fy), whole(tz_first)],
        out_specs=line_spec,
        out_shape=line_shape,
        scratch_shapes=[mode_scratch],
        compiler_params=params(40),
        name="field_forward",
    )(flow_field, fy, tz_first)
    spec_x = exchange(first)

    mixed = pl.pallas_call(
        functools.partial(mix_kernel, nx, lines),
        grid=(quads,),
        in_specs=[line_spec, weight_spec, whole(fx_wide), whole(inv_low)],
        out_specs=line_spec,
        out_shape=line_shape,
        scratch_shapes=[pltpu.VMEM((512, 128), f32)],
        compiler_params=params(40),
        name="mode_mix",
    )(spec_x, spec_weight, fx_wide, inv_low)
    mixed = exchange(mixed)

    bias = pointwise_bias.reshape(1, channels)
    output, gpre, grad_lines, local_sums = pl.pallas_call(
        functools.partial(middle_kernel, slab, ky_own),
        grid=(slab,),
        in_specs=[
            line_spec,
            plane_spec,
            plane_spec,
            whole(point_weight),
            whole(bias),
            whole(tzi_out),
            whole(ty),
            whole(fy),
            whole(tz_grad),
        ],
        out_specs=[
            plane_spec,
            plane_spec,
            line_spec,
            pl.BlockSpec((channels + 8, channels), lambda p: (0, 0)),
        ],
        out_shape=[field_shape, field_shape, line_shape, jax.ShapeDtypeStruct((channels + 8, channels), f32)],
        scratch_shapes=[
            mode_scratch,
            pltpu.VMEM((1, channels, ny, nz), f32),
            kron_scratch,
            kron_scratch,
            pltpu.VMEM((8 * channels, 128), f32),
            pltpu.VMEM((8 * channels, 8 * channels), f32),
            pltpu.VMEM((8 * channels, 2 * nz), f32),
        ],
        compiler_params=params(56),
        name="middle",
    )(mixed, flow_field, cotangent, point_weight, bias, tzi_out, ty, fy, tz_grad)
    grad_x = exchange(grad_lines)
    gathered = lax.all_gather(local_sums, "space", axis=0, tiled=False)

    grad_mixed, grad_spec = pl.pallas_call(
        functools.partial(adjoint_kernel, nx, lines),
        grid=(quads,),
        in_specs=[
            line_spec,
            line_spec,
            weight_spec,
            whole(fx_wide),
            whole(gx),
            whole(inv_wide),
        ],
        out_specs=[line_spec, weight_spec],
        out_shape=[line_shape, jax.ShapeDtypeStruct(spec_weight.shape, f32)],
        scratch_shapes=[pltpu.VMEM((4 * channels, 2 * wide), bf16), pltpu.VMEM((4 * channels, 2 * wide), bf16)],
        compiler_params=params(48),
        name="mode_adjoint",
    )(spec_x, grad_x, spec_weight, fx_wide, gx, inv_wide)
    back = exchange(grad_mixed)

    grad_field = pl.pallas_call(
        functools.partial(last_kernel, slab, ky_own),
        grid=(slab,),
        in_specs=[line_spec, plane_spec, whole(point_weight), whole(tzi_grad), whole(ty)],
        out_specs=plane_spec,
        out_shape=field_shape,
        scratch_shapes=[mode_scratch, kron_scratch, kron_scratch],
        compiler_params=params(40),
        name="field_inverse",
    )(back, gpre, point_weight, tzi_grad, ty)

    summed = jnp.sum(gathered, axis=0) * fwd_scale
    return output, grad_field, grad_spec, summed[:channels], summed[channels]


def solution(mesh):
    cells = P(("group", "space"), None, None, None)
    return jax.shard_map(
        per_device,
        mesh=mesh,
        in_specs=(cells, cells, P("space", None, None, None), P(), P()),
        out_specs=(cells, cells, cells, P("group", None), P("group")),
        check_vma=False,
    )
```

time: 547 us -> 138 us (0.25); the launches traced: 537 us -> 137 us
  matrix products: 293 us -> 0 us
  local copies, waits for them, and re-layouts: 132 us -> 10.8 us
  Pallas kernels: 0 us -> 55.5 us
  other arithmetic: 23.7 us -> 0.04 us
  starting transfers between devices: 23.5 us -> 3.53 us
    dot_general x51 -> x0, matrix products: 293 us -> none  [contract(): return jnp.einsum(form, left, right, precision=highest)]
    psum x1 -> x0, blocking collectives: 62.4 us -> none  [per_device(): summed_weight, summed_bias = lax.psum((local_weight, local_bias), 'space')]
    squeeze x7 -> x0, local copies, waits for them, and re-layouts: 59.7 us -> none  [the longest x3 59 us: split_weight(): return (shaped[:, 0], shaped[:, 1])]
    pallas_call x0 -> x5, Pallas kernels: none -> 55.5 us  [the longest x1 24.8 us: per_device(): pl.pallas_call(functools.partial(middle_kernel, slab, ky_own), grid=(slab...]
    all_to_all x0 -> x3, blocking collectives: none -> 44.1 us  [exchange(): lax.all_to_all(blocks, 'space', split_axis=0, concat_axis=0, tiled=True)]
    another operation x12 -> x0, local copies, waits for them, and re-layouts: 32.2 us -> none  [the longest x2 27.5 us: mode_grad(): jnp.stack([dw_real, dw_imag], axis=1)]
    reshape x11 -> x0, local copies, waits for them, and re-layouts: 29.8 us -> none  [the longest x1 21.8 us: split_weight(): shaped = weights.reshape(pair_total, 2, channels, kx_total, channels)]
    all_gather x0 -> x1, blocking collectives: none -> 22.5 us  [per_device(): gathered = lax.all_gather(local_sums, 'space', axis=0, tiled=False)]
  transfers between devices with their start and end apart: 4 -> 1, of which waited for: 0 -> 0; matrix products, arithmetic and copies ran while one was open for 28% -> 1% of each run, Pallas kernels for 0% -> 0%
where the time goes in v1:
time: 138 us; the launch traced here: 137 us
  blocking collectives  66.6 us (48%)
  Pallas kernels  55.5 us (40%)
  local copies, waits for them, and re-layouts  10.8 us (8%)
  starting transfers between devices  3.53 us (3%)
    all_to_all x3, blocking collectives, exchange(): lax.all_to_all(blocks, 'space', split_axis=0, concat_axis=0, tiled=True)  44.1 us
    pallas_call x1, Pallas kernels, per_device(): pl.pallas_call(functools.partial(middle_kernel, slab, ky_own), grid=(slab...  24.8 us
    all_gather x1, blocking collectives, per_device(): gathered = lax.all_gather(local_sums, 'space', axis=0, tiled=False)  22.5 us
    pallas_call x1, Pallas kernels, per_device(): pl.pallas_call(functools.partial(adjoint_kernel, nx, lines), grid=(quads,...  13.2 us
    unnamed x28, local copies, waits for them, and re-layouts  10.1 us
    pallas_call x1, Pallas kernels, per_device(): pl.pallas_call(functools.partial(last_kernel, slab, ky_own), grid=(slab,)...  9.14 us
    pallas_call x1, Pallas kernels, per_device(): pl.pallas_call(functools.partial(mix_kernel, nx, lines), grid=(quads,), i...  5.26 us
    all_to_all x1, starting transfers between devices, exchange(): lax.all_to_all(blocks, 'space', split_axis=0, concat_axis=0, tiled=True)  3.53 us
  transfers between devices with their start and end apart: 1, of which 0 were waited for; matrix products, arithmetic and copies ran while one was open for 1% of the time, Pallas kernels for 0%

profile of v1, /device:TPU:0, one launch (start us, length us, event | category | flops | bytes accessed | tf_op | source)
XLA Modules:
  0.0 137.2 jit_solution(14101877783463221045)
XLA Ops:
  0.6 0.0 copy-start.1
  0.6 2.2 %copy-done.1 = f32[2,32,128,128]{3,2,1,0:T(8,128)S(1)} copy-done((f32[2,32,128,128]{3,2,1,0:T(8,128)S(1)}, f32[2,32,128,128]{3,2,1,0:T(8,128)}, u32[]{:S(2)}) %copy-start.1) | copy-done | bytes 4194328
  2.8 0.0 copy-start.6
  2.8 0.8 copy-done.6
  3.7 0.0 copy-start.11
  3.7 0.8 copy-done.11
  4.4 0.0 copy-start.3
  4.4 0.0 copy-start.10
  4.4 3.1 %field_forward.1 = f32[512,128]{1,0:T(8,128)S(1)} custom-call(f32[2,32,128,128]{3,2,1,0:T(8,128)S(1)} %copy-done.1, bf16[128,256]{1,0:T(8,128)(2,1)S(1)} %copy-done.6, bf16[64,256]{1,0:T(8,128)(2,1)S(1)} %copy-done.11), custom_call_target="tpu_custom_call" | custom-call | tf_op jit(solution)/shard_map/field_forward/pallas_call | solution.py:422
  7.5 17.2 %all_to_all.20 = f32[16,32,128]{2,1,0:T(8,128)S(1)} all-to-all(f32[16,32,128]{2,1,0:T(8,128)S(1)} %bitcast.15), channel_id=1, replica_groups=mesh['group'=2,'space'=16] {'space'}, dimensions={0} | all-to-all | bytes 524288 | tf_op jit(solution)/shard_map/all_to_all | solution.py:420
  24.7 0.0 copy-done.3
  24.7 0.0 copy-done.10
  24.7 0.0 copy-start
  24.7 3.4 %copy-done = f32[32,2,32,1024]{3,2,1,0:T(8,128)S(1)} copy-done((f32[32,2,32,1024]{3,2,1,0:T(8,128)S(1)}, f32[32,2,32,1024]{3,2,1,0:T(8,128)}, u32[]{:S(2)}) %copy-start) | copy-done | bytes 8388632
  28.1 5.3 %mode_mix.1 = f32[512,128]{1,0:T(8,128)S(1)} custom-call(f32[512,128]{1,0:T(8,128)S(1)} %bitcast.11, f32[32,2,32,1024]{3,2,1,0:T(8,128)S(1)} %copy-done, bf16[192,2048]{1,0:T(8,128)(2,1)S(1)} %copy-done.3, bf16[64,192]{1,0:T(8,128)(2,1)S(1)} %copy-done.10), custom_call_target="tpu_custom_call" | custom-call | tf_op jit(solution)/shard_map/mode_mix/pallas_call | solution.py:434
  33.4 13.3 %all_to_all.21 = f32[16,32,128]{2,1,0:T(8,128)} all-to-all(f32[16,32,128]{2,1,0:T(8,128)S(1)} %bitcast.16), channel_id=1, replica_groups=mesh['group'=2,'space'=16] {'space'}, dimensions={0} | all-to-all | bytes 524288 | tf_op jit(solution)/shard_map/all_to_all | solution.py:420
  46.7 0.0 copy-start.4
  46.7 0.0 copy-start.9
  46.7 24.8 %middle.1 = (f32[2,32,128,128]{3,2,1,0:T(8,128)}, f32[2,32,128,128]{3,2,1,0:T(8,128)}, f32[512,128]{1,0:T(8,128)}, f32[40,32]{1,0:T(8,128)}) custom-call(f32[512,128]{1,0:T(8,128)} %bitcast.17, f32[2,32,128,128]{3,2,1,0:T(8,128)} %field_ref.3, f32[2,32,128,128]{3,2,1,0:T(8,128)} %cot_ref.1, f32[32,32]{1,0:T(8,128)} %weight_ref.7, f32[1,32]{1,0:T(1,128)} %bitcast.21, ...), custom_call_target="tpu_custom_call" | custom-call | tf_op jit(solution)/shard_map/middle/pallas_call | solution.py:447
  71.5 13.5 %all_to_all.22 = f32[16,32,128]{2,1,0:T(8,128)S(1)} all-to-all(f32[16,32,128]{2,1,0:T(8,128)} %bitcast.18), channel_id=1, replica_groups=mesh['group'=2,'space'=16] {'space'}, dimensions={0} | all-to-all | bytes 524288 | tf_op jit(solution)/shard_map/all_to_all | solution.py:420
  85.1 0.0 copy-done.4
  85.1 0.0 copy-done.9
  85.1 0.0 copy-start.12
  85.1 0.0 copy-start.5
  85.1 0.0 copy-start.7
  85.1 0.0 copy-start.8
  85.1 13.2 %mode_adjoint.1 = (f32[512,128]{1,0:T(8,128)}, f32[32,2,32,1024]{3,2,1,0:T(8,128)}) custom-call(f32[512,128]{1,0:T(8,128)S(1)} %bitcast.12, f32[512,128]{1,0:T(8,128)S(1)} %bitcast.14, f32[32,2,32,1024]{3,2,1,0:T(8,128)} %weight_ref.6, bf16[192,2048]{1,0:T(8,128)(2,1)S(1)} %copy-done.3, bf16[64,192]{1,0:T(8,128)(2,1)S(1)} %copy-done.9, ...), custom_call_target="tpu_custom_call" | custom-call | tf_op jit(solution)/shard_map/mode_adjoint/pallas_call | solution.py:483
  98.3 3.5 %all-to-all-start.3 = ((f32[16,32,128]{2,1,0:T(8,128)}), f32[16,32,128]{2,1,0:T(8,128)S(1)}, u32[]{:S(2)}, u32[]{:S(2)}) async-start(f32[16,32,128]{2,1,0:T(8,128)} %bitcast.7), calls=%async_computation.3 | async-start | bytes 524288 | tf_op jit(solution)/shard_map/all_to_all | solution.py:420
  101.9 0.0 copy-done.12
  101.9 0.1 copy.23
  101.9 22.5 %all-gather.1 = f32[16,40,32]{1,2,0:T(8,128)S(1)} all-gather(f32[1,40,32]{1,2,0:T(8,128)S(1)} %copy.23), channel_id=2, replica_groups=mesh['group'=2,'space'=16] {'space'}, dimensions={0}, use_global_device_ids=true | all-gather | bytes 87040 | tf_op jit(solution)/shard_map/all_gather | solution.py:481
  124.5 0.7 copy.24
  125.2 0.7 slice_reduce_fusion
  125.9 0.0 all-to-all-done.3
  125.9 0.0 copy-done.5
  125.9 0.0 copy-done.7
  125.9 0.0 copy-done.8
  125.9 0.0 copy-start.2
  125.9 2.2 %copy-done.2 = f32[2,32,128,128]{3,2,1,0:T(8,128)S(1)} copy-done((f32[2,32,128,128]{3,2,1,0:T(8,128)S(1)}, f32[2,32,128,128]{3,2,1,0:T(8,128)}, u32[]{:S(2)}) %copy-start.2) | copy-done | bytes 4194328
  128.1 9.1 %field_inverse.1 = f32[2,32,128,128]{3,2,1,0:T(8,128)} custom-call(f32[512,128]{1,0:T(8,128)S(1)} %bitcast.13, f32[2,32,128,128]{3,2,1,0:T(8,128)S(1)} %copy-done.2, f32[32,32]{1,0:T(8,128)S(1)} %copy-done.7, bf16[96,256]{1,0:T(8,128)(2,1)S(1)} %copy-done.8, bf16[128,192]{1,0:T(8,128)(2,1)S(1)} %copy-done.5), custom_call_target="tpu_custom_call" | custom-call | tf_op jit(solution)/shard_map/field_inverse/pallas_call | solution.py:502
  (2 shorter events, 0.0 us)
Async XLA Ops:
  0.6 2.2 %copy-start.1 = (f32[2,32,128,128]{3,2,1,0:T(8,128)S(1)}, f32[2,32,128,128]{3,2,1,0:T(8,128)}, u32[]{:S(2)}) copy-start(f32[2,32,128,128]{3,2,1,0:T(8,128)} %field_ref.3) | copy-start | bytes 12582916
  2.8 0.8 copy-start.6
  3.7 0.8 copy-start.11
  4.4 20.3 %copy-start.3 = (bf16[192,2048]{1,0:T(8,128)(2,1)S(1)}, bf16[192,2048]{1,0:T(8,128)(2,1)}, u32[]{:S(2)}) copy-start(bf16[192,2048]{1,0:T(8,128)(2,1)} %constant.30.clone.fx_ref) | copy-start | bytes 2359300
  4.4 20.3 %copy-start.10 = (bf16[64,192]{1,0:T(8,128)(2,1)S(1)}, bf16[64,192]{1,0:T(8,128)(2,1)}, u32[]{:S(2)}) copy-start(bf16[64,192]{1,0:T(8,128)(2,1)} %constant.32.clone.inv_ref) | copy-start | bytes 73732
  24.7 3.4 %copy-start = (f32[32,2,32,1024]{3,2,1,0:T(8,128)S(1)}, f32[32,2,32,1024]{3,2,1,0:T(8,128)}, u32[]{:S(2)}) copy-start(f32[32,2,32,1024]{3,2,1,0:T(8,128)} %weight_ref.6) | copy-start | bytes 25165828
  46.7 38.4 %copy-start.4 = (bf16[128,2048]{1,0:T(8,128)(2,1)S(1)}, bf16[128,2048]{1,0:T(8,128)(2,1)}, u32[]{:S(2)}) copy-start(bf16[128,2048]{1,0:T(8,128)(2,1)} %constant.33.clone.inv_ref) | copy-start | bytes 1572868
  46.7 38.4 %copy-start.9 = (bf16[64,192]{1,0:T(8,128)(2,1)S(1)}, bf16[64,192]{1,0:T(8,128)(2,1)}, u32[]{:S(2)}) copy-start(bf16[64,192]{1,0:T(8,128)(2,1)} %constant.31.clone.gx_ref) | copy-start | bytes 73732
  85.1 16.8 %copy-start.12 = (f32[40,32]{1,0:T(8,128)S(1)}, f32[40,32]{1,0:T(8,128)}, u32[]{:S(2)}) copy-start(f32[40,32]{1,0:T(8,128)} %get-tuple-element.16) | copy-start | bytes 15364
  85.1 40.8 %copy-start.5 = (bf16[128,192]{1,0:T(8,128)(2,1)S(1)}, bf16[128,192]{1,0:T(8,128)(2,1)}, u32[]{:S(2)}) copy-start(bf16[128,192]{1,0:T(8,128)(2,1)} %constant.25.clone.ty_ref) | copy-start | bytes 147460
  85.1 40.8 %copy-start.7 = (f32[32,32]{1,0:T(8,128)S(1)}, f32[32,32]{1,0:T(8,128)}, u32[]{:S(2)}) copy-start(f32[32,32]{1,0:T(8,128)} %weight_ref.7) | copy-start | bytes 12292
  85.1 40.8 %copy-start.8 = (bf16[96,256]{1,0:T(8,128)(2,1)S(1)}, bf16[96,256]{1,0:T(8,128)(2,1)}, u32[]{:S(2)}) copy-start(bf16[96,256]{1,0:T(8,128)(2,1)} %constant.29.clone.tzi_ref) | copy-start | bytes 147460
  98.3 27.5 %all-to-all-start.3 = ((f32[16,32,128]{2,1,0:T(8,128)}), f32[16,32,128]{2,1,0:T(8,128)S(1)}, u32[]{:S(2)}, u32[]{:S(2)}) async-start(f32[16,32,128]{2,1,0:T(8,128)} %bitcast.7), calls=%async_computation.3 | async-start | bytes 524288 | tf_op jit(solution)/shard_map/all_to_all | solution.py:420
  125.9 2.2 %copy-start.2 = (f32[2,32,128,128]{3,2,1,0:T(8,128)S(1)}, f32[2,32,128,128]{3,2,1,0:T(8,128)}, u32[]{:S(2)}) copy-start(f32[2,32,128,128]{3,2,1,0:T(8,128)} %get-tuple-element.14.gpre_ref) | copy-start | bytes 12582916

commit v2 on v1

v2 whole, which is shorter than its diff:
```python
import functools
import math

import jax
import jax.numpy as jnp
import ml_dtypes
import numpy as np
from jax import lax
from jax.experimental import pallas as pl
from jax.experimental.pallas import tpu as pltpu
from jax.sharding import PartitionSpec as P

MODES = 16
KY = 2 * MODES
KX = 2 * MODES
MIB = 1024 * 1024
NT = (((1,), (1,)), ((), ()))
TN = (((0,), (0,)), ((), ()))
f32 = jnp.float32
bf16 = jnp.bfloat16


def signed(n):
    j = np.arange(n)
    return np.where(j < n // 2, j, j - n)


def phases(positions, waves, length):
    angle = ((positions[:, None] * waves[None, :]) % length) * (2.0 * math.pi / length)
    return np.cos(angle), np.sin(angle)


def halves(table):
    table = np.asarray(table, np.float32)
    high = table.astype(ml_dtypes.bfloat16)
    low = (table - high.astype(np.float32)).astype(ml_dtypes.bfloat16)
    return high, low


def stack3(table, axis):
    high, low = halves(table)
    return np.concatenate([high, high, low], axis=axis)


def y_table(ny):
    cos, sin = phases(np.arange(ny), signed(KY), ny)
    return np.concatenate([cos.T, -sin.T], axis=0)


def z_table(nz, scale, factor):
    cos, sin = phases(np.arange(nz), np.arange(MODES), nz)
    weight = scale * np.where(np.arange(MODES) == 0, 1.0, factor)
    cos, sin = cos.T * weight[:, None], sin.T * weight[:, None]
    real = np.concatenate([cos, sin], axis=1)
    imag = np.concatenate([-sin, cos], axis=1)
    both = np.stack([real, imag], axis=1).reshape(4, 4, 2, 2 * nz)
    return both.transpose(1, 0, 2, 3).reshape(2 * MODES, 2 * nz)


def x_forward_table(nx, scale):
    cos, sin = phases(np.arange(nx), signed(KX), nx)
    top = np.concatenate([cos, -sin], axis=1)
    bottom = np.concatenate([sin, cos], axis=1)
    return scale * np.concatenate([top, bottom], axis=0)


def x_inverse_table(nx):
    cos, sin = phases(np.arange(nx), signed(KX), nx)
    top = np.concatenate([cos, -sin], axis=1)
    bottom = np.concatenate([sin, cos], axis=1)
    return np.concatenate([top, bottom], axis=0)


def by_low(table, axis):
    order = np.arange(2 * KX).reshape(2, KX // 4, 4).transpose(0, 2, 1).reshape(-1)
    return np.take(table, order, axis=axis)


def split(values):
    high = values.astype(bf16)
    low = (values - high.astype(f32)).astype(bf16)
    return high, low


def data3(values):
    high, low = split(values)
    return jnp.concatenate([high, low, high], axis=0)


def dot(left, right, dims=(((1,), (0,)), ((), ()))):
    return lax.dot_general(left, right, dims, preferred_element_type=f32)


def group_transpose(tiles):
    group = lax.broadcasted_iota(jnp.int32, tiles[0].shape, 1) // 32
    result = []
    for m in range(4):
        moved = [pltpu.roll(tiles[n], ((n - m) * 32) % 128, 1) if n != m else tiles[n] for n in range(4)]
        low = jnp.where(group == 0, moved[0], moved[1])
        high = jnp.where(group == 2, moved[2], moved[3])
        result.append(jnp.where(group < 2, low, high))
    return result


def block_row(ky, plane, stride, ky_own):
    return (ky // ky_own) * stride + (plane * ky_own + ky % ky_own) * 8


def forward_plane(load_channel, channels, fy_ref, tz_ref, scratch, out_ref, row_of):
    nz = scratch.shape[1]
    size = KY * channels
    for c in range(0, channels, 2):
        pair = jnp.concatenate([load_channel(c), load_channel(c + 1)], axis=1)
        high, low = split(pair)
        both = dot(fy_ref[...], jnp.concatenate([high, low], axis=0))
        half = both[: 2 * KY] + both[2 * KY :]
        for e in range(2):
            for part in range(2):
                scratch[pl.ds(part * size + c + e, KY, stride=channels), :] = half[
                    part * KY : (part + 1) * KY, e * nz : (e + 1) * nz
                ]
    high, low = split(jnp.concatenate([scratch[:size], scratch[size:]], axis=1))
    first = dot(tz_ref[...], high, NT)
    rows = first[: 2 * MODES] + first[2 * MODES :] + dot(tz_ref[: 2 * MODES, :], low, NT)
    for q in range(KY // 4):
        tiles = [rows[8 * j : 8 * j + 8, q * 128 : (q + 1) * 128] for j in range(4)]
        for e, tile in enumerate(group_transpose(tiles)):
            out_ref[pl.ds(row_of(4 * q + e), 8), :] = tile


def inverse_plane(in_ref, row_of, tz_ref, ty_ref, scratch, channels, emit):
    nz = scratch.shape[1]
    size = KY * channels
    columns = [[] for _ in range(4)]
    for q in range(KY // 4):
        tiles = [in_ref[pl.ds(row_of(4 * q + e), 8), :] for e in range(4)]
        for j, tile in enumerate(group_transpose(tiles)):
            columns[j].append(tile)
    rows = jnp.concatenate([jnp.concatenate(c, axis=1) for c in columns], axis=0)
    modes = dot(data3(rows), tz_ref[...], TN)
    for part in range(2):
        scratch[part * size : (part + 1) * size, :] = modes[:, part * nz : (part + 1) * nz]
    for c in range(0, channels, 2):
        sides = []
        for e in range(2):
            parts = [
                scratch[pl.ds(part * size + c + e, KY, stride=channels), :] for part in range(2)
            ]
            sides.append(jnp.concatenate(parts, axis=0))
        pair = dot(ty_ref[...], data3(jnp.concatenate(sides, axis=1)))
        for e in range(2):
            emit(c + e, pair[:, e * nz : (e + 1) * nz])


def spread_weight(weight, high_ref, low_ref):
    size = weight.shape[0]
    row = lax.broadcasted_iota(jnp.int32, (8 * size, size), 0) // 8
    column = lax.broadcasted_iota(jnp.int32, (8 * size, size), 1)
    expand = (row == column).astype(f32)
    tall = lax.dot_general(
        expand, weight, (((1,), (0,)), ((), ())), precision=lax.Precision.HIGHEST, preferred_element_type=f32
    )
    wide = lax.dot_general(tall, expand, NT, precision=lax.Precision.HIGHEST, preferred_element_type=f32)
    row = lax.broadcasted_iota(jnp.int32, wide.shape, 0) % 8
    column = lax.broadcasted_iota(jnp.int32, wide.shape, 1) % 8
    high, low = split(jnp.where(row == column, wide, 0.0))
    high_ref[...] = high
    low_ref[...] = low


def cell_tile(ref, plane, start):
    sides = []
    for e in range(2):
        piece = ref[plane, :, pl.ds(start + 8 * e, 8), :]
        sides.append(piece.reshape(piece.shape[0] * 8, piece.shape[2]))
    return jnp.concatenate(sides, axis=1)


def put_tile(ref, plane, start, tile):
    channels, nz = ref.shape[1], ref.shape[3]
    for e in range(2):
        ref[plane, :, pl.ds(start + 8 * e, 8), :] = tile[:, e * nz : (e + 1) * nz].reshape(channels, 8, nz)


def mix_cells(high_ref, low_ref, high, low):
    return dot(high_ref[...], high) + dot(low_ref[...], high) + dot(high_ref[...], low)


def rows_at(plane, stride, ky_own):
    def row_of(ky):
        row = block_row(ky, plane, stride, ky_own)
        return row if isinstance(row, int) else pl.multiple_of(row, 8)

    return row_of


def transfers(pairs, sems):
    return [pltpu.make_async_copy(src, dst, sems.at[i]) for i, (src, dst) in enumerate(pairs)]


def chunks(channels):
    return [slice(8 * g, 8 * g + 8) for g in range(channels // 8)]


def first_kernel(stride, ky_own, field_hbm, fy_hbm, tz_hbm, out_ref, field_ref, fy_ref, tz_ref, scratch, sems, table_sems):
    slab, channels = field_ref.shape[:2]
    tables = transfers([(fy_hbm, fy_ref), (tz_hbm, tz_ref)], table_sems)
    parts = [(field_hbm.at[p, c], field_ref.at[p, c]) for p in range(slab) for c in chunks(channels)]
    for copy in tables + transfers(parts, sems):
        copy.start()
    for copy in tables:
        copy.wait()

    def body(p, carry):
        def load_channel(c):
            if c % 8 == 0:
                part = slice(c, c + 8)
                sem = sems.at[p * (channels // 8) + c // 8]
                pltpu.make_async_copy(field_hbm.at[p, part], field_ref.at[p, part], sem).wait()
            return field_ref[p, c]

        forward_plane(load_channel, channels, fy_ref, tz_ref, scratch, out_ref, rows_at(p, stride, ky_own))
        return carry

    lax.fori_loop(0, slab, body, 0)


def point_kernel(field_ref, weight_ref, bias_ref, out_ref, kron_high, kron_low, bias_wide):
    channels = field_ref.shape[1]

    @pl.when(pl.program_id(0) == 0)
    def _():
        spread_weight(jnp.transpose(weight_ref[...]), kron_high, kron_low)
        row = lax.broadcasted_iota(jnp.int32, (8 * channels, channels), 0) // 8
        column = lax.broadcasted_iota(jnp.int32, (8 * channels, channels), 1)
        picked = jnp.where(row == column, bias_ref[...], 0.0)
        bias_wide[...] = jnp.broadcast_to(jnp.sum(picked, axis=1, keepdims=True), bias_wide.shape)

    for start in range(0, field_ref.shape[2], 16):
        high, low = split(cell_tile(field_ref, 0, start))
        put_tile(out_ref, 0, start, mix_cells(kron_high, kron_low, high, low) + bias_wide[...])


def quad_rows(ref, nx, lines, u):
    return jnp.concatenate([ref[pl.ds(2 * u + part, nx, stride=lines), :] for part in range(2)], axis=0)


def data_rows(ref, nx, lines, u):
    high, low = split(jnp.transpose(quad_rows(ref, nx, lines, u)))
    return jnp.concatenate([high, low, high], axis=1)


def weight_loads(weight_hbm, weight_ref, table_pairs, sems):
    parts = [slice(256 * t, 256 * t + 256) for t in range(4)]
    pairs = table_pairs + [(weight_hbm.at[:, :, :, part], weight_ref.at[:, :, :, part]) for part in parts]
    copies = transfers(pairs, sems)
    for copy in copies:
        copy.start()
    return copies[: len(table_pairs)], copies[len(table_pairs) :]


def mix_kernel(
    nx, lines, in_ref, weight_hbm, fx_hbm, inv_hbm, out_ref, weight_ref, fx_ref, inv_ref, left, modes, sums, sems
):
    pairs = weight_ref.shape[0]
    wide = KX * 32
    tables, loads = weight_loads(weight_hbm, weight_ref, [(fx_hbm, fx_ref), (inv_hbm, inv_ref)], sems)
    for u in range(pairs // 4):
        left[128 * u : 128 * u + 128, :] = data_rows(in_ref, nx, lines, u)
    for copy in tables:
        copy.wait()
    for t in range(4):
        cols = slice(256 * t, 256 * t + 256)
        late = slice(wide + 256 * t, wide + 256 * t + 256)
        modes[:, :256] = dot(left[...], fx_ref[:, cols])
        modes[:, 256:] = dot(left[...], fx_ref[:, late])
        loads[t].wait()

        def body(pair, carry):
            rows = pl.ds(pl.multiple_of(32 * pair, 32), 32)
            real, imag = modes[rows, :256], modes[rows, 256:]
            w_real, w_imag = weight_ref[pair, 0, :, cols], weight_ref[pair, 1, :, cols]
            products = (real * w_real - imag * w_imag, imag * w_real + real * w_imag)
            for part in range(2):
                total = jnp.sum(products[part].reshape(4, 8, 256), axis=0)
                for e in range(2):
                    base = pl.multiple_of((2 * pair + part) * 64 + 8 * (2 * t + e), 8)
                    sums[pl.ds(base, 8), :] = total[:, 128 * e : 128 * e + 128]
            return carry

        lax.fori_loop(0, pairs, body, 0, unroll=4)
    for u in range(pairs // 4):
        tiles = [[], []]
        for j in range(4):
            for part in range(2):
                base = (2 * (4 * u + j) + part) * 64
                found = [sums[pl.ds(base + s, 8, stride=8), :] for s in range(8)]
                while len(found) > 1:
                    found = [found[k] + found[k + 1] for k in range(0, len(found), 2)]
                tiles[part].append(found[0])
        mixed = jnp.concatenate(group_transpose(tiles[0]) + group_transpose(tiles[1]), axis=0)
        planes = dot(inv_ref[...], data3(mixed))
        for part in range(2):
            out_ref[pl.ds(2 * u + part, nx, stride=lines), :] = planes[part * nx : (part + 1) * nx]


def gradient_tiles(grad_ref, gx_ref, nx, lines, u):
    grads = dot(gx_ref[...], data3(quad_rows(grad_ref, nx, lines, u)))
    tiles = []
    for part in range(2):
        tiles.append(group_transpose([grads[part * 32 + 8 * b : part * 32 + 8 * b + 8, :] for b in range(4)]))
    return tiles, grads


def weight_grad_kernel(nx, lines, in_ref, grad_ref, fx_ref, gx_ref, dweight_ref):
    u = pl.program_id(0)
    wide = KX * 32
    modes = dot(data3(quad_rows(in_ref, nx, lines, u)), fx_ref[...], TN)
    tiles, _ = gradient_tiles(grad_ref, gx_ref, nx, lines, u)
    for j in range(4):
        rows = slice(32 * j, 32 * j + 32)
        for a in range(8):
            cols = slice(128 * a, 128 * a + 128)
            late = slice(wide + 128 * a, wide + 128 * a + 128)
            g_real = jnp.broadcast_to(tiles[0][j][a : a + 1, :], (32, 128))
            g_imag = jnp.broadcast_to(tiles[1][j][a : a + 1, :], (32, 128))
            s_real, s_imag = modes[rows, cols], modes[rows, late]
            dweight_ref[j, 0, :, cols] = s_real * g_real + s_imag * g_imag
            dweight_ref[j, 1, :, cols] = s_real * g_imag - s_imag * g_real


def adjoint_kernel(
    slab,
    nx,
    lines,
    extra,
    grad_ref,
    weight_hbm,
    gx_hbm,
    inv_hbm,
    sums_ref,
    out_ref,
    weight_ref,
    gx_ref,
    inv_ref,
    rows_ref,
    left,
    total,
    sems,
):
    pairs = weight_ref.shape[0]
    devices = nx // slab
    stride = slab * lines + extra
    bias = None
    tables, loads = weight_loads(weight_hbm, weight_ref, [(gx_hbm, gx_ref), (inv_hbm, inv_ref)], sems)
    for copy in tables:
        copy.wait()
    for u in range(pairs // 4):
        tiles, grads = gradient_tiles(grad_ref, gx_ref, nx, lines, u)
        bias = grads[0:1, :] if u == 0 else bias
        for part in range(2):
            for j in range(4):
                base = (2 * (4 * u + j) + part) * 8
                rows_ref[base : base + 8, :] = tiles[part][j]
    early = lax.broadcasted_iota(jnp.int32, (32, 128), 1) % 32 < 16
    for t in range(4):
        loads[t].wait()

        def body(pair, carry):
            rows = pl.ds(pl.multiple_of(32 * pair, 32), 32)
            for e in range(2):
                cols = slice(256 * t + 128 * e, 256 * t + 128 * e + 128)
                g_real, g_imag = [
                    jnp.broadcast_to(rows_ref[pl.ds((2 * pair + part) * 8 + 2 * t + e, 1), :], (32, 128))
                    for part in range(2)
                ]
                w_real, w_imag = weight_ref[pair, 0, :, cols], weight_ref[pair, 1, :, cols]
                real = g_real * w_real + g_imag * w_imag
                imag = g_imag * w_real - g_real * w_imag
                folded = jnp.where(early, real + pltpu.roll(real, 112, 1), imag + pltpu.roll(imag, 16, 1))
                high, low = split(folded)
                left[rows, 128 * e : 128 * e + 128] = high
                left[rows, 256 + 128 * e : 384 + 128 * e] = low
            return carry

        lax.fori_loop(0, pairs, body, 0, unroll=4)
        table = inv_ref[256 * t : 256 * t + 256, :]
        product = dot(left[:, :256], table) + dot(left[:, 256:], table)
        if t == 0:
            total[...] = product
        else:
            total[...] += product
    lane = lax.broadcasted_iota(jnp.int32, (nx, 128), 1)
    carried = lax.axis_index("space") == 0
    for u in range(pairs // 4):
        both = total[128 * u : 128 * u + 128, :]
        planes = jnp.transpose(both[:, : 2 * nx] + both[:, 2 * nx :])
        real, imag = planes[:nx], planes[nx:]
        if u == 0:
            imag = jnp.where((lane < 32) & carried, jnp.broadcast_to(bias, (nx, 128)), imag)
        for part, values in ((0, real), (1, imag)):
            for p in range(slab):
                out_ref[pl.ds(p * lines + 2 * u + part, devices, stride=stride), :] = values[
                    p * devices : (p + 1) * devices
                ]
    for d in range(devices):
        out_ref[d * stride + slab * lines : d * stride + slab * lines + extra, :] = sums_ref[...]


def middle_kernel(
    stride,
    ky_own,
    in_ref,
    point_ref,
    cot_ref,
    tzi_ref,
    ty_ref,
    fy_ref,
    tzf_ref,
    output_hbm,
    gpre_hbm,
    spec_ref,
    output_ref,
    gpre_ref,
    scratch,
    sems,
):
    slab, channels = point_ref.shape[:2]
    rate = math.sqrt(2.0 / math.pi)

    def stores(p, g):
        part = slice(8 * g, 8 * g + 8)
        pairs = ((output_ref, output_hbm), (gpre_ref, gpre_hbm))
        return [
            pltpu.make_async_copy(src.at[p, part], dst.at[p, part], sems.at[k, p, g])
            for k, (src, dst) in enumerate(pairs)
        ]

    def body(p, carry):
        row_of = rows_at(p, stride, ky_own)

        def emit(channel, spectral):
            values = spectral + point_ref[p, channel]
            square = values * values
            bent = jnp.tanh(rate * values * (1.0 + 0.044715 * square))
            half = 0.5 + 0.5 * bent
            output_ref[p, channel] = values * half
            slope = half + (0.5 * rate) * values * (1.0 - bent * bent) * (1.0 + (3 * 0.044715) * square)
            gpre_ref[p, channel] = cot_ref[p, channel] * slope
            if channel % 8 == 7:
                for copy in stores(p, channel // 8):
                    copy.start()

        inverse_plane(in_ref, row_of, tzi_ref, ty_ref, scratch, channels, emit)
        forward_plane(lambda c: gpre_ref[p, c], channels, fy_ref, tzf_ref, scratch, spec_ref, row_of)
        return carry

    lax.fori_loop(0, slab, body, 0)
    for p in range(slab):
        for g in range(channels // 8):
            for copy in stores(p, g):
                copy.wait()


def back_kernel(field_ref, gpre_ref, weight_ref, out_ref, sums_ref, kron_high, kron_low, outer):
    channels = field_ref.shape[1]

    @pl.when(pl.program_id(0) == 0)
    def _():
        spread_weight(weight_ref[...], kron_high, kron_low)
        outer[...] = jnp.zeros_like(outer)

    for start in range(0, field_ref.shape[2], 16):
        high, low = split(cell_tile(field_ref, 0, start))
        g_high, g_low = split(cell_tile(gpre_ref, 0, start))
        put_tile(out_ref, 0, start, mix_cells(kron_high, kron_low, g_high, g_low))
        outer[...] += dot(high, g_high, NT) + dot(low, g_high, NT) + dot(high, g_low, NT)

    @pl.when(pl.program_id(0) == pl.num_programs(0) - 1)
    def _():
        row = lax.broadcasted_iota(jnp.int32, outer.shape, 0) % 8
        column = lax.broadcasted_iota(jnp.int32, outer.shape, 1) % 8
        kept = jnp.where(row == column, outer[...], 0.0)
        kept = jnp.sum(kept.reshape(channels, 8, 8 * channels), axis=1)
        row = lax.broadcasted_iota(jnp.int32, (8 * channels, channels), 0) // 8
        column = lax.broadcasted_iota(jnp.int32, (8 * channels, channels), 1)
        pick = (row == column).astype(f32)
        small = lax.dot_general(
            kept, pick, (((1,), (0,)), ((), ())), precision=lax.Precision.HIGHEST, preferred_element_type=f32
        )
        sums_ref[...] = jnp.concatenate([small[8 * g : 8 * g + 8] for g in range(4)], axis=1)


def last_kernel(
    stride,
    ky_own,
    devices,
    sums_at,
    scales,
    in_ref,
    part_ref,
    back_hbm,
    tzi_hbm,
    ty_hbm,
    out_hbm,
    point_ref,
    bias_ref,
    scratch,
    cells_ref,
    tzi_ref,
    ty_ref,
    in_sems,
    out_sems,
    table_sems,
):
    slab, channels = cells_ref.shape[:2]
    groups = channels // 8
    places = [(p, c) for p in range(slab) for c in chunks(channels)]
    tables = transfers([(tzi_hbm, tzi_ref), (ty_hbm, ty_ref)], table_sems)
    loads = transfers([(back_hbm.at[at], cells_ref.at[at]) for at in places], in_sems)
    stores = transfers([(cells_ref.at[at], out_hbm.at[at]) for at in places], out_sems)

    def one(p, g, store):
        at = (p, slice(8 * g, 8 * g + 8))
        if store:
            return pltpu.make_async_copy(cells_ref.at[at], out_hbm.at[at], out_sems.at[p * groups + g])
        return pltpu.make_async_copy(back_hbm.at[at], cells_ref.at[at], in_sems.at[p * groups + g])

    for copy in tables + loads:
        copy.start()
    step, first = sums_at
    total = part_ref[first : first + 8, :]
    for d in range(1, devices):
        total = total + part_ref[d * step + first : d * step + first + 8, :]
    for g in range(4):
        point_ref[8 * g : 8 * g + 8, :] = total[:, 32 * g : 32 * g + 32] * scales[0]
    bias_ref[...] = in_ref[1:2, 0:32] * scales[1]
    for copy in tables:
        copy.wait()

    def body(p, carry):
        def emit(channel, values):
            if channel % 8 == 0:
                one(p, channel // 8, False).wait()
            cells_ref[p, channel] = cells_ref[p, channel] + values
            if channel % 8 == 7:
                one(p, channel // 8, True).start()

        inverse_plane(in_ref, rows_at(p, stride, ky_own), tzi_ref, ty_ref, scratch, channels, emit)
        return carry

    lax.fori_loop(0, slab, body, 0)
    for copy in stores:
        copy.wait()


VM = pl.BlockSpec(memory_space=pltpu.VMEM)
HBM = pl.BlockSpec(memory_space=pltpu.HBM)


def whole(array):
    zeros = (0,) * array.ndim
    return pl.BlockSpec(array.shape, lambda *_: zeros)


def params(megabytes):
    return pltpu.CompilerParams(vmem_limit_bytes=megabytes * MIB)


def cost(microseconds):
    return pl.CostEstimate(flops=0, bytes_accessed=int(microseconds * 3e6), transcendentals=0)


def keep(array):
    return pltpu.VMEM(array.shape, array.dtype)


def far(array):
    return pltpu.with_memory_space_constraint(array, pltpu.HBM)


def near(array):
    return pltpu.with_memory_space_constraint(array, pltpu.VMEM)


def per_device(flow_field, cotangent, spec_weight, point_weight, pointwise_bias):
    slab, channels, ny, nz = flow_field.shape
    devices = lax.axis_size("space")
    nx = slab * devices
    pair_local = spec_weight.shape[0]
    assert pair_local % MODES == 0 or slab == 1
    assert channels == 32 and nz == 128 and pair_local % 4 == 0
    ky_own = max(1, pair_local // MODES)
    lines = pair_local // 2
    rows = nx * lines
    block = slab * lines
    stride = slab * ky_own * 8
    extra = 8
    quads = pair_local // 4
    wide = KX * channels
    fwd_scale = float(nx * ny * nz) ** (-0.5)
    inv_scale = float(4 * MODES**3) ** (-0.5)

    fy_high, fy_low = halves(y_table(ny))
    fy = np.concatenate(
        [np.concatenate([fy_high, fy_high], axis=1), np.concatenate([fy_low, fy_low], axis=1)], axis=0
    )
    fy = jnp.asarray(fy)
    tz_first = jnp.asarray(np.concatenate(halves(z_table(nz, 1.0, 1.0)), axis=0))
    ty = jnp.asarray(stack3(y_table(ny).T, 1))
    tz_grad = jnp.asarray(np.concatenate(halves(z_table(nz, inv_scale, 2.0)), axis=0))
    tzi_out = jnp.asarray(stack3(z_table(nz, inv_scale, 2.0), 0))
    tzi_grad = jnp.asarray(stack3(z_table(nz, fwd_scale, 1.0), 0))
    fx = x_forward_table(nx, fwd_scale)
    fx_wide = jnp.asarray(np.repeat(stack3(fx, 0), channels, axis=1))
    gx = jnp.asarray(stack3(by_low(x_forward_table(nx, 1.0), 1).T, 1))
    inv = x_inverse_table(nx)
    inv_low = jnp.asarray(stack3(by_low(inv, 1), 1))
    by_plane = inv.reshape(2, devices, slab, 2 * KX).transpose(0, 2, 1, 3).reshape(2 * nx, 2 * KX)
    inv_wide = np.concatenate(halves(by_plane), axis=0).reshape(4 * nx, 2, KX).transpose(2, 1, 0)
    inv_wide = jnp.asarray(np.repeat(inv_wide.reshape(2 * KX, 4 * nx), channels // 2, axis=0))

    line_shape = jax.ShapeDtypeStruct((rows, 128), f32)
    line_spec = pl.BlockSpec((rows, 128), lambda p: (0, 0))
    field_shape = pltpu.HBM(flow_field.shape, f32)
    mode_scratch = pltpu.VMEM((2 * KY * channels, nz), f32)
    kron_scratch = pltpu.VMEM((8 * channels, 8 * channels), bf16)
    chunk_count = slab * (channels // 8)
    chunk_sems = pltpu.SemaphoreType.DMA((chunk_count,))
    pair_sems = pltpu.SemaphoreType.DMA((2,))
    cuts = ny // 32
    cells_spec = pl.BlockSpec((1, channels, 32, nz), lambda s: (s // cuts, 0, s % cuts, 0))

    def exchange(lines_out):
        blocks = lines_out.reshape(devices, -1, 128)
        return lax.all_to_all(blocks, "space", split_axis=0, concat_axis=0, tiled=True)

    first = pl.pallas_call(
        functools.partial(first_kernel, stride, ky_own),
        in_specs=[HBM, HBM, HBM],
        out_specs=VM,
        out_shape=line_shape,
        scratch_shapes=[
            pltpu.VMEM(flow_field.shape, f32),
            keep(fy),
            keep(tz_first),
            mode_scratch,
            chunk_sems,
            pair_sems,
        ],
        compiler_params=params(16),
        cost_estimate=cost(4),
        name="field_forward",
    )(far(flow_field), far(fy), far(tz_first))
    spec_x = exchange(first).reshape(rows, 128)

    bias = pointwise_bias.reshape(1, channels)
    pointwise = pl.pallas_call(
        point_kernel,
        grid=(slab * cuts,),
        in_specs=[cells_spec, whole(point_weight), whole(bias)],
        out_specs=cells_spec,
        out_shape=field_shape,
        scratch_shapes=[kron_scratch, kron_scratch, pltpu.VMEM((8 * channels, 2 * nz), f32)],
        compiler_params=params(16),
        cost_estimate=cost(6),
        name="pointwise",
    )(far(flow_field), point_weight, bias)

    spec_x, pointwise = lax.optimization_barrier((spec_x, pointwise))
    mixed = pl.pallas_call(
        functools.partial(mix_kernel, nx, lines),
        in_specs=[VM, HBM, HBM, HBM],
        out_specs=VM,
        out_shape=line_shape,
        scratch_shapes=[
            keep(spec_weight),
            keep(fx_wide),
            keep(inv_low),
            pltpu.VMEM((32 * pair_local, 6 * nx), bf16),
            pltpu.VMEM((32 * pair_local, 512), f32),
            pltpu.VMEM((128 * pair_local, 128), f32),
            pltpu.SemaphoreType.DMA((6,)),
        ],
        compiler_params=params(24),
        cost_estimate=cost(5),
        name="mode_mix",
    )(spec_x, far(spec_weight), far(fx_wide), far(inv_low))
    mixed = exchange(mixed).reshape(rows, 128)

    output, gpre, grad_lines = pl.pallas_call(
        functools.partial(middle_kernel, stride, ky_own),
        in_specs=[VM] * 7,
        out_specs=[HBM, HBM, VM],
        out_shape=[field_shape, field_shape, line_shape],
        scratch_shapes=[
            pltpu.VMEM(flow_field.shape, f32),
            pltpu.VMEM(flow_field.shape, f32),
            mode_scratch,
            pltpu.SemaphoreType.DMA((2, slab, channels // 8)),
        ],
        compiler_params=params(24),
        cost_estimate=cost(10),
        name="middle",
    )(mixed, near(pointwise), near(cotangent), near(tzi_out), near(ty), near(fy), near(tz_grad))
    grad_x = exchange(grad_lines).reshape(rows, 128)

    back, local_sums = pl.pallas_call(
        back_kernel,
        grid=(slab * cuts,),
        in_specs=[cells_spec, cells_spec, whole(point_weight)],
        out_specs=[cells_spec, pl.BlockSpec((extra, 128), lambda s: (0, 0))],
        out_shape=[field_shape, jax.ShapeDtypeStruct((extra, 128), f32)],
        scratch_shapes=[kron_scratch, kron_scratch, pltpu.VMEM((8 * channels, 8 * channels), f32)],
        compiler_params=params(16),
        cost_estimate=cost(8),
        name="pointwise_back",
    )(far(flow_field), far(gpre), point_weight)

    sent = devices * (block + extra)
    grad_mixed = pl.pallas_call(
        functools.partial(adjoint_kernel, slab, nx, lines, extra),
        in_specs=[VM, HBM, HBM, HBM, VM],
        out_specs=VM,
        out_shape=jax.ShapeDtypeStruct((sent, 128), f32),
        scratch_shapes=[
            keep(spec_weight),
            keep(gx),
            keep(inv_wide),
            pltpu.VMEM((16 * pair_local, 128), f32),
            pltpu.VMEM((32 * pair_local, 512), bf16),
            pltpu.VMEM((32 * pair_local, 4 * nx), f32),
            pltpu.SemaphoreType.DMA((6,)),
        ],
        compiler_params=params(24),
        cost_estimate=cost(6),
        name="mode_adjoint",
    )(grad_x, far(spec_weight), far(gx), far(inv_wide), local_sums)
    received = exchange(grad_mixed)

    grad_spec = pl.pallas_call(
        functools.partial(weight_grad_kernel, nx, lines),
        grid=(quads,),
        in_specs=[line_spec, line_spec, whole(fx_wide), whole(gx)],
        out_specs=pl.BlockSpec((4, 2, channels, wide), lambda u: (u, 0, 0, 0)),
        out_shape=pltpu.HBM(spec_weight.shape, f32),
        compiler_params=params(16),
        cost_estimate=cost(6),
        name="weight_grad",
    )(spec_x, grad_x, far(fx_wide), far(gx))

    if pair_local >= MODES:
        lines_in = sums_in = received.reshape(sent, 128)
        stride_in, sums_at = stride + extra, (stride + extra, stride)
    else:
        lines_in = received[:, :block].reshape(rows, 128)
        sums_in = received[:, block:].reshape(devices * extra, 128)
        stride_in, sums_at = stride, (extra, 0)
    grad_field, grad_point, grad_bias = pl.pallas_call(
        functools.partial(
            last_kernel, stride_in, ky_own, devices, sums_at, (fwd_scale, fwd_scale / inv_scale)
        ),
        in_specs=[VM, VM, HBM, HBM, HBM],
        out_specs=[HBM, VM, VM],
        out_shape=[
            field_shape,
            jax.ShapeDtypeStruct((channels, channels), f32),
            jax.ShapeDtypeStruct((1, channels), f32),
        ],
        scratch_shapes=[
            mode_scratch,
            pltpu.VMEM(flow_field.shape, f32),
            keep(tzi_grad),
            keep(ty),
            chunk_sems,
            chunk_sems,
            pair_sems,
        ],
        compiler_params=params(16),
        cost_estimate=cost(8),
        name="field_inverse",
    )(lines_in, sums_in, far(back), far(tzi_grad), far(ty))

    return output, grad_field, grad_spec, grad_point, grad_bias.reshape(channels)


def solution(mesh):
    cells = P(("group", "space"), None, None, None)
    return jax.shard_map(
        per_device,
        mesh=mesh,
        in_specs=(cells, cells, P("space", None, None, None), P(), P()),
        out_specs=(cells, cells, cells, P("group", None), P("group")),
        check_vma=False,
    )
```

time: 138 us -> 103 us (0.75)
  blocking collectives: 66.6 us -> 14.4 us
  starting transfers between devices: 3.53 us -> 16.9 us
  local copies, waits for them, and re-layouts: 10.8 us -> 0.04 us
  Pallas kernels: 55.5 us -> 65.2 us
  waiting for transfers between devices: 0.01 us -> 4.52 us
    all_to_all x3 -> x1, blocking collectives: 44.1 us -> 14.4 us  [exchange(): lax.all_to_all(blocks, 'space', split_axis=0, concat_axis=0, tiled=True)]
    all_gather x1 -> x0, blocking collectives: 22.5 us -> none  [per_device(): gathered = lax.all_gather(local_sums, 'space', axis=0, tiled=False)]
    all_to_all x1 -> x3, starting transfers between devices: 3.53 us -> 16.9 us  [exchange(): lax.all_to_all(blocks, 'space', split_axis=0, concat_axis=0, tiled=True)]
    unnamed x28 -> x16, local copies, waits for them, and re-layouts: 10.1 us -> 0.04 us
    pallas_call x5 -> x8, Pallas kernels: 55.5 us -> 65.2 us  [the longest x1 10.6 us: per_device(): pl.pallas_call(back_kernel, grid=(slab * cuts,), in_specs=[cells_spec, ce...]
    all_to_all x1 -> x3, waiting for transfers between devices: 0.01 us -> 4.52 us  [exchange(): lax.all_to_all(blocks, 'space', split_axis=0, concat_axis=0, tiled=True)]
  transfers between devices with their start and end apart: 1 -> 3, of which waited for: 0 -> 2; matrix products, arithmetic and copies ran while one was open for 1% -> 0% of each run, Pallas kernels for 0% -> 27%
where the time goes in v2:
time: 103 us; the launch traced here: 102 us
  Pallas kernels  65.2 us (63%)
  starting transfers between devices  16.9 us (16%)
  blocking collectives  14.4 us (14%)
  waiting for transfers between devices  4.52 us (4%)
    all_to_all x3, starting transfers between devices, exchange(): lax.all_to_all(blocks, 'space', split_axis=0, concat_axis=0, tiled=True)  16.9 us
    all_to_all x1, blocking collectives, exchange(): lax.all_to_all(blocks, 'space', split_axis=0, concat_axis=0, tiled=True)  14.4 us
    pallas_call x1, Pallas kernels, per_device(): pl.pallas_call(back_kernel, grid=(slab * cuts,), in_specs=[cells_spec, ce...  10.6 us
    pallas_call x1, Pallas kernels, per_device(): pl.pallas_call(functools.partial(adjoint_kernel, slab, nx, lines, extra),...  9.79 us
    pallas_call x1, Pallas kernels, per_device(): pl.pallas_call(functools.partial(middle_kernel, stride, ky_own), in_specs...  9.21 us
    pallas_call x1, Pallas kernels, per_device(): pl.pallas_call(point_kernel, grid=(slab * cuts,), in_specs=[cells_spec, w...  8.59 us
    pallas_call x1, Pallas kernels, per_device(): pl.pallas_call(functools.partial(weight_grad_kernel, nx, lines), grid=(qu...  8.03 us
    pallas_call x1, Pallas kernels, per_device(): pl.pallas_call(functools.partial(last_kernel, stride_in, ky_own, devices,...  7.36 us
  transfers between devices with their start and end apart: 3, of which 2 were waited for; matrix products, arithmetic and copies ran while one was open for 0% of the time, Pallas kernels for 27%

profile of v2, /device:TPU:0, one launch (start us, length us, event | category | flops | bytes accessed | tf_op | source)
XLA Modules:
  0.0 102.1 jit_solution(6470901121478182300)
XLA Ops:
  0.6 0.0 copy-start.4
  0.6 0.0 copy-start.7
  0.7 6.4 %field_forward.1 = f32[512,128]{1,0:T(8,128)} custom-call(f32[2,32,128,128]{3,2,1,0:T(8,128)} %field_ref.3, bf16[128,256]{1,0:T(8,128)(2,1)} %constant.20.clone.fy_hbm.fy_ref, bf16[64,256]{1,0:T(8,128)(2,1)} %constant.21.clone.tz_hbm), custom_call_target="tpu_custom_call" | custom-call | bytes 12000000 | tf_op jit(solution)/shard_map/field_forward/pallas_call | solution.py:638
  7.1 7.4 %all-to-all-start = ((f32[16,32,128]{2,1,0:T(8,128)}), f32[16,32,128]{2,1,0:T(8,128)S(1)}, u32[]{:S(2)}, u32[]{:S(2)}) async-start(f32[16,32,128]{2,1,0:T(8,128)} %bitcast), calls=%async_computation | async-start | bytes 524288 | tf_op jit(solution)/shard_map/all_to_all | solution.py:636
  14.4 0.0 copy-done.4
  14.4 0.0 copy-done.7
  14.5 8.6 %pointwise.1.point_ref = f32[2,32,128,128]{3,2,1,0:T(8,128)} custom-call(f32[2,32,128,128]{3,2,1,0:T(8,128)} %field_ref.3, f32[32,32]{1,0:T(8,128)S(1)} %copy-done.4, f32[1,32]{1,0:T(1,128)S(1)} %bitcast.18), custom_call_target="tpu_custom_call" | custom-call | bytes 18000000 | tf_op jit(solution)/shard_map/pointwise/pallas_call | solution.py:658
  23.0 1.4 %all-to-all-done = f32[16,32,128]{2,1,0:T(8,128)S(1)} async-done(((f32[16,32,128]{2,1,0:T(8,128)}), f32[16,32,128]{2,1,0:T(8,128)S(1)}, u32[]{:S(2)}, u32[]{:S(2)}) %all-to-all-start) | async-done | bytes 262176 | tf_op jit(solution)/shard_map/all_to_all | solution.py:636
  24.5 0.0 copy-start
  24.5 0.0 copy-start.1
  24.5 0.0 copy-start.2
  24.5 0.0 copy-start.3
  24.5 0.0 copy-start.5
  24.5 0.0 copy-start.6
  24.5 5.3 %mode_mix.1 = f32[512,128]{1,0:T(8,128)S(1)} custom-call(f32[512,128]{1,0:T(8,128)S(1)} %bitcast.12, f32[32,2,32,1024]{3,2,1,0:T(8,128)} %weight_hbm.3, bf16[192,2048]{1,0:T(8,128)(2,1)} %constant.26.clone.fx_hbm.fx_ref, bf16[64,192]{1,0:T(8,128)(2,1)} %constant.28.clone.inv_hbm), custom_call_target="tpu_custom_call" | custom-call | bytes 15000000 | tf_op jit(solution)/shard_map/mode_mix/pallas_call | solution.py:671
  29.8 14.4 %all_to_all.20 = f32[16,32,128]{2,1,0:T(8,128)S(1)} all-to-all(f32[16,32,128]{2,1,0:T(8,128)S(1)} %bitcast.17), channel_id=1, replica_groups=mesh['group'=2,'space'=16] {'space'}, dimensions={0} | all-to-all | bytes 524288 | tf_op jit(solution)/shard_map/all_to_all | solution.py:636
  44.2 0.0 copy-done
  44.2 0.0 copy-done.1
  44.2 0.0 copy-done.2
  44.3 0.0 copy-done.3
  44.3 0.0 copy-done.5
  44.3 0.0 copy-done.6
  44.3 9.2 %middle.1 = (f32[2,32,128,128]{3,2,1,0:T(8,128)}, f32[2,32,128,128]{3,2,1,0:T(8,128)}, f32[512,128]{1,0:T(8,128)}) custom-call(f32[512,128]{1,0:T(8,128)S(1)} %bitcast.16, f32[2,32,128,128]{3,2,1,0:T(8,128)S(1)} %copy-done, f32[2,32,128,128]{3,2,1,0:T(8,128)S(1)} %copy-done.1, bf16[96,256]{1,0:T(8,128)(2,1)S(1)} %copy-done.5, ...), custom_call_target="tpu_custom_call" | custom-call | bytes 30000000 | tf_op jit(solution)/shard_map/middle/pallas_call | solution.py:691
  53.5 3.7 %all-to-all-start.2 = ((f32[16,32,128]{2,1,0:T(8,128)}), f32[16,32,128]{2,1,0:T(8,128)S(1)}, u32[]{:S(2)}, u32[]{:S(2)}) async-start(f32[16,32,128]{2,1,0:T(8,128)} %bitcast.5), calls=%async_computation.2 | async-start | bytes 524288 | tf_op jit(solution)/shard_map/all_to_all | solution.py:636
  57.2 10.6 %pointwise_back.1 = (f32[2,32,128,128]{3,2,1,0:T(8,128)}, f32[8,128]{1,0:T(8,128)S(1)}) custom-call(f32[2,32,128,128]{3,2,1,0:T(8,128)} %field_ref.3, f32[2,32,128,128]{3,2,1,0:T(8,128)} %get-tuple-element.19.gpre_ref, f32[32,32]{1,0:T(8,128)S(1)} %copy-done.4), custom_call_target="tpu_custom_call" | custom-call | bytes 24000000 | tf_op jit(solution)/shard_map/pointwise_back/pallas_call | solution.py:708
  67.8 0.0 all-to-all-done.2
  67.8 9.8 %mode_adjoint.1 = f32[640,128]{1,0:T(8,128)} custom-call(f32[512,128]{1,0:T(8,128)S(1)} %bitcast.14, f32[32,2,32,1024]{3,2,1,0:T(8,128)} %weight_hbm.3, bf16[64,192]{1,0:T(8,128)(2,1)} %constant.27.clone.gx_hbm.gx_ref, bf16[1024,128]{1,0:T(8,128)(2,1)} %constant.29.clone.inv_hbm, f32[8,128]{1,0:T(8,128)S(1)} %get-tuple-element.20.sums_ref), custom_call_target="tpu_custom_call" | custom-call | bytes 18000000 | tf_op jit(solution)/shard_map/mode_adjoint/pallas_call | solution.py:721
  77.6 5.8 %all-to-all-start.3 = ((f32[16,40,128]{2,1,0:T(8,128)}), f32[16,40,128]{2,1,0:T(8,128)S(1)}, u32[]{:S(2)}, u32[]{:S(2)}) async-start(f32[16,40,128]{2,1,0:T(8,128)} %bitcast.7), calls=%async_computation.3 | async-start | bytes 655360 | tf_op jit(solution)/shard_map/all_to_all | solution.py:636
  83.4 8.0 %weight_grad.1 = f32[32,2,32,1024]{3,2,1,0:T(8,128)} custom-call(f32[512,128]{1,0:T(8,128)S(1)} %bitcast.13, f32[512,128]{1,0:T(8,128)S(1)} %bitcast.15, bf16[192,2048]{1,0:T(8,128)(2,1)} %constant.26.clone.fx_hbm.fx_ref, bf16[64,192]{1,0:T(8,128)(2,1)} %constant.27.clone.gx_hbm.gx_ref), custom_call_target="tpu_custom_call" | custom-call | bytes 18000000 | tf_op jit(solution)/shard_map/weight_grad/pallas_call | solution.py:741
  91.5 3.1 %all-to-all-done.3 = f32[16,40,128]{2,1,0:T(8,128)S(1)} async-done(((f32[16,40,128]{2,1,0:T(8,128)}), f32[16,40,128]{2,1,0:T(8,128)S(1)}, u32[]{:S(2)}, u32[]{:S(2)}) %all-to-all-start.3) | async-done | bytes 327712 | tf_op jit(solution)/shard_map/all_to_all | solution.py:636
  94.5 7.4 %field_inverse.1 = (f32[2,32,128,128]{3,2,1,0:T(8,128)}, f32[32,32]{1,0:T(8,128)}, f32[1,32]{1,0:T(1,128)}) custom-call(f32[640,128]{1,0:T(8,128)S(1)} %bitcast.10, f32[640,128]{1,0:T(8,128)S(1)} %bitcast.11, f32[2,32,128,128]{3,2,1,0:T(8,128)} %get-tuple-element.21.back_hbm, bf16[96,256]{1,0:T(8,128)(2,1)} %constant.25.clone.tzi_hbm, ...), custom_call_target="tpu_custom_call" | custom-call | bytes 24000000 | tf_op jit(solution)/shard_map/field_inverse/pallas_call | solution.py:759
Async XLA Ops:
  0.6 13.8 %copy-start.4 = (f32[32,32]{1,0:T(8,128)S(1)}, f32[32,32]{1,0:T(8,128)}, u32[]{:S(2)}) copy-start(f32[32,32]{1,0:T(8,128)} %weight_ref.3) | copy-start | bytes 12292
  0.6 13.8 %copy-start.7 = (f32[32]{0:T(128)S(1)}, f32[32]{0:T(128)}, u32[]{:S(2)}) copy-start(f32[32]{0:T(128)} %param.19) | copy-start | bytes 388
  7.1 17.4 %all-to-all-start = ((f32[16,32,128]{2,1,0:T(8,128)}), f32[16,32,128]{2,1,0:T(8,128)S(1)}, u32[]{:S(2)}, u32[]{:S(2)}) async-start(f32[16,32,128]{2,1,0:T(8,128)} %bitcast), calls=%async_computation | async-start | bytes 524288 | tf_op jit(solution)/shard_map/all_to_all | solution.py:636
  24.5 19.8 %copy-start = (f32[2,32,128,128]{3,2,1,0:T(8,128)S(1)}, f32[2,32,128,128]{3,2,1,0:T(8,128)}, u32[]{:S(2)}) copy-start(f32[2,32,128,128]{3,2,1,0:T(8,128)} %pointwise.1.point_ref) | copy-start | bytes 12582916
  24.5 19.8 %copy-start.1 = (f32[2,32,128,128]{3,2,1,0:T(8,128)S(1)}, f32[2,32,128,128]{3,2,1,0:T(8,128)}, u32[]{:S(2)}) copy-start(f32[2,32,128,128]{3,2,1,0:T(8,128)} %cot_ref.1) | copy-start | bytes 12582916
  24.5 19.8 %copy-start.2 = (bf16[128,192]{1,0:T(8,128)(2,1)S(1)}, bf16[128,192]{1,0:T(8,128)(2,1)}, u32[]{:S(2)}) copy-start(bf16[128,192]{1,0:T(8,128)(2,1)} %constant.22.clone.ty_ref.ty_hbm) | copy-start | bytes 147460
  24.5 19.8 %copy-start.3 = (bf16[128,256]{1,0:T(8,128)(2,1)S(1)}, bf16[128,256]{1,0:T(8,128)(2,1)}, u32[]{:S(2)}) copy-start(bf16[128,256]{1,0:T(8,128)(2,1)} %constant.20.clone.fy_hbm.fy_ref) | copy-start | bytes 196612
  24.5 19.8 %copy-start.5 = (bf16[96,256]{1,0:T(8,128)(2,1)S(1)}, bf16[96,256]{1,0:T(8,128)(2,1)}, u32[]{:S(2)}) copy-start(bf16[96,256]{1,0:T(8,128)(2,1)} %constant.24.clone.tzi_ref) | copy-start | bytes 147460
  24.5 19.8 %copy-start.6 = (bf16[64,256]{1,0:T(8,128)(2,1)S(1)}, bf16[64,256]{1,0:T(8,128)(2,1)}, u32[]{:S(2)}) copy-start(bf16[64,256]{1,0:T(8,128)(2,1)} %constant.23.clone.tzf_ref) | copy-start | bytes 98308
  53.5 14.3 %all-to-all-start.2 = ((f32[16,32,128]{2,1,0:T(8,128)}), f32[16,32,128]{2,1,0:T(8,128)S(1)}, u32[]{:S(2)}, u32[]{:S(2)}) async-start(f32[16,32,128]{2,1,0:T(8,128)} %bitcast.5), calls=%async_computation.2 | async-start | bytes 524288 | tf_op jit(solution)/shard_map/all_to_all | solution.py:636
  77.6 16.9 %all-to-all-start.3 = ((f32[16,40,128]{2,1,0:T(8,128)}), f32[16,40,128]{2,1,0:T(8,128)S(1)}, u32[]{:S(2)}, u32[]{:S(2)}) async-start(f32[16,40,128]{2,1,0:T(8,128)} %bitcast.7), calls=%async_computation.3 | async-start | bytes 655360 | tf_op jit(solution)/shard_map/all_to_all | solution.py:636

commit v3 on v2

--- a/solution.py
+++ b/solution.py
@@ -106,19 +106,21 @@
     return (ky // ky_own) * stride + (plane * ky_own + ky % ky_own) * 8
 
 
-def forward_plane(load_channel, channels, fy_ref, tz_ref, scratch, out_ref, row_of):
+def forward_pair(c, channels, pair, fy_ref, scratch):
     nz = scratch.shape[1]
     size = KY * channels
-    for c in range(0, channels, 2):
-        pair = jnp.concatenate([load_channel(c), load_channel(c + 1)], axis=1)
-        high, low = split(pair)
-        both = dot(fy_ref[...], jnp.concatenate([high, low], axis=0))
-        half = both[: 2 * KY] + both[2 * KY :]
-        for e in range(2):
-            for part in range(2):
-                scratch[pl.ds(part * size + c + e, KY, stride=channels), :] = half[
-                    part * KY : (part + 1) * KY, e * nz : (e + 1) * nz
-                ]
+    high, low = split(pair)
+    both = dot(fy_ref[...], jnp.concatenate([high, low], axis=0))
+    half = both[: 2 * KY] + both[2 * KY :]
+    for e in range(2):
+        for part in range(2):
+            scratch[pl.ds(part * size + c + e, KY, stride=channels), :] = half[
+                part * KY : (part + 1) * KY, e * nz : (e + 1) * nz
+            ]
+
+
+def forward_finish(channels, tz_ref, scratch, out_ref, row_of):
+    size = KY * channels
     high, low = split(jnp.concatenate([scratch[:size], scratch[size:]], axis=1))
     first = dot(tz_ref[...], high, NT)
     rows = first[: 2 * MODES] + first[2 * MODES :] + dot(tz_ref[: 2 * MODES, :], low, NT)
@@ -128,7 +130,7 @@
             out_ref[pl.ds(row_of(4 * q + e), 8), :] = tile
 
 
-def inverse_plane(in_ref, row_of, tz_ref, ty_ref, scratch, channels, emit):
+def inverse_plane(in_ref, row_of, tz_ref, ty_ref, scratch, channels, emit, after, before=lambda h: None):
     nz = scratch.shape[1]
     size = KY * channels
     columns = [[] for _ in range(4)]
@@ -140,19 +142,31 @@
     modes = dot(data3(rows), tz_ref[...], TN)
     for part in range(2):
         scratch[part * size : (part + 1) * size, :] = modes[:, part * nz : (part + 1) * nz]
-    for c in range(0, channels, 2):
-        sides = []
-        for e in range(2):
-            parts = [
-                scratch[pl.ds(part * size + c + e, KY, stride=channels), :] for part in range(2)
-            ]
-            sides.append(jnp.concatenate(parts, axis=0))
-        pair = dot(ty_ref[...], data3(jnp.concatenate(sides, axis=1)))
-        for e in range(2):
-            emit(c + e, pair[:, e * nz : (e + 1) * nz])
-
-
-def spread_weight(weight, high_ref, low_ref):
+
+    def group(h, carry):
+        before(h)
+        for k in range(0, 16, 2):
+            sides = []
+            for e in range(2):
+                parts = [scratch[pl.ds(part * size + 16 * h + k + e, KY, stride=channels), :] for part in range(2)]
+                sides.append(jnp.concatenate(parts, axis=0))
+            emit(16 * h + k, dot(ty_ref[...], data3(jnp.concatenate(sides, axis=1))))
+        after(h)
+        return carry
+
+    lax.fori_loop(0, channels // 16, group, 0)
+
+
+def two(ref, p, c):
+    return jnp.concatenate([ref[p, c], ref[p, c + 1]], axis=1)
+
+
+def put_two(ref, p, c, values):
+    nz = values.shape[1] // 2
+    ref[p, c], ref[p, c + 1] = values[:, :nz], values[:, nz:]
+
+
+def spread_weight(weight, kron_ref):
     size = weight.shape[0]
     row = lax.broadcasted_iota(jnp.int32, (8 * size, size), 0) // 8
     column = lax.broadcasted_iota(jnp.int32, (8 * size, size), 1)
@@ -163,9 +177,7 @@
     wide = lax.dot_general(tall, expand, NT, precision=lax.Precision.HIGHEST, preferred_element_type=f32)
     row = lax.broadcasted_iota(jnp.int32, wide.shape, 0) % 8
     column = lax.broadcasted_iota(jnp.int32, wide.shape, 1) % 8
-    high, low = split(jnp.where(row == column, wide, 0.0))
-    high_ref[...] = high
-    low_ref[...] = low
+    kron_ref[...] = jnp.concatenate(split(jnp.where(row == column, wide, 0.0)), axis=0)
 
 
 def cell_tile(ref, plane, start):
@@ -182,8 +194,10 @@
         ref[plane, :, pl.ds(start + 8 * e, 8), :] = tile[:, e * nz : (e + 1) * nz].reshape(channels, 8, nz)
 
 
-def mix_cells(high_ref, low_ref, high, low):
-    return dot(high_ref[...], high) + dot(low_ref[...], high) + dot(high_ref[...], low)
+def mix_cells(kron_ref, high, low):
+    size = high.shape[0]
+    both = dot(kron_ref[...], high)
+    return both[:size] + both[size:] + dot(kron_ref[:size, :], low)
 
 
 def rows_at(plane, stride, ky_own):
@@ -212,33 +226,64 @@
         copy.wait()
 
     def body(p, carry):
-        def load_channel(c):
-            if c % 8 == 0:
-                part = slice(c, c + 8)
-                sem = sems.at[p * (channels // 8) + c // 8]
-                pltpu.make_async_copy(field_hbm.at[p, part], field_ref.at[p, part], sem).wait()
-            return field_ref[p, c]
-
-        forward_plane(load_channel, channels, fy_ref, tz_ref, scratch, out_ref, rows_at(p, stride, ky_own))
+        for c in range(0, channels, 2):
+            if c % 16 == 0:
+                for g in (c // 8, c // 8 + 1):
+                    part = slice(8 * g, 8 * g + 8)
+                    sem = sems.at[p * (channels // 8) + g]
+                    pltpu.make_async_copy(field_hbm.at[p, part], field_ref.at[p, part], sem).wait()
+            forward_pair(c, channels, two(field_ref, p, c), fy_ref, scratch)
+        forward_finish(channels, tz_ref, scratch, out_ref, rows_at(p, stride, ky_own))
         return carry
 
     lax.fori_loop(0, slab, body, 0)
 
 
-def point_kernel(field_ref, weight_ref, bias_ref, out_ref, kron_high, kron_low, bias_wide):
-    channels = field_ref.shape[1]
-
-    @pl.when(pl.program_id(0) == 0)
-    def _():
-        spread_weight(jnp.transpose(weight_ref[...]), kron_high, kron_low)
+def cell_copies(array_hbm, array_ref, sems, store=False):
+    cuts = array_ref.shape[2] // 32
+
+    def copy(n):
+        at = (n // cuts, slice(None), pl.ds(32 * (n % cuts), 32))
+        ends = (array_hbm.at[at], array_ref.at[at])
+        return pltpu.make_async_copy(*(ends[::-1] if store else ends), sems.at[n])
+
+    return copy, array_ref.shape[0] * cuts
+
+
+def mix_field(field_hbm, out_hbm, cells_ref, kron, offset, in_sems, out_sems, prepare):
+    load, count = cell_copies(field_hbm, cells_ref, in_sems)
+    store, _ = cell_copies(out_hbm, cells_ref, out_sems, True)
+    for n in range(count):
+        load(n).start()
+    prepare()
+    cuts = cells_ref.shape[2] // 32
+
+    def body(n, carry):
+        load(n).wait()
+        for e in range(2):
+            start = pl.multiple_of(32 * (n % cuts) + 16 * e, 16)
+            high, low = split(cell_tile(cells_ref, n // cuts, start))
+            values = mix_cells(kron, high, low)
+            put_tile(cells_ref, n // cuts, start, values if offset is None else values + offset[...])
+        store(n).start()
+        return carry
+
+    lax.fori_loop(0, count, body, 0)
+    for n in range(count):
+        store(n).wait()
+
+
+def point_kernel(field_hbm, weight_ref, bias_ref, out_hbm, cells_ref, kron, bias_wide, in_sems, out_sems):
+    channels = cells_ref.shape[1]
+
+    def prepare():
+        spread_weight(jnp.transpose(weight_ref[...]), kron)
         row = lax.broadcasted_iota(jnp.int32, (8 * channels, channels), 0) // 8
         column = lax.broadcasted_iota(jnp.int32, (8 * channels, channels), 1)
         picked = jnp.where(row == column, bias_ref[...], 0.0)
         bias_wide[...] = jnp.broadcast_to(jnp.sum(picked, axis=1, keepdims=True), bias_wide.shape)
 
-    for start in range(0, field_ref.shape[2], 16):
-        high, low = split(cell_tile(field_ref, 0, start))
-        put_tile(out_ref, 0, start, mix_cells(kron_high, kron_low, high, low) + bias_wide[...])
+    mix_field(field_hbm, out_hbm, cells_ref, kron, bias_wide, in_sems, out_sems, prepare)
 
 
 def quad_rows(ref, nx, lines, u):
@@ -312,21 +357,54 @@
     return tiles, grads
 
 
-def weight_grad_kernel(nx, lines, in_ref, grad_ref, fx_ref, gx_ref, dweight_ref):
-    u = pl.program_id(0)
+def gradient_rows(grad_ref, gx_ref, nx, lines, quads, rows_ref):
+    bias = None
+    for u in range(quads):
+        tiles, grads = gradient_tiles(grad_ref, gx_ref, nx, lines, u)
+        bias = grads[0:1, :] if u == 0 else bias
+        for part in range(2):
+            for j in range(4):
+                base = (2 * (4 * u + j) + part) * 8
+                rows_ref[base : base + 8, :] = tiles[part][j]
+    return bias
+
+
+def weight_grad_kernel(
+    nx, lines, in_ref, grad_ref, fx_hbm, gx_hbm, out_hbm, fx_ref, gx_ref, left, modes, rows_ref, grads_ref, sems, table_sems
+):
+    pairs = grads_ref.shape[1]
     wide = KX * 32
-    modes = dot(data3(quad_rows(in_ref, nx, lines, u)), fx_ref[...], TN)
-    tiles, _ = gradient_tiles(grad_ref, gx_ref, nx, lines, u)
-    for j in range(4):
-        rows = slice(32 * j, 32 * j + 32)
-        for a in range(8):
-            cols = slice(128 * a, 128 * a + 128)
-            late = slice(wide + 128 * a, wide + 128 * a + 128)
-            g_real = jnp.broadcast_to(tiles[0][j][a : a + 1, :], (32, 128))
-            g_imag = jnp.broadcast_to(tiles[1][j][a : a + 1, :], (32, 128))
-            s_real, s_imag = modes[rows, cols], modes[rows, late]
-            dweight_ref[j, 0, :, cols] = s_real * g_real + s_imag * g_imag
-            dweight_ref[j, 1, :, cols] = s_real * g_imag - s_imag * g_real
+    tables = transfers([(gx_hbm, gx_ref), (fx_hbm, fx_ref)], table_sems)
+    for copy in tables:
+        copy.start()
+    for u in range(pairs // 4):
+        left[128 * u : 128 * u + 128, :] = data_rows(in_ref, nx, lines, u)
+    for copy in tables:
+        copy.wait()
+    gradient_rows(grad_ref, gx_ref, nx, lines, pairs // 4, rows_ref)
+    parts = [(grads_ref.at[t], out_hbm.at[:, :, :, pl.ds(256 * t, 256)]) for t in range(4)]
+    stores = transfers(parts, sems)
+    for t in range(4):
+        modes[:, :256] = dot(left[...], fx_ref[:, 256 * t : 256 * t + 256])
+        modes[:, 256:] = dot(left[...], fx_ref[:, wide + 256 * t : wide + 256 * t + 256])
+
+        def body(pair, carry):
+            rows = pl.ds(pl.multiple_of(32 * pair, 32), 32)
+            for e in range(2):
+                g_real, g_imag = [
+                    jnp.broadcast_to(rows_ref[pl.ds((2 * pair + part) * 8 + 2 * t + e, 1), :], (32, 128))
+                    for part in range(2)
+                ]
+                cols = slice(128 * e, 128 * e + 128)
+                real, imag = modes[rows, cols], modes[rows, 256 + 128 * e : 384 + 128 * e]
+                grads_ref[t, pair, 0, :, cols] = real * g_real + imag * g_imag
+                grads_ref[t, pair, 1, :, cols] = real * g_imag - imag * g_real
+            return carry
+
+        lax.fori_loop(0, pairs, body, 0, unroll=4)
+        stores[t].start()
+    for copy in stores:
+        copy.wait()
 
 
 def adjoint_kernel(
@@ -344,32 +422,28 @@
     gx_ref,
     inv_ref,
     rows_ref,
-    left,
+    soon,
+    late,
     total,
     sems,
 ):
     pairs = weight_ref.shape[0]
     devices = nx // slab
     stride = slab * lines + extra
-    bias = None
     tables, loads = weight_loads(weight_hbm, weight_ref, [(gx_hbm, gx_ref), (inv_hbm, inv_ref)], sems)
     for copy in tables:
         copy.wait()
-    for u in range(pairs // 4):
-        tiles, grads = gradient_tiles(grad_ref, gx_ref, nx, lines, u)
-        bias = grads[0:1, :] if u == 0 else bias
-        for part in range(2):
-            for j in range(4):
-                base = (2 * (4 * u + j) + part) * 8
-                rows_ref[base : base + 8, :] = tiles[part][j]
+    bias = gradient_rows(grad_ref, gx_ref, nx, lines, pairs // 4, rows_ref)
+    total[...] = jnp.zeros_like(total)
+    late[...] = jnp.zeros_like(late)
     early = lax.broadcasted_iota(jnp.int32, (32, 128), 1) % 32 < 16
-    for t in range(4):
-        loads[t].wait()
-
-        def body(pair, carry):
-            rows = pl.ds(pl.multiple_of(32 * pair, 32), 32)
+    count = pairs // 2
+
+    def products(t, first, target):
+        for k in range(count):
+            pair = first + k
             for e in range(2):
-                cols = slice(256 * t + 128 * e, 256 * t + 128 * e + 128)
+                cols = pl.ds(pl.multiple_of(256 * t + 128 * e, 128), 128)
                 g_real, g_imag = [
                     jnp.broadcast_to(rows_ref[pl.ds((2 * pair + part) * 8 + 2 * t + e, 1), :], (32, 128))
                     for part in range(2)
@@ -379,17 +453,27 @@
                 imag = g_imag * w_real - g_real * w_imag
                 folded = jnp.where(early, real + pltpu.roll(real, 112, 1), imag + pltpu.roll(imag, 16, 1))
                 high, low = split(folded)
-                left[rows, 128 * e : 128 * e + 128] = high
-                left[rows, 256 + 128 * e : 384 + 128 * e] = low
-            return carry
-
-        lax.fori_loop(0, pairs, body, 0, unroll=4)
-        table = inv_ref[256 * t : 256 * t + 256, :]
-        product = dot(left[:, :256], table) + dot(left[:, 256:], table)
-        if t == 0:
-            total[...] = product
-        else:
-            total[...] += product
+                target[32 * k : 32 * k + 32, 128 * e : 128 * e + 128] = high
+                target[32 * k : 32 * k + 32, 256 + 128 * e : 384 + 128 * e] = low
+
+    def gather(t, source, first):
+        table = inv_ref[pl.ds(pl.multiple_of(256 * t, 256), 256), :]
+        rows = slice(32 * first, 32 * (first + count))
+        total[rows, :] += dot(source[:, :256], table) + dot(source[:, 256:], table)
+
+    def body(t, carry):
+        part = pl.ds(pl.multiple_of(256 * t, 256), 256)
+        pltpu.make_async_copy(
+            weight_hbm.at[:, :, :, part], weight_ref.at[:, :, :, part], sems.at[len(tables) + t]
+        ).wait()
+        gather(jnp.maximum(t - 1, 0), late, count)
+        products(t, 0, soon)
+        gather(t, soon, 0)
+        products(t, count, late)
+        return carry
+
+    lax.fori_loop(0, 4, body, 0)
+    gather(3, late, count)
     lane = lax.broadcasted_iota(jnp.int32, (nx, 128), 1)
     carried = lax.axis_index("space") == 0
     for u in range(pairs // 4):
@@ -429,7 +513,7 @@
     rate = math.sqrt(2.0 / math.pi)
 
     def stores(p, g):
-        part = slice(8 * g, 8 * g + 8)
+        part = pl.ds(8 * g, 8)
         pairs = ((output_ref, output_hbm), (gpre_ref, gpre_hbm))
         return [
             pltpu.make_async_copy(src.at[p, part], dst.at[p, part], sems.at[k, p, g])
@@ -439,20 +523,28 @@
     def body(p, carry):
         row_of = rows_at(p, stride, ky_own)
 
-        def emit(channel, spectral):
-            values = spectral + point_ref[p, channel]
+        def emit(c, spectral):
+            values = spectral + two(point_ref, p, c)
             square = values * values
-            bent = jnp.tanh(rate * values * (1.0 + 0.044715 * square))
-            half = 0.5 + 0.5 * bent
-            output_ref[p, channel] = values * half
-            slope = half + (0.5 * rate) * values * (1.0 - bent * bent) * (1.0 + (3 * 0.044715) * square)
-            gpre_ref[p, channel] = cot_ref[p, channel] * slope
-            if channel % 8 == 7:
-                for copy in stores(p, channel // 8):
+            half = 0.5 + 0.5 * jnp.tanh(values * (rate + (0.044715 * rate) * square))
+            result = values * half
+            put_two(output_ref, p, c, result)
+            slope = half + result * (1.0 - half) * (2.0 * rate + (6 * 0.044715 * rate) * square)
+            put_two(gpre_ref, p, c, two(cot_ref, p, c) * slope)
+
+        def after(h):
+            for g in range(2):
+                for copy in stores(p, 2 * h + g):
                     copy.start()
 
-        inverse_plane(in_ref, row_of, tzi_ref, ty_ref, scratch, channels, emit)
-        forward_plane(lambda c: gpre_ref[p, c], channels, fy_ref, tzf_ref, scratch, spec_ref, row_of)
+        inverse_plane(in_ref, row_of, tzi_ref, ty_ref, scratch, channels, emit, after)
+
+        def pair(k, carry):
+            forward_pair(2 * k, channels, two(gpre_ref, p, 2 * k), fy_ref, scratch)
+            return carry
+
+        lax.fori_loop(0, channels // 2, pair, 0, unroll=8)
+        forward_finish(channels, tzf_ref, scratch, spec_ref, row_of)
         return carry
 
     lax.fori_loop(0, slab, body, 0)
@@ -462,33 +554,46 @@
                 copy.wait()
 
 
-def back_kernel(field_ref, gpre_ref, weight_ref, out_ref, sums_ref, kron_high, kron_low, outer):
+def back_kernel(gpre_hbm, weight_ref, out_hbm, cells_ref, kron, in_sems, out_sems):
+    prepare = lambda: spread_weight(weight_ref[...], kron)
+    mix_field(gpre_hbm, out_hbm, cells_ref, kron, None, in_sems, out_sems, prepare)
+
+
+def outer_kernel(field_hbm, gpre_hbm, sums_ref, field_ref, gpre_ref, outer, field_sems, gpre_sems):
     channels = field_ref.shape[1]
-
-    @pl.when(pl.program_id(0) == 0)
-    def _():
-        spread_weight(weight_ref[...], kron_high, kron_low)
-        outer[...] = jnp.zeros_like(outer)
-
-    for start in range(0, field_ref.shape[2], 16):
-        high, low = split(cell_tile(field_ref, 0, start))
-        g_high, g_low = split(cell_tile(gpre_ref, 0, start))
-        put_tile(out_ref, 0, start, mix_cells(kron_high, kron_low, g_high, g_low))
-        outer[...] += dot(high, g_high, NT) + dot(low, g_high, NT) + dot(high, g_low, NT)
-
-    @pl.when(pl.program_id(0) == pl.num_programs(0) - 1)
-    def _():
-        row = lax.broadcasted_iota(jnp.int32, outer.shape, 0) % 8
-        column = lax.broadcasted_iota(jnp.int32, outer.shape, 1) % 8
-        kept = jnp.where(row == column, outer[...], 0.0)
-        kept = jnp.sum(kept.reshape(channels, 8, 8 * channels), axis=1)
-        row = lax.broadcasted_iota(jnp.int32, (8 * channels, channels), 0) // 8
-        column = lax.broadcasted_iota(jnp.int32, (8 * channels, channels), 1)
-        pick = (row == column).astype(f32)
-        small = lax.dot_general(
-            kept, pick, (((1,), (0,)), ((), ())), precision=lax.Precision.HIGHEST, preferred_element_type=f32
-        )
-        sums_ref[...] = jnp.concatenate([small[8 * g : 8 * g + 8] for g in range(4)], axis=1)
+    load, count = cell_copies(field_hbm, field_ref, field_sems)
+    load_gpre, _ = cell_copies(gpre_hbm, gpre_ref, gpre_sems)
+    for n in range(count):
+        load(n).start()
+        load_gpre(n).start()
+    outer[...] = jnp.zeros_like(outer)
+    cuts = field_ref.shape[2] // 32
+
+    def body(n, carry):
+        load(n).wait()
+        load_gpre(n).wait()
+        total = outer[...]
+        for e in range(2):
+            start = pl.multiple_of(32 * (n % cuts) + 16 * e, 16)
+            high, low = split(cell_tile(field_ref, n // cuts, start))
+            g_high, g_low = split(cell_tile(gpre_ref, n // cuts, start))
+            both = dot(jnp.concatenate([high, low], axis=0), g_high, NT)
+            total = total + (both[: 8 * channels] + both[8 * channels :] + dot(high, g_low, NT))
+        outer[...] = total
+        return carry
+
+    lax.fori_loop(0, count, body, 0)
+    row = lax.broadcasted_iota(jnp.int32, outer.shape, 0) % 8
+    column = lax.broadcasted_iota(jnp.int32, outer.shape, 1) % 8
+    kept = jnp.where(row == column, outer[...], 0.0)
+    kept = jnp.sum(kept.reshape(channels, 8, 8 * channels), axis=1)
+    row = lax.broadcasted_iota(jnp.int32, (8 * channels, channels), 0) // 8
+    column = lax.broadcasted_iota(jnp.int32, (8 * channels, channels), 1)
+    pick = (row == column).astype(f32)
+    small = lax.dot_general(
+        kept, pick, (((1,), (0,)), ((), ())), precision=lax.Precision.HIGHEST, preferred_element_type=f32
+    )
+    sums_ref[...] = jnp.concatenate([small[8 * g : 8 * g + 8] for g in range(4)], axis=1)
 
 
 def last_kernel(
@@ -521,7 +626,7 @@
     stores = transfers([(cells_ref.at[at], out_hbm.at[at]) for at in places], out_sems)
 
     def one(p, g, store):
-        at = (p, slice(8 * g, 8 * g + 8))
+        at = (p, pl.ds(8 * g, 8))
         if store:
             return pltpu.make_async_copy(cells_ref.at[at], out_hbm.at[at], out_sems.at[p * groups + g])
         return pltpu.make_async_copy(back_hbm.at[at], cells_ref.at[at], in_sems.at[p * groups + g])
@@ -539,14 +644,20 @@
         copy.wait()
 
     def body(p, carry):
-        def emit(channel, values):
-            if channel % 8 == 0:
-                one(p, channel // 8, False).wait()
-            cells_ref[p, channel] = cells_ref[p, channel] + values
-            if channel % 8 == 7:
-                one(p, channel // 8, True).start()
-
-        inverse_plane(in_ref, rows_at(p, stride, ky_own), tzi_ref, ty_ref, scratch, channels, emit)
+        def before(h):
+            one(p, 2 * h, False).wait()
+            one(p, 2 * h + 1, False).wait()
+
+        def emit(c, values):
+            put_two(cells_ref, p, c, two(cells_ref, p, c) + values)
+
+        def after(h):
+            one(p, 2 * h, True).start()
+            one(p, 2 * h + 1, True).start()
+
+        inverse_plane(
+            in_ref, rows_at(p, stride, ky_own), tzi_ref, ty_ref, scratch, channels, emit, after, before
+        )
         return carry
 
     lax.fori_loop(0, slab, body, 0)
@@ -556,11 +667,6 @@
 
 VM = pl.BlockSpec(memory_space=pltpu.VMEM)
 HBM = pl.BlockSpec(memory_space=pltpu.HBM)
-
-
-def whole(array):
-    zeros = (0,) * array.ndim
-    return pl.BlockSpec(array.shape, lambda *_: zeros)
 
 
 def params(megabytes):
@@ -596,7 +702,6 @@
     block = slab * lines
     stride = slab * ky_own * 8
     extra = 8
-    quads = pair_local // 4
     wide = KX * channels
     fwd_scale = float(nx * ny * nz) ** (-0.5)
     inv_scale = float(4 * MODES**3) ** (-0.5)
@@ -621,15 +726,13 @@
     inv_wide = jnp.asarray(np.repeat(inv_wide.reshape(2 * KX, 4 * nx), channels // 2, axis=0))
 
     line_shape = jax.ShapeDtypeStruct((rows, 128), f32)
-    line_spec = pl.BlockSpec((rows, 128), lambda p: (0, 0))
     field_shape = pltpu.HBM(flow_field.shape, f32)
     mode_scratch = pltpu.VMEM((2 * KY * channels, nz), f32)
-    kron_scratch = pltpu.VMEM((8 * channels, 8 * channels), bf16)
+    kron_scratch = pltpu.VMEM((16 * channels, 8 * channels), bf16)
     chunk_count = slab * (channels // 8)
     chunk_sems = pltpu.SemaphoreType.DMA((chunk_count,))
     pair_sems = pltpu.SemaphoreType.DMA((2,))
-    cuts = ny // 32
-    cells_spec = pl.BlockSpec((1, channels, 32, nz), lambda s: (s // cuts, 0, s % cuts, 0))
+    cell_sems = pltpu.SemaphoreType.DMA((slab * (ny // 32),))
 
     def exchange(lines_out):
         blocks = lines_out.reshape(devices, -1, 128)
@@ -657,11 +760,16 @@
     bias = pointwise_bias.reshape(1, channels)
     pointwise = pl.pallas_call(
         point_kernel,
-        grid=(slab * cuts,),
-        in_specs=[cells_spec, whole(point_weight), whole(bias)],
-        out_specs=cells_spec,
+        in_specs=[HBM, VM, VM],
+        out_specs=HBM,
         out_shape=field_shape,
-        scratch_shapes=[kron_scratch, kron_scratch, pltpu.VMEM((8 * channels, 2 * nz), f32)],
+        scratch_shapes=[
+            keep(flow_field),
+            kron_scratch,
+            pltpu.VMEM((8 * channels, 2 * nz), f32),
+            cell_sems,
+            cell_sems,
+        ],
         compiler_params=params(16),
         cost_estimate=cost(6),
         name="pointwise",
@@ -705,17 +813,22 @@
     )(mixed, near(pointwise), near(cotangent), near(tzi_out), near(ty), near(fy), near(tz_grad))
     grad_x = exchange(grad_lines).reshape(rows, 128)
 
-    back, local_sums = pl.pallas_call(
-        back_kernel,
-        grid=(slab * cuts,),
-        in_specs=[cells_spec, cells_spec, whole(point_weight)],
-        out_specs=[cells_spec, pl.BlockSpec((extra, 128), lambda s: (0, 0))],
-        out_shape=[field_shape, jax.ShapeDtypeStruct((extra, 128), f32)],
-        scratch_shapes=[kron_scratch, kron_scratch, pltpu.VMEM((8 * channels, 8 * channels), f32)],
+    local_sums = pl.pallas_call(
+        outer_kernel,
+        in_specs=[HBM, HBM],
+        out_specs=VM,
+        out_shape=jax.ShapeDtypeStruct((extra, 128), f32),
+        scratch_shapes=[
+            keep(flow_field),
+            keep(flow_field),
+            pltpu.VMEM((8 * channels, 8 * channels), f32),
+            cell_sems,
+            cell_sems,
+        ],
         compiler_params=params(16),
-        cost_estimate=cost(8),
-        name="pointwise_back",
-    )(far(flow_field), far(gpre), point_weight)
+        cost_estimate=cost(6),
+        name="outer_sums",
+    )(far(flow_field), far(gpre))
 
     sent = devices * (block + extra)
     grad_mixed = pl.pallas_call(
@@ -728,7 +841,8 @@
             keep(gx),
             keep(inv_wide),
             pltpu.VMEM((16 * pair_local, 128), f32),
-            pltpu.VMEM((32 * pair_local, 512), bf16),
+            pltpu.VMEM((16 * pair_local, 512), bf16),
+            pltpu.VMEM((16 * pair_local, 512), bf16),
             pltpu.VMEM((32 * pair_local, 4 * nx), f32),
             pltpu.SemaphoreType.DMA((6,)),
         ],
@@ -736,18 +850,38 @@
         cost_estimate=cost(6),
         name="mode_adjoint",
     )(grad_x, far(spec_weight), far(gx), far(inv_wide), local_sums)
-    received = exchange(grad_mixed)
-
     grad_spec = pl.pallas_call(
         functools.partial(weight_grad_kernel, nx, lines),
-        grid=(quads,),
-        in_specs=[line_spec, line_spec, whole(fx_wide), whole(gx)],
-        out_specs=pl.BlockSpec((4, 2, channels, wide), lambda u: (u, 0, 0, 0)),
+        in_specs=[VM, VM, HBM, HBM],
+        out_specs=HBM,
         out_shape=pltpu.HBM(spec_weight.shape, f32),
-        compiler_params=params(16),
+        scratch_shapes=[
+            keep(fx_wide),
+            keep(gx),
+            pltpu.VMEM((32 * pair_local, 6 * nx), bf16),
+            pltpu.VMEM((32 * pair_local, 512), f32),
+            pltpu.VMEM((16 * pair_local, 128), f32),
+            pltpu.VMEM((4, pair_local, 2, channels, wide // 4), f32),
+            pltpu.SemaphoreType.DMA((4,)),
+            pair_sems,
+        ],
+        compiler_params=params(24),
         cost_estimate=cost(6),
         name="weight_grad",
     )(spec_x, grad_x, far(fx_wide), far(gx))
+
+    gpre, grad_mixed = lax.optimization_barrier((gpre, grad_mixed))
+    received = exchange(grad_mixed)
+    back = pl.pallas_call(
+        back_kernel,
+        in_specs=[HBM, VM],
+        out_specs=HBM,
+        out_shape=field_shape,
+        scratch_shapes=[keep(flow_field), kron_scratch, cell_sems, cell_sems],
+        compiler_params=params(16),
+        cost_estimate=cost(6),
+        name="pointwise_back",
+    )(far(gpre), point_weight)
 
     if pair_local >= MODES:
         lines_in = sums_in = received.reshape(sent, 128)

time: 103 us -> 92.4 us (0.90)
  Pallas kernels: 65.2 us -> 53.8 us
  waiting for transfers between devices: 4.52 us -> 9.71 us
  starting transfers between devices: 16.9 us -> 14.7 us
  blocking collectives: 14.4 us -> 12.8 us
    pallas_call x3 -> x4, Pallas kernels: 27.2 us -> 21.2 us  [the longest x1 5.57 us: per_device(): pl.pallas_call(functools.partial(weight_grad_kernel, nx, lines), in_specs...]
    all_to_all x3, waiting for transfers between devices: 4.52 us -> 9.71 us  [exchange(): lax.all_to_all(blocks, 'space', split_axis=0, concat_axis=0, tiled=True)]
    pallas_call x1, Pallas kernels: 9.79 us -> 6.04 us  [per_device(): pl.pallas_call(functools.partial(adjoint_kernel, slab, nx, lines, extra),...]
    all_to_all x3, starting transfers between devices: 16.9 us -> 14.7 us  [exchange(): lax.all_to_all(blocks, 'space', split_axis=0, concat_axis=0, tiled=True)]
    all_to_all x1, blocking collectives: 14.4 us -> 12.8 us  [exchange(): lax.all_to_all(blocks, 'space', split_axis=0, concat_axis=0, tiled=True)]
  transfers between devices with their start and end apart: 3 -> 3, of which waited for: 2 -> 3; matrix products, arithmetic and copies ran while one was open for 0% -> 0% of each run, Pallas kernels for 27% -> 23%
where the time goes in v3:
time: 92.4 us; the launch traced here: 92 us
  Pallas kernels  53.8 us (58%)
  starting transfers between devices  14.7 us (16%)
  blocking collectives  12.8 us (14%)
  waiting for transfers between devices  9.71 us (11%)
  between operations  0.96 us (1%)
    all_to_all x3, starting transfers between devices, exchange(): lax.all_to_all(blocks, 'space', split_axis=0, concat_axis=0, tiled=True)  14.7 us
    all_to_all x1, blocking collectives, exchange(): lax.all_to_all(blocks, 'space', split_axis=0, concat_axis=0, tiled=True)  12.8 us
    all_to_all x3, waiting for transfers between devices, exchange(): lax.all_to_all(blocks, 'space', split_axis=0, concat_axis=0, tiled=True)  9.71 us
    pallas_call x1, Pallas kernels, per_device(): pl.pallas_call(functools.partial(middle_kernel, stride, ky_own), in_specs...  8.75 us
    pallas_call x1, Pallas kernels, per_device(): pl.pallas_call(functools.partial(last_kernel, stride_in, ky_own, devices,...  6.76 us
    pallas_call x1, Pallas kernels, per_device(): pl.pallas_call(functools.partial(adjoint_kernel, slab, nx, lines, extra),...  6.04 us
    pallas_call x1, Pallas kernels, per_device(): pl.pallas_call(functools.partial(first_kernel, stride, ky_own), in_specs=...  5.79 us
    pallas_call x1, Pallas kernels, per_device(): pl.pallas_call(functools.partial(weight_grad_kernel, nx, lines), in_specs...  5.57 us
  transfers between devices with their start and end apart: 3, of which 3 were waited for; matrix products, arithmetic and copies ran while one was open for 0% of the time, Pallas kernels for 23%

profile of v3, /device:TPU:0, one launch (start us, length us, event | category | flops | bytes accessed | tf_op | source)
XLA Modules:
  0.0 92.0 jit_solution(4177229046152137672)
XLA Ops:
  0.6 0.0 copy-start.4
  0.6 0.0 copy-start.7
  0.7 5.8 %field_forward.1 = f32[512,128]{1,0:T(8,128)} custom-call(f32[2,32,128,128]{3,2,1,0:T(8,128)} %field_hbm.5, bf16[128,256]{1,0:T(8,128)(2,1)} %constant.20.clone.fy_hbm.fy_ref, bf16[64,256]{1,0:T(8,128)(2,1)} %constant.21.clone.tz_hbm), custom_call_target="tpu_custom_call" | custom-call | bytes 12000000 | tf_op jit(solution)/shard_map/field_forward/pallas_call | solution.py:741
  6.4 7.4 %all-to-all-start = ((f32[16,32,128]{2,1,0:T(8,128)}), f32[16,32,128]{2,1,0:T(8,128)S(1)}, u32[]{:S(2)}, u32[]{:S(2)}) async-start(f32[16,32,128]{2,1,0:T(8,128)} %bitcast), calls=%async_computation | async-start | bytes 524288 | tf_op jit(solution)/shard_map/all_to_all | solution.py:739
  13.8 0.0 copy-done.4
  13.8 0.0 copy-done.7
  13.8 5.6 %pointwise.1.point_ref = f32[2,32,128,128]{3,2,1,0:T(8,128)} custom-call(f32[2,32,128,128]{3,2,1,0:T(8,128)} %field_hbm.5, f32[32,32]{1,0:T(8,128)S(1)} %copy-done.4, f32[1,32]{1,0:T(1,128)S(1)} %bitcast.18), custom_call_target="tpu_custom_call" | custom-call | bytes 18000000 | tf_op jit(solution)/shard_map/pointwise/pallas_call | solution.py:761
  19.4 4.5 %all-to-all-done = f32[16,32,128]{2,1,0:T(8,128)S(1)} async-done(((f32[16,32,128]{2,1,0:T(8,128)}), f32[16,32,128]{2,1,0:T(8,128)S(1)}, u32[]{:S(2)}, u32[]{:S(2)}) %all-to-all-start) | async-done | bytes 262176 | tf_op jit(solution)/shard_map/all_to_all | solution.py:739
  23.9 0.0 copy-start
  23.9 0.0 copy-start.1
  23.9 0.0 copy-start.2
  23.9 0.0 copy-start.3
  23.9 0.0 copy-start.5
  23.9 0.0 copy-start.6
  23.9 5.3 %mode_mix.1 = f32[512,128]{1,0:T(8,128)S(1)} custom-call(f32[512,128]{1,0:T(8,128)S(1)} %bitcast.12, f32[32,2,32,1024]{3,2,1,0:T(8,128)} %weight_hbm.3, bf16[192,2048]{1,0:T(8,128)(2,1)} %constant.26.clone.fx_hbm, bf16[64,192]{1,0:T(8,128)(2,1)} %constant.28.clone.inv_hbm), custom_call_target="tpu_custom_call" | custom-call | bytes 15000000 | tf_op jit(solution)/shard_map/mode_mix/pallas_call | solution.py:779
  29.2 12.8 %all_to_all.20 = f32[16,32,128]{2,1,0:T(8,128)S(1)} all-to-all(f32[16,32,128]{2,1,0:T(8,128)S(1)} %bitcast.17), channel_id=1, replica_groups=mesh['group'=2,'space'=16] {'space'}, dimensions={0} | all-to-all | bytes 524288 | tf_op jit(solution)/shard_map/all_to_all | solution.py:739
  42.0 0.0 copy-done
  42.0 0.0 copy-done.1
  42.0 0.0 copy-done.2
  42.0 0.0 copy-done.3
  42.0 0.0 copy-done.5
  42.1 0.0 copy-done.6
  42.1 8.7 %middle.1 = (f32[2,32,128,128]{3,2,1,0:T(8,128)}, f32[2,32,128,128]{3,2,1,0:T(8,128)}, f32[512,128]{1,0:T(8,128)}) custom-call(f32[512,128]{1,0:T(8,128)S(1)} %bitcast.16, f32[2,32,128,128]{3,2,1,0:T(8,128)S(1)} %copy-done, f32[2,32,128,128]{3,2,1,0:T(8,128)S(1)} %copy-done.1, bf16[96,256]{1,0:T(8,128)(2,1)S(1)} %copy-done.5, ...), custom_call_target="tpu_custom_call" | custom-call | bytes 30000000 | tf_op jit(solution)/shard_map/middle/pallas_call | solution.py:799
  50.8 3.5 %all-to-all-start.2 = ((f32[16,32,128]{2,1,0:T(8,128)}), f32[16,32,128]{2,1,0:T(8,128)S(1)}, u32[]{:S(2)}, u32[]{:S(2)}) async-start(f32[16,32,128]{2,1,0:T(8,128)} %bitcast.5), calls=%async_computation.2 | async-start | bytes 524288 | tf_op jit(solution)/shard_map/all_to_all | solution.py:739
  54.4 5.0 %outer_sums.1.sums_ref = f32[8,128]{1,0:T(8,128)S(1)} custom-call(f32[2,32,128,128]{3,2,1,0:T(8,128)} %field_hbm.5, f32[2,32,128,128]{3,2,1,0:T(8,128)} %get-tuple-element.21.gpre_hbm), custom_call_target="tpu_custom_call" | custom-call | bytes 18000000 | tf_op jit(solution)/shard_map/outer_sums/pallas_call | solution.py:816
  59.4 5.0 %all-to-all-done.2 = f32[16,32,128]{2,1,0:T(8,128)S(1)} async-done(((f32[16,32,128]{2,1,0:T(8,128)}), f32[16,32,128]{2,1,0:T(8,128)S(1)}, u32[]{:S(2)}, u32[]{:S(2)}) %all-to-all-start.2) | async-done | bytes 262176 | tf_op jit(solution)/shard_map/all_to_all | solution.py:739
  64.4 6.0 %mode_adjoint.1 = f32[640,128]{1,0:T(8,128)} custom-call(f32[512,128]{1,0:T(8,128)S(1)} %bitcast.14, f32[32,2,32,1024]{3,2,1,0:T(8,128)} %weight_hbm.3, bf16[64,192]{1,0:T(8,128)(2,1)} %constant.27.clone.gx_hbm, bf16[1024,128]{1,0:T(8,128)(2,1)} %constant.29.clone.inv_hbm, f32[8,128]{1,0:T(8,128)S(1)} %outer_sums.1.sums_ref), custom_call_target="tpu_custom_call" | custom-call | bytes 18000000 | tf_op jit(solution)/shard_map/mode_adjoint/pallas_call | solution.py:834
  70.4 3.7 %all-to-all-start.3 = ((f32[16,40,128]{2,1,0:T(8,128)}), f32[16,40,128]{2,1,0:T(8,128)S(1)}, u32[]{:S(2)}, u32[]{:S(2)}) async-start(f32[16,40,128]{2,1,0:T(8,128)} %bitcast.7), calls=%async_computation.3 | async-start | bytes 655360 | tf_op jit(solution)/shard_map/all_to_all | solution.py:739
  74.2 5.6 %weight_grad.1 = f32[32,2,32,1024]{3,2,1,0:T(8,128)} custom-call(f32[512,128]{1,0:T(8,128)S(1)} %bitcast.13, f32[512,128]{1,0:T(8,128)S(1)} %bitcast.15, bf16[192,2048]{1,0:T(8,128)(2,1)} %constant.26.clone.fx_hbm, bf16[64,192]{1,0:T(8,128)(2,1)} %constant.27.clone.gx_hbm), custom_call_target="tpu_custom_call" | custom-call | bytes 18000000 | tf_op jit(solution)/shard_map/weight_grad/pallas_call | solution.py:853
  79.7 5.0 %pointwise_back.1.back_hbm = f32[2,32,128,128]{3,2,1,0:T(8,128)} custom-call(f32[2,32,128,128]{3,2,1,0:T(8,128)} %get-tuple-element.21.gpre_hbm, f32[32,32]{1,0:T(8,128)S(1)} %copy-done.4), custom_call_target="tpu_custom_call" | custom-call | bytes 18000000 | tf_op jit(solution)/shard_map/pointwise_back/pallas_call | solution.py:875
  84.7 0.3 all-to-all-done.3
  85.0 6.8 %field_inverse.1 = (f32[2,32,128,128]{3,2,1,0:T(8,128)}, f32[32,32]{1,0:T(8,128)}, f32[1,32]{1,0:T(1,128)}) custom-call(f32[640,128]{1,0:T(8,128)S(1)} %bitcast.10, f32[640,128]{1,0:T(8,128)S(1)} %bitcast.11, f32[2,32,128,128]{3,2,1,0:T(8,128)} %pointwise_back.1.back_hbm, bf16[96,256]{1,0:T(8,128)(2,1)} %constant.25.clone.tzi_hbm, ...), custom_call_target="tpu_custom_call" | custom-call | bytes 24000000 | tf_op jit(solution)/shard_map/field_inverse/pallas_call | solution.py:893
Async XLA Ops:
  0.6 13.2 %copy-start.4 = (f32[32,32]{1,0:T(8,128)S(1)}, f32[32,32]{1,0:T(8,128)}, u32[]{:S(2)}) copy-start(f32[32,32]{1,0:T(8,128)} %weight_ref.3) | copy-start | bytes 12292
  0.6 13.2 %copy-start.7 = (f32[32]{0:T(128)S(1)}, f32[32]{0:T(128)}, u32[]{:S(2)}) copy-start(f32[32]{0:T(128)} %param.19) | copy-start | bytes 388
  6.4 17.4 %all-to-all-start = ((f32[16,32,128]{2,1,0:T(8,128)}), f32[16,32,128]{2,1,0:T(8,128)S(1)}, u32[]{:S(2)}, u32[]{:S(2)}) async-start(f32[16,32,128]{2,1,0:T(8,128)} %bitcast), calls=%async_computation | async-start | bytes 524288 | tf_op jit(solution)/shard_map/all_to_all | solution.py:739
  23.9 18.2 %copy-start = (f32[2,32,128,128]{3,2,1,0:T(8,128)S(1)}, f32[2,32,128,128]{3,2,1,0:T(8,128)}, u32[]{:S(2)}) copy-start(f32[2,32,128,128]{3,2,1,0:T(8,128)} %pointwise.1.point_ref) | copy-start | bytes 12582916
  23.9 18.2 %copy-start.1 = (f32[2,32,128,128]{3,2,1,0:T(8,128)S(1)}, f32[2,32,128,128]{3,2,1,0:T(8,128)}, u32[]{:S(2)}) copy-start(f32[2,32,128,128]{3,2,1,0:T(8,128)} %cot_ref.1) | copy-start | bytes 12582916
  23.9 18.2 %copy-start.2 = (bf16[128,192]{1,0:T(8,128)(2,1)S(1)}, bf16[128,192]{1,0:T(8,128)(2,1)}, u32[]{:S(2)}) copy-start(bf16[128,192]{1,0:T(8,128)(2,1)} %constant.22.clone.ty_ref.ty_hbm) | copy-start | bytes 147460
  23.9 18.2 %copy-start.3 = (bf16[128,256]{1,0:T(8,128)(2,1)S(1)}, bf16[128,256]{1,0:T(8,128)(2,1)}, u32[]{:S(2)}) copy-start(bf16[128,256]{1,0:T(8,128)(2,1)} %constant.20.clone.fy_hbm.fy_ref) | copy-start | bytes 196612
  23.9 18.2 %copy-start.5 = (bf16[96,256]{1,0:T(8,128)(2,1)S(1)}, bf16[96,256]{1,0:T(8,128)(2,1)}, u32[]{:S(2)}) copy-start(bf16[96,256]{1,0:T(8,128)(2,1)} %constant.24.clone.tzi_ref) | copy-start | bytes 147460
  23.9 18.2 %copy-start.6 = (bf16[64,256]{1,0:T(8,128)(2,1)S(1)}, bf16[64,256]{1,0:T(8,128)(2,1)}, u32[]{:S(2)}) copy-start(bf16[64,256]{1,0:T(8,128)(2,1)} %constant.23.clone.tzf_ref) | copy-start | bytes 98308
  50.8 13.6 %all-to-all-start.2 = ((f32[16,32,128]{2,1,0:T(8,128)}), f32[16,32,128]{2,1,0:T(8,128)S(1)}, u32[]{:S(2)}, u32[]{:S(2)}) async-start(f32[16,32,128]{2,1,0:T(8,128)} %bitcast.5), calls=%async_computation.2 | async-start | bytes 524288 | tf_op jit(solution)/shard_map/all_to_all | solution.py:739
  70.4 14.6 %all-to-all-start.3 = ((f32[16,40,128]{2,1,0:T(8,128)}), f32[16,40,128]{2,1,0:T(8,128)S(1)}, u32[]{:S(2)}, u32[]{:S(2)}) async-start(f32[16,40,128]{2,1,0:T(8,128)} %bitcast.7), calls=%async_computation.3 | async-start | bytes 655360 | tf_op jit(solution)/shard_map/all_to_all | solution.py:739

commit v4 on v3

--- a/solution.py
+++ b/solution.py
@@ -43,8 +43,9 @@
 
 
 def y_table(ny):
-    cos, sin = phases(np.arange(ny), signed(KY), ny)
-    return np.concatenate([cos.T, -sin.T], axis=0)
+    cos, sin = phases(np.arange(ny), np.arange(MODES + 1), ny)
+    order = [MODES] + list(range(1, MODES))
+    return np.concatenate([cos.T[:MODES], -sin.T[order], cos.T[MODES:], np.zeros((7, ny))], axis=0)
 
 
 def z_table(nz, scale, factor):
@@ -106,51 +107,79 @@
     return (ky // ky_own) * stride + (plane * ky_own + ky % ky_own) * 8
 
 
+COS16 = MODES * 32
+SINES = COS16 + 128
+SLOTS = SINES + MODES * 32
+
+
 def forward_pair(c, channels, pair, fy_ref, scratch):
     nz = scratch.shape[1]
-    size = KY * channels
     high, low = split(pair)
     both = dot(fy_ref[...], jnp.concatenate([high, low], axis=0))
-    half = both[: 2 * KY] + both[2 * KY :]
+    half = both[: 2 * MODES + 8] + both[2 * MODES + 8 :]
     for e in range(2):
-        for part in range(2):
-            scratch[pl.ds(part * size + c + e, KY, stride=channels), :] = half[
-                part * KY : (part + 1) * KY, e * nz : (e + 1) * nz
-            ]
+        side = slice(e * nz, (e + 1) * nz)
+        scratch[pl.ds(c + e, MODES, stride=channels), :] = half[:MODES, side]
+        scratch[pl.ds(SINES + c + e, MODES, stride=channels), :] = half[MODES : 2 * MODES, side]
+        scratch[pl.ds(COS16 + c + e, 1), :] = half[2 * MODES : 2 * MODES + 1, side]
 
 
 def forward_finish(channels, tz_ref, scratch, out_ref, row_of):
-    size = KY * channels
-    high, low = split(jnp.concatenate([scratch[:size], scratch[size:]], axis=1))
-    first = dot(tz_ref[...], high, NT)
-    rows = first[: 2 * MODES] + first[2 * MODES :] + dot(tz_ref[: 2 * MODES, :], low, NT)
-    for q in range(KY // 4):
-        tiles = [rows[8 * j : 8 * j + 8, q * 128 : (q + 1) * 128] for j in range(4)]
-        for e, tile in enumerate(group_transpose(tiles)):
-            out_ref[pl.ds(row_of(4 * q + e), 8), :] = tile
+    count = 2 * MODES
+    sides = []
+    for part, rows in ((0, slice(0, SINES)), (1, slice(SINES, SLOTS))):
+        both = dot(tz_ref[2 * part * count : 2 * (part + 1) * count, :], jnp.concatenate(split(scratch[rows, :]), axis=1), NT)
+        sides.append(both[:count] + both[count:])
+    first = lax.broadcasted_iota(jnp.int32, (8, 128), 1) < 32
+    for q in range(MODES // 4):
+        tiles = ([], [])
+        for j in range(4):
+            rows, cols = slice(8 * j, 8 * j + 8), slice(q * 128, (q + 1) * 128)
+            even, odd = sides[0][rows, cols], sides[1][rows, cols]
+            last = sides[0][rows, COS16 : COS16 + 128]
+            tiles[0].append(jnp.where(first, even, even + odd) if q == 0 else even + odd)
+            tiles[1].append((jnp.where(first, last, even) if q == 0 else even) - odd)
+        for sign in range(2):
+            for e, tile in enumerate(group_transpose(tiles[sign])):
+                k = 4 * q + e
+                ky = k if sign == 0 else (KY - k if k else MODES)
+                out_ref[pl.ds(row_of(ky), 8), :] = tile
 
 
 def inverse_plane(in_ref, row_of, tz_ref, ty_ref, scratch, channels, emit, after, before=lambda h: None):
     nz = scratch.shape[1]
-    size = KY * channels
-    columns = [[] for _ in range(4)]
-    for q in range(KY // 4):
-        tiles = [in_ref[pl.ds(row_of(4 * q + e), 8), :] for e in range(4)]
-        for j, tile in enumerate(group_transpose(tiles)):
-            columns[j].append(tile)
-    rows = jnp.concatenate([jnp.concatenate(c, axis=1) for c in columns], axis=0)
-    modes = dot(data3(rows), tz_ref[...], TN)
-    for part in range(2):
-        scratch[part * size : (part + 1) * size, :] = modes[:, part * nz : (part + 1) * nz]
+    tile = lambda ky: in_ref[pl.ds(row_of(ky), 8), :]
+    columns = ([[] for _ in range(4)], [[] for _ in range(4)])
+    for q in range(MODES // 4):
+        sums, differences = [], []
+        for k in range(4 * q, 4 * q + 4):
+            sums.append(tile(k) + tile(KY - k) if k else tile(0))
+            differences.append(tile(k) - tile(KY - k) if k else -tile(MODES))
+        for sign, tiles in ((0, sums), (1, differences)):
+            for j, found in enumerate(group_transpose(tiles)):
+                columns[sign][j].append(found)
+    for j, found in enumerate(group_transpose([tile(MODES)] * 4)):
+        columns[0][j].append(found)
+    depth = tz_ref.shape[0] // 2
+    for sign, rows in ((0, slice(0, SINES)), (1, slice(SINES, SLOTS))):
+        data = jnp.concatenate([jnp.concatenate(c, axis=1) for c in columns[sign]], axis=0)
+        scratch[rows, :] = dot(data3(data), tz_ref[sign * depth : (sign + 1) * depth, :], TN)
+    at = lax.broadcasted_iota(jnp.int32, (8, 2 * nz), 0)
+    slant = jnp.where((at == 3) | (at == 5) | (at == 4), -1.0, 1.0) * jnp.where(at % 2 == 1, math.sqrt(0.5), 1.0)
+    wave = jnp.where(at % 4 == 2, 0.0, slant)
 
     def group(h, carry):
         before(h)
         for k in range(0, 16, 2):
-            sides = []
+            c = 16 * h + k
+            sides, tops = [], []
             for e in range(2):
-                parts = [scratch[pl.ds(part * size + 16 * h + k + e, KY, stride=channels), :] for part in range(2)]
+                parts = [scratch[pl.ds(first + c + e, MODES, stride=channels), :] for first in (0, SINES)]
                 sides.append(jnp.concatenate(parts, axis=0))
-            emit(16 * h + k, dot(ty_ref[...], data3(jnp.concatenate(sides, axis=1))))
+                tops.append(scratch[pl.ds(COS16 + c + e, 1), :])
+            pair = dot(ty_ref[...], data3(jnp.concatenate(sides, axis=1)))
+            extra = wave * jnp.concatenate(tops, axis=1)
+            emit(c, pair + jnp.concatenate([extra] * (pair.shape[0] // 8), axis=0))
         after(h)
         return carry
 
@@ -695,7 +724,7 @@
     nx = slab * devices
     pair_local = spec_weight.shape[0]
     assert pair_local % MODES == 0 or slab == 1
-    assert channels == 32 and nz == 128 and pair_local % 4 == 0
+    assert channels == 32 and ny == nz == 128 and pair_local % 4 == 0
     ky_own = max(1, pair_local // MODES)
     lines = pair_local // 2
     rows = nx * lines
@@ -706,16 +735,22 @@
     fwd_scale = float(nx * ny * nz) ** (-0.5)
     inv_scale = float(4 * MODES**3) ** (-0.5)
 
-    fy_high, fy_low = halves(y_table(ny))
-    fy = np.concatenate(
-        [np.concatenate([fy_high, fy_high], axis=1), np.concatenate([fy_low, fy_low], axis=1)], axis=0
-    )
-    fy = jnp.asarray(fy)
-    tz_first = jnp.asarray(np.concatenate(halves(z_table(nz, 1.0, 1.0)), axis=0))
-    ty = jnp.asarray(stack3(y_table(ny).T, 1))
-    tz_grad = jnp.asarray(np.concatenate(halves(z_table(nz, inv_scale, 2.0)), axis=0))
-    tzi_out = jnp.asarray(stack3(z_table(nz, inv_scale, 2.0), 0))
-    tzi_grad = jnp.asarray(stack3(z_table(nz, fwd_scale, 1.0), 0))
+    def twice(table):
+        high, low = halves(table)
+        return np.concatenate([np.tile(high, (1, 2)), np.tile(low, (1, 2))], axis=0)
+
+    def forward_z(table):
+        return jnp.asarray(np.concatenate([twice(table[:, :nz]), twice(table[:, nz:])], axis=0))
+
+    def inverse_z(table):
+        return jnp.asarray(np.concatenate([stack3(table[:, :nz], 0), stack3(table[:, nz:], 0)], axis=0))
+
+    fy = jnp.asarray(twice(y_table(ny)))
+    ty = jnp.asarray(stack3(y_table(ny)[: 2 * MODES].T, 1))
+    tz_first = forward_z(z_table(nz, 1.0, 1.0))
+    tz_grad = forward_z(z_table(nz, inv_scale, 2.0))
+    tzi_out = inverse_z(z_table(nz, inv_scale, 2.0))
+    tzi_grad = inverse_z(z_table(nz, fwd_scale, 1.0))
     fx = x_forward_table(nx, fwd_scale)
     fx_wide = jnp.asarray(np.repeat(stack3(fx, 0), channels, axis=1))
     gx = jnp.asarray(stack3(by_low(x_forward_table(nx, 1.0), 1).T, 1))
@@ -727,7 +762,7 @@
 
     line_shape = jax.ShapeDtypeStruct((rows, 128), f32)
     field_shape = pltpu.HBM(flow_field.shape, f32)
-    mode_scratch = pltpu.VMEM((2 * KY * channels, nz), f32)
+    mode_scratch = pltpu.VMEM((SLOTS, nz), f32)
     kron_scratch = pltpu.VMEM((16 * channels, 8 * channels), bf16)
     chunk_count = slab * (channels // 8)
     chunk_sems = pltpu.SemaphoreType.DMA((chunk_count,))

time: 92.4 us -> 89.5 us (0.969)
  Pallas kernels: 53.8 us -> 50.9 us
    pallas_call x1, Pallas kernels: 8.75 us -> 7.44 us  [per_device(): pl.pallas_call(functools.partial(middle_kernel, stride, ky_own), in_specs...]
    pallas_call x1, Pallas kernels: 6.76 us -> 5.8 us  [per_device(): pl.pallas_call(functools.partial(last_kernel, stride_in, ky_own, devices,...]
  transfers between devices with their start and end apart: 3 -> 3, of which waited for: 3 -> 3; matrix products, arithmetic and copies ran while one was open for 0% -> 0% of each run, Pallas kernels for 23% -> 24%
where the time goes in v4:
time: 89.5 us; the launch traced here: 89.1 us
  Pallas kernels  50.9 us (57%)
  starting transfers between devices  14.7 us (16%)
  blocking collectives  12.8 us (14%)
  waiting for transfers between devices  9.71 us (11%)
  between operations  0.96 us (1%)
    all_to_all x3, starting transfers between devices, exchange(): lax.all_to_all(blocks, 'space', split_axis=0, concat_axis=0, tiled=True)  14.7 us
    all_to_all x1, blocking collectives, exchange(): lax.all_to_all(blocks, 'space', split_axis=0, concat_axis=0, tiled=True)  12.8 us
    all_to_all x3, waiting for transfers between devices, exchange(): lax.all_to_all(blocks, 'space', split_axis=0, concat_axis=0, tiled=True)  9.71 us
    pallas_call x1, Pallas kernels, per_device(): pl.pallas_call(functools.partial(middle_kernel, stride, ky_own), in_specs...  7.44 us
    pallas_call x1, Pallas kernels, per_device(): pl.pallas_call(functools.partial(adjoint_kernel, slab, nx, lines, extra),...  6.02 us
    pallas_call x1, Pallas kernels, per_device(): pl.pallas_call(functools.partial(last_kernel, stride_in, ky_own, devices,...  5.8 us
    pallas_call x1, Pallas kernels, per_device(): pl.pallas_call(functools.partial(weight_grad_kernel, nx, lines), in_specs...  5.57 us
    pallas_call x1, Pallas kernels, per_device(): pl.pallas_call(point_kernel, in_specs=[HBM, VM, VM], out_specs=HBM, out_s...  5.55 us
  transfers between devices with their start and end apart: 3, of which 3 were waited for; matrix products, arithmetic and copies ran while one was open for 0% of the time, Pallas kernels for 24%

profile of v4, /device:TPU:0, one launch (start us, length us, event | category | flops | bytes accessed | tf_op | source)
XLA Modules:
  0.0 89.1 jit_solution(4020426597868614468)
XLA Ops:
  0.6 0.0 copy-start.5
  0.6 0.0 copy-start.7
  0.7 5.2 %field_forward.1 = f32[512,128]{1,0:T(8,128)} custom-call(f32[2,32,128,128]{3,2,1,0:T(8,128)} %field_hbm.5, bf16[80,256]{1,0:T(8,128)(2,1)} %constant.20.clone.fy_hbm.fy_ref, bf16[128,256]{1,0:T(8,128)(2,1)} %constant.22.clone.tz_hbm), custom_call_target="tpu_custom_call" | custom-call | bytes 12000000 | tf_op jit(solution)/shard_map/field_forward/pallas_call | solution.py:776
  5.9 7.4 %all-to-all-start = ((f32[16,32,128]{2,1,0:T(8,128)}), f32[16,32,128]{2,1,0:T(8,128)S(1)}, u32[]{:S(2)}, u32[]{:S(2)}) async-start(f32[16,32,128]{2,1,0:T(8,128)} %bitcast), calls=%async_computation | async-start | bytes 524288 | tf_op jit(solution)/shard_map/all_to_all | solution.py:774
  13.2 0.0 copy-done.5
  13.2 0.0 copy-done.7
  13.3 5.6 %pointwise.1.point_ref = f32[2,32,128,128]{3,2,1,0:T(8,128)} custom-call(f32[2,32,128,128]{3,2,1,0:T(8,128)} %field_hbm.5, f32[32,32]{1,0:T(8,128)S(1)} %copy-done.5, f32[1,32]{1,0:T(1,128)S(1)} %bitcast.18), custom_call_target="tpu_custom_call" | custom-call | bytes 18000000 | tf_op jit(solution)/shard_map/pointwise/pallas_call | solution.py:796
  18.8 4.5 %all-to-all-done = f32[16,32,128]{2,1,0:T(8,128)S(1)} async-done(((f32[16,32,128]{2,1,0:T(8,128)}), f32[16,32,128]{2,1,0:T(8,128)S(1)}, u32[]{:S(2)}, u32[]{:S(2)}) %all-to-all-start) | async-done | bytes 262176 | tf_op jit(solution)/shard_map/all_to_all | solution.py:774
  23.3 0.0 copy-start
  23.3 0.0 copy-start.1
  23.3 0.0 copy-start.2
  23.3 0.0 copy-start.3
  23.3 0.0 copy-start.4
  23.3 0.0 copy-start.6
  23.3 5.3 %mode_mix.1 = f32[512,128]{1,0:T(8,128)S(1)} custom-call(f32[512,128]{1,0:T(8,128)S(1)} %bitcast.12, f32[32,2,32,1024]{3,2,1,0:T(8,128)} %weight_hbm.3, bf16[192,2048]{1,0:T(8,128)(2,1)} %constant.26.clone.fx_hbm, bf16[64,192]{1,0:T(8,128)(2,1)} %constant.28.clone.inv_hbm), custom_call_target="tpu_custom_call" | custom-call | bytes 15000000 | tf_op jit(solution)/shard_map/mode_mix/pallas_call | solution.py:814
  28.6 12.8 %all_to_all.20 = f32[16,32,128]{2,1,0:T(8,128)S(1)} all-to-all(f32[16,32,128]{2,1,0:T(8,128)S(1)} %bitcast.17), channel_id=1, replica_groups=mesh['group'=2,'space'=16] {'space'}, dimensions={0} | all-to-all | bytes 524288 | tf_op jit(solution)/shard_map/all_to_all | solution.py:774
  41.4 0.0 copy-done
  41.4 0.0 copy-done.1
  41.4 0.0 copy-done.2
  41.4 0.0 copy-done.3
  41.4 0.0 copy-done.4
  41.5 0.0 copy-done.6
  41.5 7.4 %middle.1 = (f32[2,32,128,128]{3,2,1,0:T(8,128)}, f32[2,32,128,128]{3,2,1,0:T(8,128)}, f32[512,128]{1,0:T(8,128)}) custom-call(f32[512,128]{1,0:T(8,128)S(1)} %bitcast.16, f32[2,32,128,128]{3,2,1,0:T(8,128)S(1)} %copy-done, f32[2,32,128,128]{3,2,1,0:T(8,128)S(1)} %copy-done.1, bf16[192,128]{1,0:T(8,128)(2,1)S(1)} %copy-done.6, ...), custom_call_target="tpu_custom_call" | custom-call | bytes 30000000 | tf_op jit(solution)/shard_map/middle/pallas_call | solution.py:834
  48.9 3.5 %all-to-all-start.2 = ((f32[16,32,128]{2,1,0:T(8,128)}), f32[16,32,128]{2,1,0:T(8,128)S(1)}, u32[]{:S(2)}, u32[]{:S(2)}) async-start(f32[16,32,128]{2,1,0:T(8,128)} %bitcast.5), calls=%async_computation.2 | async-start | bytes 524288 | tf_op jit(solution)/shard_map/all_to_all | solution.py:774
  52.5 5.0 %outer_sums.1.sums_ref = f32[8,128]{1,0:T(8,128)S(1)} custom-call(f32[2,32,128,128]{3,2,1,0:T(8,128)} %field_hbm.5, f32[2,32,128,128]{3,2,1,0:T(8,128)} %get-tuple-element.21.gpre_hbm), custom_call_target="tpu_custom_call" | custom-call | bytes 18000000 | tf_op jit(solution)/shard_map/outer_sums/pallas_call | solution.py:851
  57.5 5.0 %all-to-all-done.2 = f32[16,32,128]{2,1,0:T(8,128)S(1)} async-done(((f32[16,32,128]{2,1,0:T(8,128)}), f32[16,32,128]{2,1,0:T(8,128)S(1)}, u32[]{:S(2)}, u32[]{:S(2)}) %all-to-all-start.2) | async-done | bytes 262176 | tf_op jit(solution)/shard_map/all_to_all | solution.py:774
  62.5 6.0 %mode_adjoint.1 = f32[640,128]{1,0:T(8,128)} custom-call(f32[512,128]{1,0:T(8,128)S(1)} %bitcast.14, f32[32,2,32,1024]{3,2,1,0:T(8,128)} %weight_hbm.3, bf16[64,192]{1,0:T(8,128)(2,1)} %constant.27.clone.gx_hbm, bf16[1024,128]{1,0:T(8,128)(2,1)} %constant.29.clone.inv_hbm, f32[8,128]{1,0:T(8,128)S(1)} %outer_sums.1.sums_ref), custom_call_target="tpu_custom_call" | custom-call | bytes 18000000 | tf_op jit(solution)/shard_map/mode_adjoint/pallas_call | solution.py:869
  68.5 3.7 %all-to-all-start.3 = ((f32[16,40,128]{2,1,0:T(8,128)}), f32[16,40,128]{2,1,0:T(8,128)S(1)}, u32[]{:S(2)}, u32[]{:S(2)}) async-start(f32[16,40,128]{2,1,0:T(8,128)} %bitcast.7), calls=%async_computation.3 | async-start | bytes 655360 | tf_op jit(solution)/shard_map/all_to_all | solution.py:774
  72.2 5.6 %weight_grad.1 = f32[32,2,32,1024]{3,2,1,0:T(8,128)} custom-call(f32[512,128]{1,0:T(8,128)S(1)} %bitcast.13, f32[512,128]{1,0:T(8,128)S(1)} %bitcast.15, bf16[192,2048]{1,0:T(8,128)(2,1)} %constant.26.clone.fx_hbm, bf16[64,192]{1,0:T(8,128)(2,1)} %constant.27.clone.gx_hbm), custom_call_target="tpu_custom_call" | custom-call | bytes 18000000 | tf_op jit(solution)/shard_map/weight_grad/pallas_call | solution.py:888
  77.8 5.0 %pointwise_back.1.back_hbm = f32[2,32,128,128]{3,2,1,0:T(8,128)} custom-call(f32[2,32,128,128]{3,2,1,0:T(8,128)} %get-tuple-element.21.gpre_hbm, f32[32,32]{1,0:T(8,128)S(1)} %copy-done.5), custom_call_target="tpu_custom_call" | custom-call | bytes 18000000 | tf_op jit(solution)/shard_map/pointwise_back/pallas_call | solution.py:910
  82.8 0.3 all-to-all-done.3
  83.1 5.8 %field_inverse.1 = (f32[2,32,128,128]{3,2,1,0:T(8,128)}, f32[32,32]{1,0:T(8,128)}, f32[1,32]{1,0:T(1,128)}) custom-call(f32[640,128]{1,0:T(8,128)S(1)} %bitcast.10, f32[640,128]{1,0:T(8,128)S(1)} %bitcast.11, f32[2,32,128,128]{3,2,1,0:T(8,128)} %pointwise_back.1.back_hbm, bf16[192,128]{1,0:T(8,128)(2,1)} %constant.25.clone.tzi_hbm, ...), custom_call_target="tpu_custom_call" | custom-call | bytes 24000000 | tf_op jit(solution)/shard_map/field_inverse/pallas_call | solution.py:928
Async XLA Ops:
  0.6 12.6 %copy-start.5 = (f32[32,32]{1,0:T(8,128)S(1)}, f32[32,32]{1,0:T(8,128)}, u32[]{:S(2)}) copy-start(f32[32,32]{1,0:T(8,128)} %weight_ref.3) | copy-start | bytes 12292
  0.6 12.6 %copy-start.7 = (f32[32]{0:T(128)S(1)}, f32[32]{0:T(128)}, u32[]{:S(2)}) copy-start(f32[32]{0:T(128)} %param.19) | copy-start | bytes 388
  5.9 17.4 %all-to-all-start = ((f32[16,32,128]{2,1,0:T(8,128)}), f32[16,32,128]{2,1,0:T(8,128)S(1)}, u32[]{:S(2)}, u32[]{:S(2)}) async-start(f32[16,32,128]{2,1,0:T(8,128)} %bitcast), calls=%async_computation | async-start | bytes 524288 | tf_op jit(solution)/shard_map/all_to_all | solution.py:774
  23.3 18.1 %copy-start = (f32[2,32,128,128]{3,2,1,0:T(8,128)S(1)}, f32[2,32,128,128]{3,2,1,0:T(8,128)}, u32[]{:S(2)}) copy-start(f32[2,32,128,128]{3,2,1,0:T(8,128)} %pointwise.1.point_ref) | copy-start | bytes 12582916
  23.3 18.1 %copy-start.1 = (f32[2,32,128,128]{3,2,1,0:T(8,128)S(1)}, f32[2,32,128,128]{3,2,1,0:T(8,128)}, u32[]{:S(2)}) copy-start(f32[2,32,128,128]{3,2,1,0:T(8,128)} %cot_ref.1) | copy-start | bytes 12582916
  23.3 18.1 %copy-start.2 = (bf16[80,256]{1,0:T(8,128)(2,1)S(1)}, bf16[80,256]{1,0:T(8,128)(2,1)}, u32[]{:S(2)}) copy-start(bf16[80,256]{1,0:T(8,128)(2,1)} %constant.20.clone.fy_hbm.fy_ref) | copy-start | bytes 122884
  23.3 18.2 %copy-start.3 = (bf16[128,96]{1,0:T(8,128)(2,1)S(1)}, bf16[128,96]{1,0:T(8,128)(2,1)}, u32[]{:S(2)}) copy-start(bf16[128,96]{1,0:T(8,128)(2,1)} %constant.21.clone.ty_ref.ty_hbm) | copy-start | bytes 73732
  23.3 18.2 %copy-start.4 = (bf16[128,256]{1,0:T(8,128)(2,1)S(1)}, bf16[128,256]{1,0:T(8,128)(2,1)}, u32[]{:S(2)}) copy-start(bf16[128,256]{1,0:T(8,128)(2,1)} %constant.23.clone.tzf_ref) | copy-start | bytes 196612
  23.3 18.2 %copy-start.6 = (bf16[192,128]{1,0:T(8,128)(2,1)S(1)}, bf16[192,128]{1,0:T(8,128)(2,1)}, u32[]{:S(2)}) copy-start(bf16[192,128]{1,0:T(8,128)(2,1)} %constant.24.clone.tzi_ref) | copy-start | bytes 147460
  48.9 13.6 %all-to-all-start.2 = ((f32[16,32,128]{2,1,0:T(8,128)}), f32[16,32,128]{2,1,0:T(8,128)S(1)}, u32[]{:S(2)}, u32[]{:S(2)}) async-start(f32[16,32,128]{2,1,0:T(8,128)} %bitcast.5), calls=%async_computation.2 | async-start | bytes 524288 | tf_op jit(solution)/shard_map/all_to_all | solution.py:774
  68.5 14.6 %all-to-all-start.3 = ((f32[16,40,128]{2,1,0:T(8,128)}), f32[16,40,128]{2,1,0:T(8,128)S(1)}, u32[]{:S(2)}, u32[]{:S(2)}) async-start(f32[16,40,128]{2,1,0:T(8,128)} %bitcast.7), calls=%async_computation.3 | async-start | bytes 655360 | tf_op jit(solution)/shard_map/all_to_all | solution.py:774

commit v5 on v4

--- a/solution.py
+++ b/solution.py
@@ -249,10 +249,10 @@
     slab, channels = field_ref.shape[:2]
     tables = transfers([(fy_hbm, fy_ref), (tz_hbm, tz_ref)], table_sems)
     parts = [(field_hbm.at[p, c], field_ref.at[p, c]) for p in range(slab) for c in chunks(channels)]
-    for copy in tables + transfers(parts, sems):
+    loads = transfers(parts, sems)
+    for copy in tables[:1] + loads[:2] + tables[1:] + loads[2:]:
         copy.start()
-    for copy in tables:
-        copy.wait()
+    tables[0].wait()
 
     def body(p, carry):
         for c in range(0, channels, 2):
@@ -262,6 +262,11 @@
                     sem = sems.at[p * (channels // 8) + g]
                     pltpu.make_async_copy(field_hbm.at[p, part], field_ref.at[p, part], sem).wait()
             forward_pair(c, channels, two(field_ref, p, c), fy_ref, scratch)
+
+        @pl.when(p == 0)
+        def _():
+            tables[1].wait()
+
         forward_finish(channels, tz_ref, scratch, out_ref, rows_at(p, stride, ky_own))
         return carry
 
@@ -324,13 +329,18 @@
     return jnp.concatenate([high, low, high], axis=1)
 
 
-def weight_loads(weight_hbm, weight_ref, table_pairs, sems):
-    parts = [slice(256 * t, 256 * t + 256) for t in range(4)]
-    pairs = table_pairs + [(weight_hbm.at[:, :, :, part], weight_ref.at[:, :, :, part]) for part in parts]
-    copies = transfers(pairs, sems)
-    for copy in copies:
+def weight_part(ref, t, h):
+    half = ref.shape[0] // 2
+    start = 256 * t if isinstance(t, int) else pl.multiple_of(256 * t, 256)
+    return ref.at[half * h : half * (h + 1), :, :, pl.ds(start, 256)]
+
+
+def weight_loads(weight_hbm, weight_ref, tables, sems):
+    parts = [(weight_part(weight_hbm, t, h), weight_part(weight_ref, t, h)) for t in range(4) for h in range(2)]
+    copies = transfers(tables + parts, sems)
+    for copy in copies[:1] + copies[2:3] + copies[1:2] + copies[3:]:
         copy.start()
-    return copies[: len(table_pairs)], copies[len(table_pairs) :]
+    return copies[:2], copies[2:]
 
 
 def mix_kernel(
@@ -341,14 +351,12 @@
     tables, loads = weight_loads(weight_hbm, weight_ref, [(fx_hbm, fx_ref), (inv_hbm, inv_ref)], sems)
     for u in range(pairs // 4):
         left[128 * u : 128 * u + 128, :] = data_rows(in_ref, nx, lines, u)
-    for copy in tables:
-        copy.wait()
+    tables[0].wait()
     for t in range(4):
         cols = slice(256 * t, 256 * t + 256)
         late = slice(wide + 256 * t, wide + 256 * t + 256)
         modes[:, :256] = dot(left[...], fx_ref[:, cols])
         modes[:, 256:] = dot(left[...], fx_ref[:, late])
-        loads[t].wait()
 
         def body(pair, carry):
             rows = pl.ds(pl.multiple_of(32 * pair, 32), 32)
@@ -362,7 +370,10 @@
                     sums[pl.ds(base, 8), :] = total[:, 128 * e : 128 * e + 128]
             return carry
 
-        lax.fori_loop(0, pairs, body, 0, unroll=4)
+        for h in range(2):
+            loads[2 * t + h].wait()
+            lax.fori_loop(h * (pairs // 2), (h + 1) * (pairs // 2), body, 0, unroll=min(4, pairs // 2))
+    tables[1].wait()
     for u in range(pairs // 4):
         tiles = [[], []]
         for j in range(4):
@@ -460,13 +471,17 @@
     devices = nx // slab
     stride = slab * lines + extra
     tables, loads = weight_loads(weight_hbm, weight_ref, [(gx_hbm, gx_ref), (inv_hbm, inv_ref)], sems)
-    for copy in tables:
-        copy.wait()
+    tables[0].wait()
     bias = gradient_rows(grad_ref, gx_ref, nx, lines, pairs // 4, rows_ref)
     total[...] = jnp.zeros_like(total)
     late[...] = jnp.zeros_like(late)
+    tables[1].wait()
     early = lax.broadcasted_iota(jnp.int32, (32, 128), 1) % 32 < 16
     count = pairs // 2
+
+    def arrive(t, h):
+        ends = (weight_part(weight_hbm, t, h), weight_part(weight_ref, t, h))
+        pltpu.make_async_copy(*ends, sems.at[2 + 2 * t + h]).wait()
 
     def products(t, first, target):
         for k in range(count):
@@ -491,12 +506,10 @@
         total[rows, :] += dot(source[:, :256], table) + dot(source[:, 256:], table)
 
     def body(t, carry):
-        part = pl.ds(pl.multiple_of(256 * t, 256), 256)
-        pltpu.make_async_copy(
-            weight_hbm.at[:, :, :, part], weight_ref.at[:, :, :, part], sems.at[len(tables) + t]
-        ).wait()
+        arrive(t, 0)
         gather(jnp.maximum(t - 1, 0), late, count)
         products(t, 0, soon)
+        arrive(t, 1)
         gather(t, soon, 0)
         products(t, count, late)
         return carry
@@ -572,7 +585,7 @@
             forward_pair(2 * k, channels, two(gpre_ref, p, 2 * k), fy_ref, scratch)
             return carry
 
-        lax.fori_loop(0, channels // 2, pair, 0, unroll=8)
+        lax.fori_loop(0, channels // 2, pair, 0, unroll=16)
         forward_finish(channels, tzf_ref, scratch, spec_ref, row_of)
         return carry
 
@@ -583,19 +596,18 @@
                 copy.wait()
 
 
-def back_kernel(gpre_hbm, weight_ref, out_hbm, cells_ref, kron, in_sems, out_sems):
-    prepare = lambda: spread_weight(weight_ref[...], kron)
-    mix_field(gpre_hbm, out_hbm, cells_ref, kron, None, in_sems, out_sems, prepare)
-
-
-def outer_kernel(field_hbm, gpre_hbm, sums_ref, field_ref, gpre_ref, outer, field_sems, gpre_sems):
+def outer_kernel(
+    field_hbm, gpre_hbm, weight_ref, sums_ref, back_hbm, field_ref, gpre_ref, kron, outer, field_sems, gpre_sems, out_sems
+):
     channels = field_ref.shape[1]
     load, count = cell_copies(field_hbm, field_ref, field_sems)
     load_gpre, _ = cell_copies(gpre_hbm, gpre_ref, gpre_sems)
+    store, _ = cell_copies(back_hbm, gpre_ref, out_sems, True)
     for n in range(count):
         load(n).start()
         load_gpre(n).start()
     outer[...] = jnp.zeros_like(outer)
+    spread_weight(weight_ref[...], kron)
     cuts = field_ref.shape[2] // 32
 
     def body(n, carry):
@@ -608,10 +620,14 @@
             g_high, g_low = split(cell_tile(gpre_ref, n // cuts, start))
             both = dot(jnp.concatenate([high, low], axis=0), g_high, NT)
             total = total + (both[: 8 * channels] + both[8 * channels :] + dot(high, g_low, NT))
+            put_tile(gpre_ref, n // cuts, start, mix_cells(kron, g_high, g_low))
         outer[...] = total
+        store(n).start()
         return carry
 
     lax.fori_loop(0, count, body, 0)
+    for n in range(count):
+        store(n).wait()
     row = lax.broadcasted_iota(jnp.int32, outer.shape, 0) % 8
     column = lax.broadcasted_iota(jnp.int32, outer.shape, 1) % 8
     kept = jnp.where(row == column, outer[...], 0.0)
@@ -823,7 +839,7 @@
             pltpu.VMEM((32 * pair_local, 6 * nx), bf16),
             pltpu.VMEM((32 * pair_local, 512), f32),
             pltpu.VMEM((128 * pair_local, 128), f32),
-            pltpu.SemaphoreType.DMA((6,)),
+            pltpu.SemaphoreType.DMA((10,)),
         ],
         compiler_params=params(24),
         cost_estimate=cost(5),
@@ -848,22 +864,24 @@
     )(mixed, near(pointwise), near(cotangent), near(tzi_out), near(ty), near(fy), near(tz_grad))
     grad_x = exchange(grad_lines).reshape(rows, 128)
 
-    local_sums = pl.pallas_call(
+    local_sums, back = pl.pallas_call(
         outer_kernel,
-        in_specs=[HBM, HBM],
-        out_specs=VM,
-        out_shape=jax.ShapeDtypeStruct((extra, 128), f32),
+        in_specs=[HBM, HBM, VM],
+        out_specs=[VM, HBM],
+        out_shape=[jax.ShapeDtypeStruct((extra, 128), f32), field_shape],
         scratch_shapes=[
             keep(flow_field),
             keep(flow_field),
+            kron_scratch,
             pltpu.VMEM((8 * channels, 8 * channels), f32),
+            cell_sems,
             cell_sems,
             cell_sems,
         ],
         compiler_params=params(16),
-        cost_estimate=cost(6),
-        name="outer_sums",
-    )(far(flow_field), far(gpre))
+        cost_estimate=cost(8),
+        name="outer_and_back",
+    )(far(flow_field), far(gpre), point_weight)
 
     sent = devices * (block + extra)
     grad_mixed = pl.pallas_call(
@@ -879,7 +897,7 @@
             pltpu.VMEM((16 * pair_local, 512), bf16),
             pltpu.VMEM((16 * pair_local, 512), bf16),
             pltpu.VMEM((32 * pair_local, 4 * nx), f32),
-            pltpu.SemaphoreType.DMA((6,)),
+            pltpu.SemaphoreType.DMA((10,)),
         ],
         compiler_params=params(24),
         cost_estimate=cost(6),
@@ -905,18 +923,7 @@
         name="weight_grad",
     )(spec_x, grad_x, far(fx_wide), far(gx))
 
-    gpre, grad_mixed = lax.optimization_barrier((gpre, grad_mixed))
     received = exchange(grad_mixed)
-    back = pl.pallas_call(
-        back_kernel,
-        in_specs=[HBM, VM],
-        out_specs=HBM,
-        out_shape=field_shape,
-        scratch_shapes=[keep(flow_field), kron_scratch, cell_sems, cell_sems],
-        compiler_params=params(16),
-        cost_estimate=cost(6),
-        name="pointwise_back",
-    )(far(gpre), point_weight)
 
     if pair_local >= MODES:
         lines_in = sums_in = received.reshape(sent, 128)

time: 89.5 us -> 89.1 us (level)
  Pallas kernels: 50.9 us -> 47.7 us
  waiting for transfers between devices: 9.71 us -> 12.4 us
    all_to_all x3, waiting for transfers between devices: 9.71 us -> 12.4 us  [exchange(): lax.all_to_all(blocks, 'space', split_axis=0, concat_axis=0, tiled=True)]
    pallas_call x2 -> x1, Pallas kernels: 10 us -> 7.41 us  [per_device(): pl.pallas_call(outer_kernel, in_specs=[HBM, HBM, VM], out_specs=[VM, HBM]...]
  transfers between devices with their start and end apart: 3 -> 3, of which waited for: 3 -> 3; matrix products, arithmetic and copies ran while one was open for 0% -> 0% of each run, Pallas kernels for 24% -> 21%
where the time goes in v5:
time: 89.1 us; the launch traced here: 88.6 us
  Pallas kernels  47.7 us (54%)
  starting transfers between devices  14.6 us (16%)
  blocking collectives  12.9 us (14%)
  waiting for transfers between devices  12.4 us (14%)
  between operations  0.95 us (1%)
    all_to_all x3, starting transfers between devices, exchange(): lax.all_to_all(blocks, 'space', split_axis=0, concat_axis=0, tiled=True)  14.6 us
    all_to_all x1, blocking collectives, exchange(): lax.all_to_all(blocks, 'space', split_axis=0, concat_axis=0, tiled=True)  12.9 us
    all_to_all x3, waiting for transfers between devices, exchange(): lax.all_to_all(blocks, 'space', split_axis=0, concat_axis=0, tiled=True)  12.4 us
    pallas_call x1, Pallas kernels, per_device(): pl.pallas_call(outer_kernel, in_specs=[HBM, HBM, VM], out_specs=[VM, HBM]...  7.41 us
    pallas_call x1, Pallas kernels, per_device(): pl.pallas_call(functools.partial(middle_kernel, stride, ky_own), in_specs...  7.32 us
    pallas_call x1, Pallas kernels, per_device(): pl.pallas_call(functools.partial(adjoint_kernel, slab, nx, lines, extra),...  5.94 us
    pallas_call x1, Pallas kernels, per_device(): pl.pallas_call(functools.partial(last_kernel, stride_in, ky_own, devices,...  5.8 us
    pallas_call x1, Pallas kernels, per_device(): pl.pallas_call(functools.partial(weight_grad_kernel, nx, lines), in_specs...  5.57 us
  transfers between devices with their start and end apart: 3, of which 3 were waited for; matrix products, arithmetic and copies ran while one was open for 0% of the time, Pallas kernels for 21%

profile of v5, /device:TPU:0, one launch (start us, length us, event | category | flops | bytes accessed | tf_op | source)
XLA Modules:
  0.0 88.6 jit_solution(2590973110603321110)
XLA Ops:
  0.6 0.0 copy-start.5
  0.6 0.0 copy-start.7
  0.7 5.0 %field_forward.1 = f32[512,128]{1,0:T(8,128)} custom-call(f32[2,32,128,128]{3,2,1,0:T(8,128)} %field_hbm.5, bf16[80,256]{1,0:T(8,128)(2,1)} %constant.20.clone.fy_hbm.fy_ref, bf16[128,256]{1,0:T(8,128)(2,1)} %constant.22.clone.tz_hbm), custom_call_target="tpu_custom_call" | custom-call | bytes 12000000 | tf_op jit(solution)/shard_map/field_forward/pallas_call | solution.py:792
  5.7 7.4 %all-to-all-start = ((f32[16,32,128]{2,1,0:T(8,128)}), f32[16,32,128]{2,1,0:T(8,128)S(1)}, u32[]{:S(2)}, u32[]{:S(2)}) async-start(f32[16,32,128]{2,1,0:T(8,128)} %bitcast), calls=%async_computation | async-start | bytes 524288 | tf_op jit(solution)/shard_map/all_to_all | solution.py:790
  13.0 0.0 copy-done.5
  13.0 0.0 copy-done.7
  13.0 5.6 %pointwise.1.point_ref = f32[2,32,128,128]{3,2,1,0:T(8,128)} custom-call(f32[2,32,128,128]{3,2,1,0:T(8,128)} %field_hbm.5, f32[32,32]{1,0:T(8,128)S(1)} %copy-done.5, f32[1,32]{1,0:T(1,128)S(1)} %bitcast.18), custom_call_target="tpu_custom_call" | custom-call | bytes 18000000 | tf_op jit(solution)/shard_map/pointwise/pallas_call | solution.py:812
  18.6 4.5 %all-to-all-done = f32[16,32,128]{2,1,0:T(8,128)S(1)} async-done(((f32[16,32,128]{2,1,0:T(8,128)}), f32[16,32,128]{2,1,0:T(8,128)S(1)}, u32[]{:S(2)}, u32[]{:S(2)}) %all-to-all-start) | async-done | bytes 262176 | tf_op jit(solution)/shard_map/all_to_all | solution.py:790
  23.1 0.0 copy-start
  23.1 0.0 copy-start.1
  23.1 0.0 copy-start.2
  23.1 0.0 copy-start.3
  23.1 0.0 copy-start.4
  23.1 0.0 copy-start.6
  23.1 5.1 %mode_mix.1 = f32[512,128]{1,0:T(8,128)S(1)} custom-call(f32[512,128]{1,0:T(8,128)S(1)} %bitcast.12, f32[32,2,32,1024]{3,2,1,0:T(8,128)} %weight_hbm.3, bf16[192,2048]{1,0:T(8,128)(2,1)} %constant.26.clone.fx_hbm, bf16[64,192]{1,0:T(8,128)(2,1)} %constant.28.clone.inv_hbm), custom_call_target="tpu_custom_call" | custom-call | bytes 15000000 | tf_op jit(solution)/shard_map/mode_mix/pallas_call | solution.py:830
  28.2 12.9 %all_to_all.20 = f32[16,32,128]{2,1,0:T(8,128)S(1)} all-to-all(f32[16,32,128]{2,1,0:T(8,128)S(1)} %bitcast.17), channel_id=1, replica_groups=mesh['group'=2,'space'=16] {'space'}, dimensions={0} | all-to-all | bytes 524288 | tf_op jit(solution)/shard_map/all_to_all | solution.py:790
  41.2 0.0 copy-done
  41.2 0.0 copy-done.1
  41.2 0.0 copy-done.2
  41.2 0.0 copy-done.3
  41.2 0.0 copy-done.4
  41.2 0.0 copy-done.6
  41.2 7.3 %middle.1 = (f32[2,32,128,128]{3,2,1,0:T(8,128)}, f32[2,32,128,128]{3,2,1,0:T(8,128)}, f32[512,128]{1,0:T(8,128)}) custom-call(f32[512,128]{1,0:T(8,128)S(1)} %bitcast.16, f32[2,32,128,128]{3,2,1,0:T(8,128)S(1)} %copy-done, f32[2,32,128,128]{3,2,1,0:T(8,128)S(1)} %copy-done.1, bf16[192,128]{1,0:T(8,128)(2,1)S(1)} %copy-done.6, ...), custom_call_target="tpu_custom_call" | custom-call | bytes 30000000 | tf_op jit(solution)/shard_map/middle/pallas_call | solution.py:850
  48.5 3.5 %all-to-all-start.2 = ((f32[16,32,128]{2,1,0:T(8,128)}), f32[16,32,128]{2,1,0:T(8,128)S(1)}, u32[]{:S(2)}, u32[]{:S(2)}) async-start(f32[16,32,128]{2,1,0:T(8,128)} %bitcast.5), calls=%async_computation.2 | async-start | bytes 524288 | tf_op jit(solution)/shard_map/all_to_all | solution.py:790
  52.1 7.4 %outer_and_back.1 = (f32[8,128]{1,0:T(8,128)S(1)}, f32[2,32,128,128]{3,2,1,0:T(8,128)}) custom-call(f32[2,32,128,128]{3,2,1,0:T(8,128)} %field_hbm.5, f32[2,32,128,128]{3,2,1,0:T(8,128)} %get-tuple-element.19.gpre_hbm, f32[32,32]{1,0:T(8,128)S(1)} %copy-done.5), custom_call_target="tpu_custom_call" | custom-call | bytes 24000000 | tf_op jit(solution)/shard_map/outer_and_back/pallas_call | solution.py:867
  59.5 2.6 %all-to-all-done.2 = f32[16,32,128]{2,1,0:T(8,128)S(1)} async-done(((f32[16,32,128]{2,1,0:T(8,128)}), f32[16,32,128]{2,1,0:T(8,128)S(1)}, u32[]{:S(2)}, u32[]{:S(2)}) %all-to-all-start.2) | async-done | bytes 262176 | tf_op jit(solution)/shard_map/all_to_all | solution.py:790
  62.1 5.9 %mode_adjoint.1 = f32[640,128]{1,0:T(8,128)} custom-call(f32[512,128]{1,0:T(8,128)S(1)} %bitcast.14, f32[32,2,32,1024]{3,2,1,0:T(8,128)} %weight_hbm.3, bf16[64,192]{1,0:T(8,128)(2,1)} %constant.27.clone.gx_hbm, bf16[1024,128]{1,0:T(8,128)(2,1)} %constant.29.clone.inv_hbm, f32[8,128]{1,0:T(8,128)S(1)} %get-tuple-element.20.sums_ref), custom_call_target="tpu_custom_call" | custom-call | bytes 18000000 | tf_op jit(solution)/shard_map/mode_adjoint/pallas_call | solution.py:887
  68.1 3.7 %all-to-all-start.3 = ((f32[16,40,128]{2,1,0:T(8,128)}), f32[16,40,128]{2,1,0:T(8,128)S(1)}, u32[]{:S(2)}, u32[]{:S(2)}) async-start(f32[16,40,128]{2,1,0:T(8,128)} %bitcast.7), calls=%async_computation.3 | async-start | bytes 655360 | tf_op jit(solution)/shard_map/all_to_all | solution.py:790
  71.8 5.6 %weight_grad.1 = f32[32,2,32,1024]{3,2,1,0:T(8,128)} custom-call(f32[512,128]{1,0:T(8,128)S(1)} %bitcast.13, f32[512,128]{1,0:T(8,128)S(1)} %bitcast.15, bf16[192,2048]{1,0:T(8,128)(2,1)} %constant.26.clone.fx_hbm, bf16[64,192]{1,0:T(8,128)(2,1)} %constant.27.clone.gx_hbm), custom_call_target="tpu_custom_call" | custom-call | bytes 18000000 | tf_op jit(solution)/shard_map/weight_grad/pallas_call | solution.py:906
  77.4 5.3 %all-to-all-done.3 = f32[16,40,128]{2,1,0:T(8,128)S(1)} async-done(((f32[16,40,128]{2,1,0:T(8,128)}), f32[16,40,128]{2,1,0:T(8,128)S(1)}, u32[]{:S(2)}, u32[]{:S(2)}) %all-to-all-start.3) | async-done | bytes 327712 | tf_op jit(solution)/shard_map/all_to_all | solution.py:790
  82.7 5.8 %field_inverse.1 = (f32[2,32,128,128]{3,2,1,0:T(8,128)}, f32[32,32]{1,0:T(8,128)}, f32[1,32]{1,0:T(1,128)}) custom-call(f32[640,128]{1,0:T(8,128)S(1)} %bitcast.10, f32[640,128]{1,0:T(8,128)S(1)} %bitcast.11, f32[2,32,128,128]{3,2,1,0:T(8,128)} %get-tuple-element.21.back_hbm, bf16[192,128]{1,0:T(8,128)(2,1)} %constant.25.clone.tzi_hbm, ...), custom_call_target="tpu_custom_call" | custom-call | bytes 24000000 | tf_op jit(solution)/shard_map/field_inverse/pallas_call | solution.py:935
Async XLA Ops:
  0.6 12.4 %copy-start.5 = (f32[32,32]{1,0:T(8,128)S(1)}, f32[32,32]{1,0:T(8,128)}, u32[]{:S(2)}) copy-start(f32[32,32]{1,0:T(8,128)} %weight_ref.3) | copy-start | bytes 12292
  0.6 12.4 %copy-start.7 = (f32[32]{0:T(128)S(1)}, f32[32]{0:T(128)}, u32[]{:S(2)}) copy-start(f32[32]{0:T(128)} %param.19) | copy-start | bytes 388
  5.7 17.4 %all-to-all-start = ((f32[16,32,128]{2,1,0:T(8,128)}), f32[16,32,128]{2,1,0:T(8,128)S(1)}, u32[]{:S(2)}, u32[]{:S(2)}) async-start(f32[16,32,128]{2,1,0:T(8,128)} %bitcast), calls=%async_computation | async-start | bytes 524288 | tf_op jit(solution)/shard_map/all_to_all | solution.py:790
  23.1 18.1 %copy-start = (f32[2,32,128,128]{3,2,1,0:T(8,128)S(1)}, f32[2,32,128,128]{3,2,1,0:T(8,128)}, u32[]{:S(2)}) copy-start(f32[2,32,128,128]{3,2,1,0:T(8,128)} %pointwise.1.point_ref) | copy-start | bytes 12582916
  23.1 18.1 %copy-start.1 = (f32[2,32,128,128]{3,2,1,0:T(8,128)S(1)}, f32[2,32,128,128]{3,2,1,0:T(8,128)}, u32[]{:S(2)}) copy-start(f32[2,32,128,128]{3,2,1,0:T(8,128)} %cot_ref.1) | copy-start | bytes 12582916
  23.1 18.1 %copy-start.2 = (bf16[80,256]{1,0:T(8,128)(2,1)S(1)}, bf16[80,256]{1,0:T(8,128)(2,1)}, u32[]{:S(2)}) copy-start(bf16[80,256]{1,0:T(8,128)(2,1)} %constant.20.clone.fy_hbm.fy_ref) | copy-start | bytes 122884
  23.1 18.1 %copy-start.3 = (bf16[128,96]{1,0:T(8,128)(2,1)S(1)}, bf16[128,96]{1,0:T(8,128)(2,1)}, u32[]{:S(2)}) copy-start(bf16[128,96]{1,0:T(8,128)(2,1)} %constant.21.clone.ty_ref.ty_hbm) | copy-start | bytes 73732
  23.1 18.1 %copy-start.4 = (bf16[128,256]{1,0:T(8,128)(2,1)S(1)}, bf16[128,256]{1,0:T(8,128)(2,1)}, u32[]{:S(2)}) copy-start(bf16[128,256]{1,0:T(8,128)(2,1)} %constant.23.clone.tzf_ref) | copy-start | bytes 196612
  23.1 18.1 %copy-start.6 = (bf16[192,128]{1,0:T(8,128)(2,1)S(1)}, bf16[192,128]{1,0:T(8,128)(2,1)}, u32[]{:S(2)}) copy-start(bf16[192,128]{1,0:T(8,128)(2,1)} %constant.24.clone.tzi_ref) | copy-start | bytes 147460
  48.5 13.6 %all-to-all-start.2 = ((f32[16,32,128]{2,1,0:T(8,128)}), f32[16,32,128]{2,1,0:T(8,128)S(1)}, u32[]{:S(2)}, u32[]{:S(2)}) async-start(f32[16,32,128]{2,1,0:T(8,128)} %bitcast.5), calls=%async_computation.2 | async-start | bytes 524288 | tf_op jit(solution)/shard_map/all_to_all | solution.py:790
  68.1 14.6 %all-to-all-start.3 = ((f32[16,40,128]{2,1,0:T(8,128)}), f32[16,40,128]{2,1,0:T(8,128)S(1)}, u32[]{:S(2)}, u32[]{:S(2)}) async-start(f32[16,40,128]{2,1,0:T(8,128)} %bitcast.7), calls=%async_computation.3 | async-start | bytes 655360 | tf_op jit(solution)/shard_map/all_to_all | solution.py:790

commit v6 on v5

--- a/solution.py
+++ b/solution.py
@@ -372,7 +372,7 @@
 
         for h in range(2):
             loads[2 * t + h].wait()
-            lax.fori_loop(h * (pairs // 2), (h + 1) * (pairs // 2), body, 0, unroll=min(4, pairs // 2))
+            lax.fori_loop(h * (pairs // 2), (h + 1) * (pairs // 2), body, 0, unroll=min(8, pairs // 2))
     tables[1].wait()
     for u in range(pairs // 4):
         tiles = [[], []]

time: 89.1 us -> 89 us (level)
  no operation moved by 1% of the time
where the time goes in v6:
time: 89 us; the launch traced here: 88.5 us
  Pallas kernels  47.6 us (53%)
  starting transfers between devices  14.6 us (16%)
  blocking collectives  13 us (15%)
  waiting for transfers between devices  12.4 us (14%)
  between operations  0.95 us (1%)
    all_to_all x3, starting transfers between devices, exchange(): lax.all_to_all(blocks, 'space', split_axis=0, concat_axis=0, tiled=True)  14.6 us
    all_to_all x1, blocking collectives, exchange(): lax.all_to_all(blocks, 'space', split_axis=0, concat_axis=0, tiled=True)  13 us
    all_to_all x3, waiting for transfers between devices, exchange(): lax.all_to_all(blocks, 'space', split_axis=0, concat_axis=0, tiled=True)  12.4 us
    pallas_call x1, Pallas kernels, per_device(): pl.pallas_call(outer_kernel, in_specs=[HBM, HBM, VM], out_specs=[VM, HBM]...  7.41 us
    pallas_call x1, Pallas kernels, per_device(): pl.pallas_call(functools.partial(middle_kernel, stride, ky_own), in_specs...  7.32 us
    pallas_call x1, Pallas kernels, per_device(): pl.pallas_call(functools.partial(adjoint_kernel, slab, nx, lines, extra),...  5.94 us
    pallas_call x1, Pallas kernels, per_device(): pl.pallas_call(functools.partial(last_kernel, stride_in, ky_own, devices,...  5.8 us
    pallas_call x1, Pallas kernels, per_device(): pl.pallas_call(functools.partial(weight_grad_kernel, nx, lines), in_specs...  5.57 us
  transfers between devices with their start and end apart: 3, of which 3 were waited for; matrix products, arithmetic and copies ran while one was open for 0% of the time, Pallas kernels for 21%

profile of v6, /device:TPU:0, one launch (start us, length us, event | category | flops | bytes accessed | tf_op | source)
XLA Modules:
  0.0 88.5 jit_solution(17732201954228301012)
XLA Ops:
  0.6 0.0 copy-start.5
  0.6 0.0 copy-start.7
  0.7 5.0 %field_forward.1 = f32[512,128]{1,0:T(8,128)} custom-call(f32[2,32,128,128]{3,2,1,0:T(8,128)} %field_hbm.5, bf16[80,256]{1,0:T(8,128)(2,1)} %constant.20.clone.fy_hbm.fy_ref, bf16[128,256]{1,0:T(8,128)(2,1)} %constant.22.clone.tz_hbm), custom_call_target="tpu_custom_call" | custom-call | bytes 12000000 | tf_op jit(solution)/shard_map/field_forward/pallas_call | solution.py:792
  5.7 7.4 %all-to-all-start = ((f32[16,32,128]{2,1,0:T(8,128)}), f32[16,32,128]{2,1,0:T(8,128)S(1)}, u32[]{:S(2)}, u32[]{:S(2)}) async-start(f32[16,32,128]{2,1,0:T(8,128)} %bitcast), calls=%async_computation | async-start | bytes 524288 | tf_op jit(solution)/shard_map/all_to_all | solution.py:790
  13.0 0.0 copy-done.5
  13.0 0.0 copy-done.7
  13.0 5.6 %pointwise.1.point_ref = f32[2,32,128,128]{3,2,1,0:T(8,128)} custom-call(f32[2,32,128,128]{3,2,1,0:T(8,128)} %field_hbm.5, f32[32,32]{1,0:T(8,128)S(1)} %copy-done.5, f32[1,32]{1,0:T(1,128)S(1)} %bitcast.18), custom_call_target="tpu_custom_call" | custom-call | bytes 18000000 | tf_op jit(solution)/shard_map/pointwise/pallas_call | solution.py:812
  18.6 4.5 %all-to-all-done = f32[16,32,128]{2,1,0:T(8,128)S(1)} async-done(((f32[16,32,128]{2,1,0:T(8,128)}), f32[16,32,128]{2,1,0:T(8,128)S(1)}, u32[]{:S(2)}, u32[]{:S(2)}) %all-to-all-start) | async-done | bytes 262176 | tf_op jit(solution)/shard_map/all_to_all | solution.py:790
  23.1 0.0 copy-start
  23.1 0.0 copy-start.1
  23.1 0.0 copy-start.2
  23.1 0.0 copy-start.3
  23.1 0.0 copy-start.4
  23.1 0.0 copy-start.6
  23.1 5.0 %mode_mix.1 = f32[512,128]{1,0:T(8,128)S(1)} custom-call(f32[512,128]{1,0:T(8,128)S(1)} %bitcast.12, f32[32,2,32,1024]{3,2,1,0:T(8,128)} %weight_hbm.3, bf16[192,2048]{1,0:T(8,128)(2,1)} %constant.26.clone.fx_hbm, bf16[64,192]{1,0:T(8,128)(2,1)} %constant.28.clone.inv_hbm), custom_call_target="tpu_custom_call" | custom-call | bytes 15000000 | tf_op jit(solution)/shard_map/mode_mix/pallas_call | solution.py:830
  28.1 13.0 %all_to_all.20 = f32[16,32,128]{2,1,0:T(8,128)S(1)} all-to-all(f32[16,32,128]{2,1,0:T(8,128)S(1)} %bitcast.17), channel_id=1, replica_groups=mesh['group'=2,'space'=16] {'space'}, dimensions={0} | all-to-all | bytes 524288 | tf_op jit(solution)/shard_map/all_to_all | solution.py:790
  41.1 0.0 copy-done
  41.1 0.0 copy-done.1
  41.1 0.0 copy-done.2
  41.1 0.0 copy-done.3
  41.1 0.0 copy-done.4
  41.1 0.0 copy-done.6
  41.1 7.3 %middle.1 = (f32[2,32,128,128]{3,2,1,0:T(8,128)}, f32[2,32,128,128]{3,2,1,0:T(8,128)}, f32[512,128]{1,0:T(8,128)}) custom-call(f32[512,128]{1,0:T(8,128)S(1)} %bitcast.16, f32[2,32,128,128]{3,2,1,0:T(8,128)S(1)} %copy-done, f32[2,32,128,128]{3,2,1,0:T(8,128)S(1)} %copy-done.1, bf16[192,128]{1,0:T(8,128)(2,1)S(1)} %copy-done.6, ...), custom_call_target="tpu_custom_call" | custom-call | bytes 30000000 | tf_op jit(solution)/shard_map/middle/pallas_call | solution.py:850
  48.5 3.5 %all-to-all-start.2 = ((f32[16,32,128]{2,1,0:T(8,128)}), f32[16,32,128]{2,1,0:T(8,128)S(1)}, u32[]{:S(2)}, u32[]{:S(2)}) async-start(f32[16,32,128]{2,1,0:T(8,128)} %bitcast.5), calls=%async_computation.2 | async-start | bytes 524288 | tf_op jit(solution)/shard_map/all_to_all | solution.py:790
  52.0 7.4 %outer_and_back.1 = (f32[8,128]{1,0:T(8,128)S(1)}, f32[2,32,128,128]{3,2,1,0:T(8,128)}) custom-call(f32[2,32,128,128]{3,2,1,0:T(8,128)} %field_hbm.5, f32[2,32,128,128]{3,2,1,0:T(8,128)} %get-tuple-element.19.gpre_hbm, f32[32,32]{1,0:T(8,128)S(1)} %copy-done.5), custom_call_target="tpu_custom_call" | custom-call | bytes 24000000 | tf_op jit(solution)/shard_map/outer_and_back/pallas_call | solution.py:867
  59.4 2.6 %all-to-all-done.2 = f32[16,32,128]{2,1,0:T(8,128)S(1)} async-done(((f32[16,32,128]{2,1,0:T(8,128)}), f32[16,32,128]{2,1,0:T(8,128)S(1)}, u32[]{:S(2)}, u32[]{:S(2)}) %all-to-all-start.2) | async-done | bytes 262176 | tf_op jit(solution)/shard_map/all_to_all | solution.py:790
  62.0 5.9 %mode_adjoint.1 = f32[640,128]{1,0:T(8,128)} custom-call(f32[512,128]{1,0:T(8,128)S(1)} %bitcast.14, f32[32,2,32,1024]{3,2,1,0:T(8,128)} %weight_hbm.3, bf16[64,192]{1,0:T(8,128)(2,1)} %constant.27.clone.gx_hbm, bf16[1024,128]{1,0:T(8,128)(2,1)} %constant.29.clone.inv_hbm, f32[8,128]{1,0:T(8,128)S(1)} %get-tuple-element.20.sums_ref), custom_call_target="tpu_custom_call" | custom-call | bytes 18000000 | tf_op jit(solution)/shard_map/mode_adjoint/pallas_call | solution.py:887
  68.0 3.7 %all-to-all-start.3 = ((f32[16,40,128]{2,1,0:T(8,128)}), f32[16,40,128]{2,1,0:T(8,128)S(1)}, u32[]{:S(2)}, u32[]{:S(2)}) async-start(f32[16,40,128]{2,1,0:T(8,128)} %bitcast.7), calls=%async_computation.3 | async-start | bytes 655360 | tf_op jit(solution)/shard_map/all_to_all | solution.py:790
  71.7 5.6 %weight_grad.1 = f32[32,2,32,1024]{3,2,1,0:T(8,128)} custom-call(f32[512,128]{1,0:T(8,128)S(1)} %bitcast.13, f32[512,128]{1,0:T(8,128)S(1)} %bitcast.15, bf16[192,2048]{1,0:T(8,128)(2,1)} %constant.26.clone.fx_hbm, bf16[64,192]{1,0:T(8,128)(2,1)} %constant.27.clone.gx_hbm), custom_call_target="tpu_custom_call" | custom-call | bytes 18000000 | tf_op jit(solution)/shard_map/weight_grad/pallas_call | solution.py:906
  77.3 5.3 %all-to-all-done.3 = f32[16,40,128]{2,1,0:T(8,128)S(1)} async-done(((f32[16,40,128]{2,1,0:T(8,128)}), f32[16,40,128]{2,1,0:T(8,128)S(1)}, u32[]{:S(2)}, u32[]{:S(2)}) %all-to-all-start.3) | async-done | bytes 327712 | tf_op jit(solution)/shard_map/all_to_all | solution.py:790
  82.6 5.8 %field_inverse.1 = (f32[2,32,128,128]{3,2,1,0:T(8,128)}, f32[32,32]{1,0:T(8,128)}, f32[1,32]{1,0:T(1,128)}) custom-call(f32[640,128]{1,0:T(8,128)S(1)} %bitcast.10, f32[640,128]{1,0:T(8,128)S(1)} %bitcast.11, f32[2,32,128,128]{3,2,1,0:T(8,128)} %get-tuple-element.21.back_hbm, bf16[192,128]{1,0:T(8,128)(2,1)} %constant.25.clone.tzi_hbm, ...), custom_call_target="tpu_custom_call" | custom-call | bytes 24000000 | tf_op jit(solution)/shard_map/field_inverse/pallas_call | solution.py:935
Async XLA Ops:
  0.6 12.4 %copy-start.5 = (f32[32,32]{1,0:T(8,128)S(1)}, f32[32,32]{1,0:T(8,128)}, u32[]{:S(2)}) copy-start(f32[32,32]{1,0:T(8,128)} %weight_ref.3) | copy-start | bytes 12292
  0.6 12.4 %copy-start.7 = (f32[32]{0:T(128)S(1)}, f32[32]{0:T(128)}, u32[]{:S(2)}) copy-start(f32[32]{0:T(128)} %param.19) | copy-start | bytes 388
  5.7 17.4 %all-to-all-start = ((f32[16,32,128]{2,1,0:T(8,128)}), f32[16,32,128]{2,1,0:T(8,128)S(1)}, u32[]{:S(2)}, u32[]{:S(2)}) async-start(f32[16,32,128]{2,1,0:T(8,128)} %bitcast), calls=%async_computation | async-start | bytes 524288 | tf_op jit(solution)/shard_map/all_to_all | solution.py:790
  23.1 18.0 %copy-start = (f32[2,32,128,128]{3,2,1,0:T(8,128)S(1)}, f32[2,32,128,128]{3,2,1,0:T(8,128)}, u32[]{:S(2)}) copy-start(f32[2,32,128,128]{3,2,1,0:T(8,128)} %pointwise.1.point_ref) | copy-start | bytes 12582916
  23.1 18.0 %copy-start.1 = (f32[2,32,128,128]{3,2,1,0:T(8,128)S(1)}, f32[2,32,128,128]{3,2,1,0:T(8,128)}, u32[]{:S(2)}) copy-start(f32[2,32,128,128]{3,2,1,0:T(8,128)} %cot_ref.1) | copy-start | bytes 12582916
  23.1 18.0 %copy-start.2 = (bf16[80,256]{1,0:T(8,128)(2,1)S(1)}, bf16[80,256]{1,0:T(8,128)(2,1)}, u32[]{:S(2)}) copy-start(bf16[80,256]{1,0:T(8,128)(2,1)} %constant.20.clone.fy_hbm.fy_ref) | copy-start | bytes 122884
  23.1 18.0 %copy-start.3 = (bf16[128,96]{1,0:T(8,128)(2,1)S(1)}, bf16[128,96]{1,0:T(8,128)(2,1)}, u32[]{:S(2)}) copy-start(bf16[128,96]{1,0:T(8,128)(2,1)} %constant.21.clone.ty_ref.ty_hbm) | copy-start | bytes 73732
  23.1 18.0 %copy-start.4 = (bf16[128,256]{1,0:T(8,128)(2,1)S(1)}, bf16[128,256]{1,0:T(8,128)(2,1)}, u32[]{:S(2)}) copy-start(bf16[128,256]{1,0:T(8,128)(2,1)} %constant.23.clone.tzf_ref) | copy-start | bytes 196612
  23.1 18.0 %copy-start.6 = (bf16[192,128]{1,0:T(8,128)(2,1)S(1)}, bf16[192,128]{1,0:T(8,128)(2,1)}, u32[]{:S(2)}) copy-start(bf16[192,128]{1,0:T(8,128)(2,1)} %constant.24.clone.tzi_ref) | copy-start | bytes 147460
  48.5 13.6 %all-to-all-start.2 = ((f32[16,32,128]{2,1,0:T(8,128)}), f32[16,32,128]{2,1,0:T(8,128)S(1)}, u32[]{:S(2)}, u32[]{:S(2)}) async-start(f32[16,32,128]{2,1,0:T(8,128)} %bitcast.5), calls=%async_computation.2 | async-start | bytes 524288 | tf_op jit(solution)/shard_map/all_to_all | solution.py:790
  68.0 14.6 %all-to-all-start.3 = ((f32[16,40,128]{2,1,0:T(8,128)}), f32[16,40,128]{2,1,0:T(8,128)S(1)}, u32[]{:S(2)}, u32[]{:S(2)}) async-start(f32[16,40,128]{2,1,0:T(8,128)} %bitcast.7), calls=%async_computation.3 | async-start | bytes 655360 | tf_op jit(solution)/shard_map/all_to_all | solution.py:790
